TPU v7x, 32 devices: a whole 2x2x4 slice. The times are simulated.
32 devices in a mesh: inpair: 4 (over y, core), outpair: 8 (over z, x).
Axes of the slice: x: 2, y: 2, z: 4, core: 2. Of those that a mesh axis runs over, the one named last changes fastest.
Arguments:
- integrals: bfloat16 [4096, 8192], P('inpair', 'outpair'), may hold values from -0.09375 to 0.09375
- amplitudes: bfloat16 [8, 512, 4096], P('outpair', None, 'inpair'), may hold values from -6 to 6
- tile_live: int32 [16, 32], P('inpair', 'outpair'), may hold values 0 or 1
- batch_owner: int32 [2], replicated, may hold values from 0 to 7
- occ_energy: float32 [2, 512], P(None, 'inpair'), may hold values from -2 to -0.5
- vir_energy: float32 [8192], P('outpair'), may hold values from 0.5 to 4
- swap_within: int32 [128], replicated, may hold values from 0 to 127, each once
Outputs:
- update: float32 [2, 512, 8192], P(None, 'inpair', 'outpair')
Inputs may be any that keep to these rules, and one draw needn't show every extreme that they name: `swap_within`: each value once.
All inputs are finite; a program needn't handle non-finite values. No bound on the sum of `tile_live` on one device may be relied on, other than what follows from the above.
Results may differ from a plain program's by a relative error of at most 0.0003.
Values may be sent and summed in bfloat16 or wider, within the bound.
No kernel may reach another device: no remote copies, remote signals or barrier semaphores. Data moves between devices by JAX's collectives and lax.ppermute only.
A program may use at most 64 MiB of HBM per device.

v0:
```python
import jax
import jax.numpy as jnp
from jax import lax
from jax.sharding import PartitionSpec as P

SUB_R = 256
SUB_C = 256
NB = 2


def spread(block, axis, holder):
    block = jnp.where(lax.axis_index(axis) == holder, block, jnp.zeros_like(block))
    return lax.psum(block, axis)


def on_device(integrals, amplitudes, tile_live, batch_owner, occ_energy, vir_energy, swap_within):
    parties = lax.axis_size("outpair")
    tile_mask = jnp.repeat(jnp.repeat(tile_live, SUB_R, 0), SUB_C, 1).astype(jnp.bfloat16)
    weights = integrals * tile_mask
    batches = []
    for index in range(NB):
        batches.append(spread(amplitudes[0], "outpair", batch_owner[index]))
    groups = lax.axis_size("inpair")
    stacked = jnp.stack(batches)
    share = stacked.shape[1] // groups
    depth = stacked.shape[2]
    ordered = jnp.transpose(stacked.reshape(NB, groups, share, depth), (1, 0, 2, 3)).reshape(
        groups * NB * share, depth
    )
    mine = lax.psum_scatter(
        jnp.dot(ordered, weights, preferred_element_type=jnp.float32),
        "inpair",
        scatter_dimension=0,
        tiled=True,
    )
    summed = mine.reshape(NB, share, mine.shape[1])
    local_rows = summed.shape[1]
    width = summed.shape[2]
    pair_grid = summed.reshape(NB, local_rows, parties, width // parties)
    received = lax.all_to_all(pair_grid, "outpair", split_axis=2, concat_axis=2, tiled=True)
    swapped = jnp.take(received, swap_within, axis=3).reshape(NB, local_rows, width)
    denominator = vir_energy[None, None, :] - occ_energy[:, :, None]
    return (summed + swapped) / denominator


def solution(mesh):
    return jax.shard_map(
        on_device,
        mesh=mesh,
        in_specs=(
            P("inpair", "outpair"),
            P("outpair", None, "inpair"),
            P("inpair", "outpair"),
            P(),
            P(None, "inpair"),
            P("outpair"),
            P(),
        ),
        out_specs=P(None, "inpair", "outpair"),
        check_vma=False,
    )
```

profile of v0, /device:TPU:0, one launch (start us, length us, event | category | flops | bytes accessed | tf_op | source)
XLA Modules:
  0.0 212.2 jit_solution(2025686651923900589)
XLA Ops:
  6.5 0.0 all-reduce.3.cloned.1.call-start
  6.5 1.3 fusion.4
  9.2 0.0 copy-start.2
  9.2 2.7 %broadcast_select_fusion.1 = (bf16[1,512,1024]{2,1,0:T(8,128)(2,1)}, bf16[1,512,1024]{2,1,0:T(8,128)(2,1)}) fusion(bf16[1,512,1024]{2,1,0:T(8,128)(2,1)} %param.8, pred[]{:T(512)S(6)} %eq.6, pred[]{:T(512)S(6)} %eq.7), kind=kLoop, calls=%fused_computation.8 | loop fusion | flops 1048576 | bytes 3145730 | tf_op jit(solution)/shard_map/jit(_where)/select_n | solution.py:12
  11.9 0.0 all-reduce.3.cloned.1.call-update
  11.9 0.0 reduce-scatter.2.cloned.1.call-start
  11.9 0.0 copy-done.2
  12.0 1.2 broadcast_in_dim.25
  13.3 0.5 copy.18
  13.8 103.2 %all-reduce.3.cloned.1.call-done = (bf16[1,4,128,1024]{3,2,0,1:T(8,128)(2,1)}, bf16[1,4,128,1024]{3,2,0,1:T(8,128)(2,1)}) async-done(((bf16[1,4,128,1024]{3,2,0,1:T(8,128)(2,1)}, bf16[1,4,128,1024]{3,2,0,1:T(8,128)(2,1)}), (bf16[1,4,128,1024]{3,2,0,1:T(8,128)(2,1)}, bf16[1,4,128,1024]{3,2,0,1:T(8,128)(2,1)})) %all-reduce.3.cloned.1.call-update) | async-done | bytes 2097168 | tf_op jit(solution)/shard_map/psum | solution.py:13
  116.9 0.0 copy-start.4
  116.9 1.9 pad_maximum_fusion
  118.8 0.3 copy-done.4
  119.1 4.3 %fusion = f32[1024,1024]{1,0:T(8,128)} fusion(bf16[1024,1024]{1,0:T(8,128)(2,1)S(1)} %bitcast.32, bf16[1024,1024]{1,0:T(8,128)(2,1)S(1)} %copy-done.4, bf16[1024,1024]{1,0:T(8,128)(2,1)S(1)} %bitcast.31), kind=kOutput, calls=%fused_computation.2 | convolution fusion | flops 2148532224 | bytes 10485760 | tf_op jit(solution)/shard_map/dot_general | solution.py:31
  123.5 0.0 reduce-scatter.2.cloned.1.call-update
  123.5 44.4 %reduce-scatter.2.cloned.1.call-done = f32[256,1024]{1,0:T(8,128)} async-done(((f32[1024,1024]{1,0:T(8,128)}), f32[256,1024]{1,0:T(8,128)}) %reduce-scatter.2.cloned.1.call-update) | async-done | bytes 1048592 | tf_op jit(solution)/shard_map/reduce_scatter | solution.py:30
  167.9 1.4 copy.19
  169.3 0.0 copy-start.5
  169.3 0.0 copy-start
  169.3 1.4 copy.13
  170.7 5.5 %all-to-all-start = ((f32[2,128,8,128]{1,3,0,2:T(8,128)}), f32[2,128,8,128]{1,3,0,2:T(8,128)S(1)}, u32[]{:S(2)}, u32[]{:S(2)}) async-start(f32[2,128,8,128]{1,3,0,2:T(8,128)} %copy.13), calls=%async_computation.1 | async-start | bytes 2097152 | tf_op jit(solution)/shard_map/all_to_all | solution.py:40
  176.2 0.0 copy-done.5
  176.3 0.0 copy-done
  176.3 0.3 copy.16
  176.6 25.4 %all-to-all-done = f32[2,128,8,128]{1,3,0,2:T(8,128)S(1)} async-done(((f32[2,128,8,128]{1,3,0,2:T(8,128)}), f32[2,128,8,128]{1,3,0,2:T(8,128)S(1)}, u32[]{:S(2)}, u32[]{:S(2)}) %all-to-all-start) | async-done | bytes 1048608 | tf_op jit(solution)/shard_map/all_to_all | solution.py:40
  202.0 0.6 copy.14
  202.6 0.0 copy-start.1
  202.6 0.0 copy-start.3
  202.6 0.7 gather_fusion
  203.3 0.3 copy.15
  203.7 0.0 copy-done.1
  203.7 0.0 copy-done.3
  203.7 0.4 fusion.3
  204.1 1.3 copy.17
  (6 shorter events, 0.1 us)
Async XLA Ops:
  6.5 110.4 %all-reduce.3.cloned.1.call-start = ((), (), s32[]{:S(2)}) async-start(), calls=%async_computation.3 | async-start | bytes 4194304 | tf_op jit(solution)/shard_map/psum | solution.py:13
  9.2 2.8 %copy-start.2 = (s32[4,4]{1,0:T(4,128)S(1)}, s32[4,4]{1,0:T(4,128)}, u32[]{:S(2)}) copy-start(s32[4,4]{1,0:T(4,128)} %param.9) | copy-start | bytes 196
  11.9 156.0 %reduce-scatter.2.cloned.1.call-start = ((), (), s32[]{:S(2)}) async-start(), calls=%async_computation.2 | async-start | bytes 5242880 | tf_op jit(solution)/shard_map/reduce_scatter | solution.py:30
  116.9 2.2 %copy-start.4 = (bf16[1024,1024]{1,0:T(8,128)(2,1)S(1)}, bf16[1024,1024]{1,0:T(8,128)(2,1)}, u32[]{:S(2)}) copy-start(bf16[1024,1024]{1,0:T(8,128)(2,1)} %param.7) | copy-start | bytes 6291460
  169.3 6.9 %copy-start.5 = (s32[128]{0:T(128)S(1)}, s32[128]{0:T(128)}, u32[]{:S(2)}) copy-start(s32[128]{0:T(128)} %param.13) | copy-start | bytes 1540
  169.3 6.9 %copy-start = (f32[256,1024]{1,0:T(8,128)S(1)}, f32[256,1024]{1,0:T(8,128)}, u32[]{:S(2)}) copy-start(f32[256,1024]{1,0:T(8,128)} %reduce-scatter.2.cloned.1.call-done) | copy-start | bytes 3145732
  170.7 31.3 %all-to-all-start = ((f32[2,128,8,128]{1,3,0,2:T(8,128)}), f32[2,128,8,128]{1,3,0,2:T(8,128)S(1)}, u32[]{:S(2)}, u32[]{:S(2)}) async-start(f32[2,128,8,128]{1,3,0,2:T(8,128)} %copy.13), calls=%async_computation.1 | async-start | bytes 2097152 | tf_op jit(solution)/shard_map/all_to_all | solution.py:40
  202.6 1.1 copy-start.1
  202.6 1.1 copy-start.3
Sparse Core Ops, SparseCore 0:
  12.0 104.8 all-reduce.2
  123.6 44.2 reduce-scatter.1
where the time goes:
time: 212 us
  waiting for transfers between devices  173 us (82%)
  between operations  14.9 us (7%)
  local copies, waits for them, and re-layouts  9.53 us (4%)
  starting transfers between devices  5.55 us (3%)
  other arithmetic  4.97 us (2%)
  matrix products  4.3 us (2%)
    psum x1, waiting for transfers between devices, spread(): return lax.psum(block, axis)  103 us
    reduce_scatter x1, waiting for transfers between devices, on_device(): lax.psum_scatter(jnp.dot(ordered, weights, preferred_element_type=jnp.flo...  44.4 us
    all_to_all x1, waiting for transfers between devices, on_device(): lax.all_to_all(pair_grid, 'outpair', split_axis=2, concat_axis=2, tiled=T...  25.4 us
    all_to_all x1, starting transfers between devices, on_device(): lax.all_to_all(pair_grid, 'outpair', split_axis=2, concat_axis=2, tiled=T...  5.51 us
    dot_general x1, matrix products, on_device(): jnp.dot(ordered, weights, preferred_element_type=jnp.float32)  4.3 us
  transfers between devices with their start and end apart: 3, of which 3 were waited for; matrix products, arithmetic and copies ran while one was open for 1% of the time, Pallas kernels for 0%

commit v1 on v0

v1 whole, which is shorter than its diff:
```python
import functools

import jax
import jax.numpy as jnp
from jax import lax
from jax.experimental import pallas as pl
from jax.experimental.pallas import tpu as pltpu
from jax.sharding import PartitionSpec as P

CHUNKS = 4
PARTS = 2
LEVELS = 32767.0
OCTAVE = 128.0
LANES = 128
TILE_ROWS = 16
VMEM = 8 * 1024 * 1024


def pick(array, index, axis):
    return lax.dynamic_index_in_dim(array, index, axis, keepdims=False)


def tied(values, *others):
    return lax.optimization_barrier((values, *others))[0]


def codes_of(values):
    top = jnp.max(jnp.abs(values), axis=0, keepdims=True)
    code = jnp.ceil(jnp.log2(jnp.maximum(top, 1e-30)) * OCTAVE)
    scaled = jnp.round(values * (LEVELS * jnp.exp2(code * (-1.0 / OCTAVE))))
    return jnp.clip(scaled, -LEVELS, LEVELS), code


def step_of(code):
    return jnp.exp2(code.astype(jnp.float32) * (1.0 / OCTAVE)) * (1.0 / LEVELS)


def shrink(values):
    scaled, code = codes_of(values)
    return jnp.concatenate([scaled.astype(jnp.int16), code.astype(jnp.int16)], axis=0)


def grow(coded):
    return coded[:-1].astype(jnp.float32) * step_of(coded[-1:])


def merge_kernel(x_ref, keep_ref, coded_ref, total_ref, blocks_ref):
    x = x_ref[0]
    _, rows, _ = keep_ref.shape
    parties, _, lanes = blocks_ref.shape

    @pl.loop(0, parties)
    def _(o):
        at = pl.ds(pl.multiple_of(o * lanes, lanes), lanes)
        step = step_of(coded_ref[2 * rows : 2 * rows + 1, at].astype(jnp.int32))
        first = keep_ref[0, :, at] + coded_ref[:rows, at].astype(jnp.float32) * step
        second = keep_ref[1, :, at] + coded_ref[rows : 2 * rows, at].astype(jnp.float32) * step
        total = jnp.concatenate([jnp.where(x == 0, first, second), jnp.where(x == 0, second, first)], axis=0)
        total_ref[:, at] = total
        scaled, code = codes_of(total)
        blocks_ref[o, : 2 * rows] = scaled.astype(jnp.int32).astype(jnp.int16)
        blocks_ref[o, 2 * rows :] = jnp.broadcast_to(code, (TILE_ROWS, lanes)).astype(jnp.int32).astype(jnp.int16)


def merge(x, keep, coded, parties):
    _, rows, width = keep.shape
    lanes = width // parties
    if lanes % LANES or (2 * rows) % TILE_ROWS:
        total = keep + grow(coded).reshape(keep.shape)
        total = jnp.where(x == 0, total, total[::-1]).reshape(2 * rows, width)
        coded = shrink(total)
        return total, jnp.stack([coded[:, o * lanes : (o + 1) * lanes] for o in range(parties)])
    coded = jnp.concatenate([coded, jnp.zeros((TILE_ROWS - 1, width), jnp.int16)], axis=0)
    vmem = pl.BlockSpec(memory_space=pltpu.VMEM)
    return pl.pallas_call(
        merge_kernel,
        out_shape=(
            jax.ShapeDtypeStruct((2 * rows, width), jnp.float32),
            jax.ShapeDtypeStruct((parties, 2 * rows + TILE_ROWS, lanes), jnp.int16),
        ),
        in_specs=[pl.BlockSpec(memory_space=pltpu.SMEM), vmem, vmem],
        out_specs=(vmem, vmem),
        compiler_params=pltpu.CompilerParams(vmem_limit_bytes=VMEM),
        name="merge",
    )(x.reshape(1).astype(jnp.int32), keep, coded)


def finish_kernel(total_ref, blocks_ref, swap_ref, vir_ref, occ_ref, *rest):
    out_ref = rest[-1]
    parties, padded, lanes = blocks_ref.shape
    rows = padded - TILE_ROWS
    halves = rows // (out_ref.shape[0] * out_ref.shape[1])
    swap = jnp.broadcast_to(swap_ref[...], (rows, lanes))

    @pl.loop(0, parties)
    def _(o):
        at = pl.ds(pl.multiple_of(o * lanes, lanes), lanes)
        facing = blocks_ref[o, :rows].astype(jnp.float32) * step_of(blocks_ref[o, rows : rows + 1].astype(jnp.int32))
        both = total_ref[:, at] + jnp.take_along_axis(facing, swap, axis=1)
        both = both / (vir_ref[:, at] - occ_ref[...])
        both = both.reshape(2, -1, halves, lanes)
        for h in range(2):
            for b in range(both.shape[1]):
                out_ref[b, h, 0, :, at] = both[h, b]


def finish(total, blocks, swap_within, vir_energy, occ, out, part, parts):
    rows, width = total.shape
    parties, _, lanes = blocks.shape
    batches, share = occ.shape
    count = share // 2 // parts
    shape = (batches, 2, parts, count, width)
    occ = jnp.transpose(occ.reshape(batches, 2, parts, count)[:, :, part], (1, 0, 2)).reshape(rows, 1)
    whole = lambda a: pl.BlockSpec(a.shape, lambda i: (0,) * a.ndim)
    args = [total, blocks, swap_within.reshape(1, lanes), vir_energy.reshape(1, width), occ]
    specs = [whole(a) for a in args]
    alias = {}
    if out is not None:
        alias = {len(args): 0}
        args.append(out)
        specs.append(pl.BlockSpec(memory_space=pl.ANY))
    return pl.pallas_call(
        finish_kernel,
        grid=(1,),
        out_shape=jax.ShapeDtypeStruct(shape, jnp.float32),
        in_specs=specs,
        out_specs=pl.BlockSpec((batches, 2, 1, count, width), lambda i: (0, 0, part, 0, 0)),
        input_output_aliases=alias,
        compiler_params=pltpu.CompilerParams(vmem_limit_bytes=VMEM),
        name="finish",
    )(*args)


def on_device(integrals, amplitudes, tile_live, batch_owner, occ_energy, vir_energy, swap_within):
    parties, groups = lax.axis_size("outpair"), lax.axis_size("inpair")
    me, place = lax.axis_index("outpair"), lax.axis_index("inpair")
    x, z, nz = me % 2, me // 2, parties // 2
    batches = batch_owner.shape[0]
    _, rows, depth = amplitudes.shape
    width = integrals.shape[1]
    lanes = width // parties
    share = rows // groups
    half = share // 2
    parts, chunks = (PARTS, CHUNKS) if half % (16 * CHUNKS) == 0 else (1, 1)
    deep = half // chunks
    beside = [(o, o ^ 1) for o in range(parties)]
    even = [(o, o ^ 2) for o in range(parties) if (o ^ 2) < parties]
    odd = [(o, ((o // 2 + 1) ^ 1) * 2 - 2 + o % 2) for o in range(parties)]
    odd = [(o, t) for o, t in odd if 0 <= t < parties]

    stored = amplitudes[0].reshape(groups, 2, half, depth)
    mine = pick(stored, x, 1)
    other = pick(stored, 1 - x, 1)
    cut = lambda a, c: a[:, c * deep : (c + 1) * deep]
    tall_tile, wide_tile = integrals.shape[0] // tile_live.shape[0], width // tile_live.shape[1]
    flags = jnp.repeat(tile_live.astype(jnp.bfloat16), wide_tile, 1)[:, None, :]
    live = (integrals.reshape(-1, tall_tile, width) * flags).reshape(integrals.shape)

    home = [batch_owner[b] // 2 for b in range(batches)]
    column = [batch_owner[b] % 2 for b in range(batches)]
    from_even = [(z > home[b]) == (z % 2 == 1) for b in range(batches)]

    def swap_x(values):
        return lax.ppermute(values, "outpair", beside)

    def shift(values):
        return lax.ppermute(values, "outpair", odd), lax.ppermute(values, "outpair", even)

    source = []
    for c in range(chunks):
        came = swap_x(cut(other, c))
        source.append([jnp.where(column[b] == x, cut(mine, c), came) for b in range(batches)])

    held = []
    near, far = [], []
    moved = None
    for step in range(chunks + nz - 1):
        now = source[min(step, chunks - 1)]
        if step:
            ready = [far[c] for c in range(len(far)) if step - c - nz == 1]
            by_odd, by_even = tied(moved, *ready)
            now = [
                jnp.where(z == home[b], now[b], jnp.where(from_even[b], by_even[b], by_odd[b])) for b in range(batches)
            ]
        held.append(jnp.stack(now))
        if step < chunks + nz - 2:
            moved = shift(held[-1])
        if step >= nz - 1:
            window = held[step - nz + 1 : step + 1]
            got = [pick(jnp.stack([h[b] for h in window]), jnp.abs(z - home[b]), 0) for b in range(batches)]
            near.append(jnp.stack(got))
            far.append(swap_x(near[-1]))

    dot = lambda a, w: jnp.dot(a, w, preferred_element_type=jnp.float32)
    merged = []
    arrived = []
    for p in range(parts):
        mine = slice(p * chunks // parts, (p + 1) * chunks // parts)
        tall = jnp.stack([jnp.concatenate(near[mine], axis=2), jnp.concatenate(far[mine], axis=2)])
        if p:
            tall = tied(tall, merged[-1])
        count = tall.shape[3]
        tall = tall.reshape(2 * batches, groups // 2, 2, count, depth)
        away = pick(tall, 1 - place % 2, 2).reshape(-1, depth)
        stay = pick(tall, place % 2, 2).reshape(-1, depth)
        total = lax.ppermute(dot(away, live), "inpair", [(g, g ^ 1) for g in range(groups)])
        total = (dot(stay, live) + total).reshape(2 * batches, groups // 2, count, width)
        bit = 2
        while bit < groups:
            split = total.reshape(2 * batches, total.shape[1] // 2, 2, count, width)
            side = (place // bit) % 2
            keep, give = pick(split, side, 2), pick(split, 1 - side, 2)
            coded = lax.ppermute(shrink(give.reshape(-1, width)), "inpair", [(g, g ^ bit) for g in range(groups)])
            bit *= 2
            if bit < groups:
                total = keep + grow(coded).reshape(keep.shape)
        if p:
            coded = tied(coded, arrived[-1])
        total, blocks = merge(x, keep.reshape(2, batches * count, width), coded, parties)
        merged.append(total)
        arrived.append(lax.all_to_all(blocks, "outpair", split_axis=0, concat_axis=0, tiled=True))

    out = None
    parted = []
    for p in range(parts):
        total, blocks = merged[p], arrived[p]
        if lanes % LANES == 0:
            out = finish(total, blocks, swap_within, vir_energy, occ_energy, out, p, parts)
            continue
        facing = jnp.concatenate([jnp.take(grow(blocks[o]), swap_within, axis=1) for o in range(parties)], axis=1)
        parted.append((total + facing).reshape(2, batches, -1, width))
    if out is not None:
        return out.reshape(batches, share, width)
    whole = jnp.transpose(jnp.concatenate(parted, axis=2), (1, 0, 2, 3)).reshape(batches, share, width)
    return whole / (vir_energy[None, None, :] - occ_energy[:, :, None])


def solution(mesh):
    return jax.shard_map(
        on_device,
        mesh=mesh,
        in_specs=(
            P("inpair", "outpair"),
            P("outpair", None, "inpair"),
            P("inpair", "outpair"),
            P(),
            P(None, "inpair"),
            P("outpair"),
            P(),
        ),
        out_specs=P(None, "inpair", "outpair"),
        check_vma=False,
    )
```

time: 212 us -> 124 us (0.58)
  waiting for transfers between devices: 173 us -> 41.9 us
  starting transfers between devices: 5.55 us -> 49.5 us
  between operations: 14.9 us -> 5.83 us
  local copies, waits for them, and re-layouts: 9.53 us -> 2.74 us
  Pallas kernels: 0 us -> 5.89 us
  other arithmetic: 4.97 us -> 10.1 us
  matrix products: 4.3 us -> 7.23 us
    psum x1 -> x0, waiting for transfers between devices: 103 us -> none  [spread(): return lax.psum(block, axis)]
    reduce_scatter x1 -> x0, waiting for transfers between devices: 44.4 us -> none  [on_device(): lax.psum_scatter(jnp.dot(ordered, weights, preferred_element_type=jnp.flo...]
    ppermute x0 -> x24, starting transfers between devices: none -> 38.3 us  [the longest x6 20.7 us: shift(): lax.ppermute(values, 'outpair', even)]
    ppermute x0 -> x24, waiting for transfers between devices: none -> 28.7 us  [the longest x6 18.5 us: shift(): lax.ppermute(values, 'outpair', even)]
    all_to_all x1 -> x2, waiting for transfers between devices: 25.4 us -> 13.3 us  [on_device(): lax.all_to_all(blocks, 'outpair', split_axis=0, concat_axis=0, tiled=True)]
    another operation x1 -> x26, other arithmetic: 1.88 us -> 7.96 us  [the longest x13 4.14 us: on_device(): held.append(jnp.stack(now))]
    pallas_call x0 -> x4, Pallas kernels: none -> 5.89 us  [the longest x2 3.46 us: finish(): pl.pallas_call(finish_kernel, grid=(1,), out_shape=jax.ShapeDtypeStruct(s...]
    all_to_all x1 -> x2, starting transfers between devices: 5.51 us -> 11.2 us  [on_device(): lax.all_to_all(blocks, 'outpair', split_axis=0, concat_axis=0, tiled=True)]
  transfers between devices with their start and end apart: 3 -> 26, of which waited for: 3 -> 13; matrix products, arithmetic and copies ran while one was open for 1% -> 13% of each run, Pallas kernels for 0% -> 1%
where the time goes in v1:
time: 124 us; the launch traced here: 123 us
  starting transfers between devices  49.5 us (40%)
  waiting for transfers between devices  41.9 us (34%)
  other arithmetic  10.1 us (8%)
  matrix products  7.23 us (6%)
  Pallas kernels  5.89 us (5%)
  between operations  5.83 us (5%)
  local copies, waits for them, and re-layouts  2.74 us (2%)
    ppermute x6, starting transfers between devices, shift(): lax.ppermute(values, 'outpair', even)  20.7 us
    ppermute x6, waiting for transfers between devices, shift(): lax.ppermute(values, 'outpair', even)  18.5 us
    all_to_all x2, waiting for transfers between devices, on_device(): lax.all_to_all(blocks, 'outpair', split_axis=0, concat_axis=0, tiled=True)  13.3 us
    all_to_all x2, starting transfers between devices, on_device(): lax.all_to_all(blocks, 'outpair', split_axis=0, concat_axis=0, tiled=True)  11.2 us
    ppermute x8, waiting for transfers between devices, swap_x(): return lax.ppermute(values, 'outpair', beside)  9.31 us
    ppermute x8, starting transfers between devices, swap_x(): return lax.ppermute(values, 'outpair', beside)  9.04 us
    dot_general x4, matrix products, on_device(): dot = lambda a, w: jnp.dot(a, w, preferred_element_type=jnp.float32)  7.23 us
    ppermute x6, starting transfers between devices, shift(): lax.ppermute(values, 'outpair', odd)  5.44 us
  transfers between devices with their start and end apart: 26, of which 13 were waited for; matrix products, arithmetic and copies ran while one was open for 13% of the time, Pallas kernels for 1%

profile of v1, /device:TPU:0, one launch (start us, length us, event | category | flops | bytes accessed | tf_op | source)
XLA Modules:
  0.0 123.2 jit_solution(3630227827733263128)
XLA Ops:
  0.0 1.3 %dynamic-slice_bitcast_fusion.1 = (bf16[4,64,1024]{2,1,0:T(8,128)(2,1)S(1)}, bf16[4,64,1024]{2,1,0:T(8,128)(2,1)S(1)}) fusion(bf16[4,2,64,1024]{3,2,1,0:T(8,128)(2,1)} %bitcast.174, s32[]{:T(128)S(6)} %select_n.273, s32[]{:T(128)S(6)} %select_n.274), kind=kLoop, calls=%fused_computation.54 | loop fusion | bytes 2097160 | tf_op jit(solution)/shard_map/jit(dynamic_index_in_dim)/squeeze | solution.py:20
  1.4 3.0 %collective-permute-start.2 = (bf16[4,16,1024]{2,1,0:T(8,128)(2,1)S(1)}, bf16[4,16,1024]{2,1,0:T(8,128)(2,1)S(1)}, u32[]{:S(2)}, u32[]{:S(2)}) collective-permute-start(bf16[4,16,1024]{2,1,0:T(8,128)(2,1)S(1)} %get-tuple-element.70), channel_id=1, source_target_pairs={{0,1},{1,0},{2,3},{3,2},{4,5},{5,4},{6,7},{7,6},{8,9},{9,8},{10,11... | collective-permute-start | bytes 393224 | tf_op jit(solution)/shard_map/ppermute | solution.py:164
  4.4 0.6 fusion.48
  9.0 0.7 collective-permute-start.3
  9.6 4.4 %collective-permute-start.4 = (bf16[2,4,16,1024]{3,2,1,0:T(8,128)(2,1)S(1)}, bf16[2,4,16,1024]{3,2,1,0:T(8,128)(2,1)S(1)}, u32[]{:S(2)}, u32[]{:S(2)}) collective-permute-start(bf16[2,4,16,1024]{3,2,1,0:T(8,128)(2,1)S(1)} %pad_maximum_fusion.2), channel_id=1, source_target_pairs={{0,2},{1,3},{2,0},{3,1},{4,6},{5,7},{6,4},{7,5},{8,10},{9,11},{10,... | collective-permute-start | bytes 786440 | tf_op jit(solution)/shard_map/ppermute | solution.py:167
  14.1 0.7 collective-permute-start.1
  16.2 3.6 %collective-permute-done.4 = bf16[2,4,16,1024]{3,2,1,0:T(8,128)(2,1)S(1)} collective-permute-done((bf16[2,4,16,1024]{3,2,1,0:T(8,128)(2,1)S(1)}, bf16[2,4,16,1024]{3,2,1,0:T(8,128)(2,1)S(1)}, u32[]{:S(2)}, u32[]{:S(2)}) %collective-permute-start.4) | collective-permute-done | bytes 262176 | tf_op jit(solution)/shard_map/ppermute | solution.py:167
  19.9 0.7 collective-permute-start.5
  20.6 3.5 %collective-permute-start.6 = (bf16[2,4,16,1024]{3,2,1,0:T(8,128)(2,1)S(1)}, bf16[2,4,16,1024]{3,2,1,0:T(8,128)(2,1)S(1)}, u32[]{:S(2)}, u32[]{:S(2)}) collective-permute-start(bf16[2,4,16,1024]{3,2,1,0:T(8,128)(2,1)S(1)} %pad_maximum_fusion.3), channel_id=1, source_target_pairs={{0,2},{1,3},{2,0},{3,1},{4,6},{5,7},{6,4},{7,5},{8,10},{9,11},{10,... | collective-permute-start | bytes 786440 | tf_op jit(solution)/shard_map/ppermute | solution.py:167
  24.1 0.5 collective-permute-start
  24.6 4.0 %collective-permute-done.6 = bf16[2,4,16,1024]{3,2,1,0:T(8,128)(2,1)S(1)} collective-permute-done((bf16[2,4,16,1024]{3,2,1,0:T(8,128)(2,1)S(1)}, bf16[2,4,16,1024]{3,2,1,0:T(8,128)(2,1)S(1)}, u32[]{:S(2)}, u32[]{:S(2)}) %collective-permute-start.6) | collective-permute-done | bytes 262176 | tf_op jit(solution)/shard_map/ppermute | solution.py:167
  28.7 0.4 collective-permute-done
  29.2 0.7 collective-permute-start.8
  29.8 4.3 %collective-permute-start.9 = (bf16[2,4,16,1024]{3,2,1,0:T(8,128)(2,1)S(1)}, bf16[2,4,16,1024]{3,2,1,0:T(8,128)(2,1)S(1)}, u32[]{:S(2)}, u32[]{:S(2)}) collective-permute-start(bf16[2,4,16,1024]{3,2,1,0:T(8,128)(2,1)S(1)} %pad_maximum_fusion.4), channel_id=1, source_target_pairs={{0,2},{1,3},{2,0},{3,1},{4,6},{5,7},{6,4},{7,5},{8,10},{9,11},{10,... | collective-permute-start | bytes 786440 | tf_op jit(solution)/shard_map/ppermute | solution.py:167
  34.1 0.5 collective-permute-start.7
  34.7 3.8 %collective-permute-done.9 = bf16[2,4,16,1024]{3,2,1,0:T(8,128)(2,1)S(1)} collective-permute-done((bf16[2,4,16,1024]{3,2,1,0:T(8,128)(2,1)S(1)}, bf16[2,4,16,1024]{3,2,1,0:T(8,128)(2,1)S(1)}, u32[]{:S(2)}, u32[]{:S(2)}) %collective-permute-start.9) | collective-permute-done | bytes 262176 | tf_op jit(solution)/shard_map/ppermute | solution.py:167
  38.5 0.6 collective-permute-done.7
  39.2 0.7 collective-permute-start.10
  39.9 3.2 %collective-permute-start.11 = (bf16[2,4,16,1024]{3,2,1,0:T(8,128)(2,1)S(1)}, bf16[2,4,16,1024]{3,2,1,0:T(8,128)(2,1)S(1)}, u32[]{:S(2)}, u32[]{:S(2)}) collective-permute-start(bf16[2,4,16,1024]{3,2,1,0:T(8,128)(2,1)S(1)} %pad_maximum_fusion.5), channel_id=1, source_target_pairs={{0,2},{1,3},{2,0},{3,1},{4,6},{5,7},{6,4},{7,5},{8,10},{9,11},{10,... | collective-permute-start | bytes 786440 | tf_op jit(solution)/shard_map/ppermute | solution.py:167
  43.0 4.3 %collective-permute-done.11 = bf16[2,4,16,1024]{3,2,1,0:T(8,128)(2,1)S(1)} collective-permute-done((bf16[2,4,16,1024]{3,2,1,0:T(8,128)(2,1)S(1)}, bf16[2,4,16,1024]{3,2,1,0:T(8,128)(2,1)S(1)}, u32[]{:S(2)}, u32[]{:S(2)}) %collective-permute-start.11) | collective-permute-done | bytes 262176 | tf_op jit(solution)/shard_map/ppermute | solution.py:167
  47.4 0.7 pad_maximum_fusion.6
  48.1 1.4 %collective-permute-start.12 = (bf16[2,4,16,1024]{3,2,1,0:T(8,128)(2,1)}, bf16[2,4,16,1024]{3,2,1,0:T(8,128)(2,1)}, u32[]{:S(2)}, u32[]{:S(2)}) collective-permute-start(bf16[2,4,16,1024]{3,2,1,0:T(8,128)(2,1)} %pad_maximum_fusion.6), channel_id=1, source_target_pairs={{2,4},{3,5},{4,2},{5,3},{10,12},{11,13},{12,10},{13,11},{18,20},{1... | collective-permute-start | bytes 786440 | tf_op jit(solution)/shard_map/ppermute | solution.py:167
  49.5 4.2 %collective-permute-start.13 = (bf16[2,4,16,1024]{3,2,1,0:T(8,128)(2,1)}, bf16[2,4,16,1024]{3,2,1,0:T(8,128)(2,1)}, u32[]{:S(2)}, u32[]{:S(2)}) collective-permute-start(bf16[2,4,16,1024]{3,2,1,0:T(8,128)(2,1)} %pad_maximum_fusion.6), channel_id=1, source_target_pairs={{0,2},{1,3},{2,0},{3,1},{4,6},{5,7},{6,4},{7,5},{8,10},{9,11},{10,... | collective-permute-start | bytes 786440 | tf_op jit(solution)/shard_map/ppermute | solution.py:167
  53.7 1.2 fusion.16
  54.9 0.8 pad_maximum_fusion.7
  55.7 0.5 collective-permute-start.14
  56.4 1.8 %bitcast_multiply_fusion = bf16[1024,1024]{1,0:T(8,128)(2,1)S(1)} fusion(bf16[1024,1024]{1,0:T(8,128)(2,1)} %param.7, bf16[4,1024]{1,0:T(4,128)(2,1)S(1)} %bitcast.175), kind=kLoop, calls=%fused_computation | loop fusion | flops 1048576 | bytes 4202496 | tf_op jit(solution)/shard_map/mul | solution.py:157
  58.2 1.6 %collective-permute-start.17 = (bf16[2,4,16,1024]{3,2,1,0:T(8,128)(2,1)S(1)}, bf16[2,4,16,1024]{3,2,1,0:T(8,128)(2,1)S(1)}, u32[]{:S(2)}, u32[]{:S(2)}) collective-permute-start(bf16[2,4,16,1024]{3,2,1,0:T(8,128)(2,1)S(1)} %pad_maximum_fusion.10), channel_id=1, source_target_pairs={{0,1},{1,0},{2,3},{3,2},{4,5},{5,4},{6,7},{7,6},{8,9},{9,8},{10,11... | collective-permute-start | bytes 786440 | tf_op jit(solution)/shard_map/ppermute | solution.py:164
  59.9 2.5 %collective-permute-done.14 = bf16[2,4,16,1024]{3,2,1,0:T(8,128)(2,1)} collective-permute-done((bf16[2,4,16,1024]{3,2,1,0:T(8,128)(2,1)}, bf16[2,4,16,1024]{3,2,1,0:T(8,128)(2,1)}, u32[]{:S(2)}, u32[]{:S(2)}) %collective-permute-start.14) | collective-permute-done | bytes 262176 | tf_op jit(solution)/shard_map/ppermute | solution.py:164
  62.4 1.1 fusion.35
  63.6 0.8 pad_maximum_fusion.9
  64.3 1.4 %collective-permute-start.15 = (bf16[2,4,16,1024]{3,2,1,0:T(8,128)(2,1)}, bf16[2,4,16,1024]{3,2,1,0:T(8,128)(2,1)}, u32[]{:S(2)}, u32[]{:S(2)}) collective-permute-start(bf16[2,4,16,1024]{3,2,1,0:T(8,128)(2,1)} %pad_maximum_fusion.9), channel_id=1, source_target_pairs={{2,4},{3,5},{4,2},{5,3},{10,12},{11,13},{12,10},{13,11},{18,20},{1... | collective-permute-start | bytes 786440 | tf_op jit(solution)/shard_map/ppermute | solution.py:167
  65.7 1.1 collective-permute-start.16
  66.8 1.0 maximum_bitcast_fusion.3
  67.8 0.1 pad_maximum_fusion.1
  67.9 0.1 constant_dynamic-slice_fusion.7
  68.0 1.7 %fusion.49 = f32[256,1024]{1,0:T(8,128)} fusion(bf16[256,1024]{1,0:T(8,128)(2,1)S(1)} %bitcast.173, bf16[1024,1024]{1,0:T(8,128)(2,1)S(1)} %bitcast_multiply_fusion), kind=kOutput, calls=%fused_computation.137 | convolution fusion | flops 536870912 | bytes 3670016 | tf_op jit(solution)/shard_map/dot_general | solution.py:194
  69.7 2.7 %collective-permute-done.16 = bf16[2,4,16,1024]{3,2,1,0:T(8,128)(2,1)} collective-permute-done((bf16[2,4,16,1024]{3,2,1,0:T(8,128)(2,1)}, bf16[2,4,16,1024]{3,2,1,0:T(8,128)(2,1)}, u32[]{:S(2)}, u32[]{:S(2)}) %collective-permute-start.16) | collective-permute-done | bytes 262176 | tf_op jit(solution)/shard_map/ppermute | solution.py:167
  72.4 1.2 fusion.33
  73.6 0.2 fusion.22
  73.8 0.2 fusion.25
  74.1 0.6 collective-permute-start.19
  74.7 1.6 %collective-permute-start.18 = (bf16[2,4,16,1024]{3,2,1,0:T(8,128)(2,1)S(1)}, bf16[2,4,16,1024]{3,2,1,0:T(8,128)(2,1)S(1)}, u32[]{:S(2)}, u32[]{:S(2)}) collective-permute-start(bf16[2,4,16,1024]{3,2,1,0:T(8,128)(2,1)S(1)} %pad_maximum_fusion.8), channel_id=1, source_target_pairs={{0,1},{1,0},{2,3},{3,2},{4,5},{5,4},{6,7},{7,6},{8,9},{9,8},{10,11... | collective-permute-start | bytes 786440 | tf_op jit(solution)/shard_map/ppermute | solution.py:164
  76.4 1.9 %convolution_add_fusion.1 = f32[256,1024]{1,0:T(8,128)S(1)} fusion(f32[256,1024]{1,0:T(8,128)} %collective-permute-done.20, bf16[256,1024]{1,0:T(8,128)(2,1)S(1)} %bitcast.170, bf16[1024,1024]{1,0:T(8,128)(2,1)S(1)} %bitcast_multiply_fusion), kind=kOutput, calls=%fused_computation.2 | convolution fusion | flops 537133056 | bytes 4718592 | tf_op jit(solution)/shard_map/dot_general | solution.py:194
  78.5 1.6 %collective-permute-start.21 = (s16[129,1024]{1,0:T(8,128)(2,1)S(1)}, s16[129,1024]{1,0:T(8,128)(2,1)S(1)}, u32[]{:S(2)}, u32[]{:S(2)}) collective-permute-start(s16[129,1024]{1,0:T(8,128)(2,1)S(1)} %pad_add_fusion), channel_id=1, source_target_pairs={{0,16},{8,24},{16,0},{24,8},{1,17},{9,25},{17,1},{25,9},{2,18},{10... | collective-permute-start | bytes 792584 | tf_op jit(solution)/shard_map/ppermute | solution.py:213
  80.1 3.0 %collective-permute-done.19 = bf16[2,4,16,1024]{3,2,1,0:T(8,128)(2,1)S(1)} collective-permute-done((bf16[2,4,16,1024]{3,2,1,0:T(8,128)(2,1)S(1)}, bf16[2,4,16,1024]{3,2,1,0:T(8,128)(2,1)S(1)}, u32[]{:S(2)}, u32[]{:S(2)}) %collective-permute-start.19) | collective-permute-done | bytes 262176 | tf_op jit(solution)/shard_map/ppermute | solution.py:164
  83.0 2.8 %collective-permute-done.18 = bf16[2,4,16,1024]{3,2,1,0:T(8,128)(2,1)S(1)} collective-permute-done((bf16[2,4,16,1024]{3,2,1,0:T(8,128)(2,1)S(1)}, bf16[2,4,16,1024]{3,2,1,0:T(8,128)(2,1)S(1)}, u32[]{:S(2)}, u32[]{:S(2)}) %collective-permute-start.18) | collective-permute-done | bytes 262176 | tf_op jit(solution)/shard_map/ppermute | solution.py:164
  85.9 0.1 pad_maximum_fusion
  86.1 1.2 merge.2
  87.3 0.1 constant_dynamic-slice_fusion.3
  87.4 1.7 %fusion.50 = f32[256,1024]{1,0:T(8,128)} fusion(bf16[256,1024]{1,0:T(8,128)(2,1)S(1)} %bitcast.172, bf16[1024,1024]{1,0:T(8,128)(2,1)S(1)} %bitcast_multiply_fusion), kind=kOutput, calls=%fused_computation.138 | convolution fusion | flops 536870912 | bytes 3670016 | tf_op jit(solution)/shard_map/dot_general | solution.py:194
  89.1 5.5 %all-to-all-start = ((s16[8,144,128]{2,1,0:T(8,128)(2,1)}), s16[8,144,128]{2,1,0:T(8,128)(2,1)S(1)}, u32[]{:S(2)}, u32[]{:S(2)}) async-start(s16[8,144,128]{2,1,0:T(8,128)(2,1)} %get-tuple-element.37), calls=%async_computation | async-start | bytes 589824 | tf_op jit(solution)/shard_map/all_to_all | solution.py:221
  94.6 1.9 %convolution_add_fusion = f32[256,1024]{1,0:T(8,128)S(1)} fusion(f32[256,1024]{1,0:T(8,128)} %collective-permute-done.22, bf16[256,1024]{1,0:T(8,128)(2,1)S(1)} %bitcast.171, bf16[1024,1024]{1,0:T(8,128)(2,1)S(1)} %bitcast_multiply_fusion), kind=kOutput, calls=%fused_computation.1 | convolution fusion | flops 537133056 | bytes 4718592 | tf_op jit(solution)/shard_map/dot_general | solution.py:194
  96.7 1.6 %collective-permute-start.23 = (s16[129,1024]{1,0:T(8,128)(2,1)S(1)}, s16[129,1024]{1,0:T(8,128)(2,1)S(1)}, u32[]{:S(2)}, u32[]{:S(2)}) collective-permute-start(s16[129,1024]{1,0:T(8,128)(2,1)S(1)} %pad_add_fusion.1), channel_id=1, source_target_pairs={{0,16},{8,24},{16,0},{24,8},{1,17},{9,25},{17,1},{25,9},{2,18},{10... | collective-permute-start | bytes 792584 | tf_op jit(solution)/shard_map/ppermute | solution.py:213
  98.4 6.4 %all-to-all-done.blocks_ref = s16[8,144,128]{2,1,0:T(8,128)(2,1)S(1)} async-done(((s16[8,144,128]{2,1,0:T(8,128)(2,1)}), s16[8,144,128]{2,1,0:T(8,128)(2,1)S(1)}, u32[]{:S(2)}, u32[]{:S(2)}) %all-to-all-start) | async-done | bytes 294944 | tf_op jit(solution)/shard_map/all_to_all | solution.py:221
  104.8 0.8 collective-permute-done.23
  105.6 1.2 merge.3
  106.8 5.7 %all-to-all-start.1 = ((s16[8,144,128]{2,1,0:T(8,128)(2,1)}), s16[8,144,128]{2,1,0:T(8,128)(2,1)S(1)}, u32[]{:S(2)}, u32[]{:S(2)}) async-start(s16[8,144,128]{2,1,0:T(8,128)(2,1)} %get-tuple-element.40), calls=%async_computation.1 | async-start | bytes 589824 | tf_op jit(solution)/shard_map/all_to_all | solution.py:221
  112.6 0.1 reshape.182
  112.7 0.1 reshape.186.occ_ref
  112.8 0.1 reshape.187.occ_ref
  112.9 1.7 %finish.2.rest_0_ = f32[2,2,2,32,1024]{4,3,2,1,0:T(8,128)} custom-call(f32[128,1024]{1,0:T(8,128)S(1)} %get-tuple-element.35.total_ref, s16[8,144,128]{2,1,0:T(8,128)(2,1)S(1)} %all-to-all-done.blocks_ref, s32[1,128]{1,0:T(1,128)S(1)} %bitcast.162, f32[1,1024]{1,0:T(1,128)S(1)} %bitcast.160, f32[128,1]{1,0:T(8,128)S(1)} %reshape.187.occ_ref), custom_call_target="tpu_custom_call" | custom-call | tf_op jit(solution)/shard_map/finish/pallas_call | solution.py:122
  114.6 6.8 %all-to-all-done.1.blocks_ref = s16[8,144,128]{2,1,0:T(8,128)(2,1)S(1)} async-done(((s16[8,144,128]{2,1,0:T(8,128)(2,1)}), s16[8,144,128]{2,1,0:T(8,128)(2,1)S(1)}, u32[]{:S(2)}, u32[]{:S(2)}) %all-to-all-start.1) | async-done | bytes 294944 | tf_op jit(solution)/shard_map/all_to_all | solution.py:221
  121.5 1.7 %finish.3 = f32[2,2,2,32,1024]{4,3,2,1,0:T(8,128)} custom-call(f32[128,1024]{1,0:T(8,128)S(1)} %get-tuple-element.39.total_ref, s16[8,144,128]{2,1,0:T(8,128)(2,1)S(1)} %all-to-all-done.1.blocks_ref, s32[1,128]{1,0:T(1,128)S(1)} %bitcast.163, f32[1,1024]{1,0:T(1,128)S(1)} %bitcast.161, ...), custom_call_target="tpu_custom_call", output_to_operand_aliasing={{}: (5, {})} | custom-call | tf_op jit(solution)/shard_map/finish/pallas_call | solution.py:122
  (79 shorter events, 1.2 us)
Async XLA Ops:
  0.0 4.4 %copy-start.12 = (s32[2]{0:T(128)S(1)}, s32[2]{0:T(128)}, u32[]{:S(2)}) copy-start(s32[2]{0:T(128)} %param.10) | copy-start | bytes 28
  1.4 7.5 %collective-permute-start.2 = (bf16[4,16,1024]{2,1,0:T(8,128)(2,1)S(1)}, bf16[4,16,1024]{2,1,0:T(8,128)(2,1)S(1)}, u32[]{:S(2)}, u32[]{:S(2)}) collective-permute-start(bf16[4,16,1024]{2,1,0:T(8,128)(2,1)S(1)} %get-tuple-element.70), channel_id=1, source_target_pairs={{0,1},{1,0},{2,3},{3,2},{4,5},{5,4},{6,7},{7,6},{8,9},{9,8},{10,11... | collective-permute-start | bytes 393224 | tf_op jit(solution)/shard_map/ppermute | solution.py:164
  9.0 7.2 %collective-permute-start.3 = (bf16[2,4,16,1024]{3,2,1,0:T(8,128)(2,1)S(1)}, bf16[2,4,16,1024]{3,2,1,0:T(8,128)(2,1)S(1)}, u32[]{:S(2)}, u32[]{:S(2)}) collective-permute-start(bf16[2,4,16,1024]{3,2,1,0:T(8,128)(2,1)S(1)} %pad_maximum_fusion.2), channel_id=1, source_target_pairs={{2,4},{3,5},{4,2},{5,3},{10,12},{11,13},{12,10},{13,11},{18,20},{1... | collective-permute-start | bytes 786440 | tf_op jit(solution)/shard_map/ppermute | solution.py:167
  9.6 10.2 %collective-permute-start.4 = (bf16[2,4,16,1024]{3,2,1,0:T(8,128)(2,1)S(1)}, bf16[2,4,16,1024]{3,2,1,0:T(8,128)(2,1)S(1)}, u32[]{:S(2)}, u32[]{:S(2)}) collective-permute-start(bf16[2,4,16,1024]{3,2,1,0:T(8,128)(2,1)S(1)} %pad_maximum_fusion.2), channel_id=1, source_target_pairs={{0,2},{1,3},{2,0},{3,1},{4,6},{5,7},{6,4},{7,5},{8,10},{9,11},{10,... | collective-permute-start | bytes 786440 | tf_op jit(solution)/shard_map/ppermute | solution.py:167
  14.1 5.7 %collective-permute-start.1 = (bf16[4,16,1024]{2,1,0:T(8,128)(2,1)S(1)}, bf16[4,16,1024]{2,1,0:T(8,128)(2,1)S(1)}, u32[]{:S(2)}, u32[]{:S(2)}) collective-permute-start(bf16[4,16,1024]{2,1,0:T(8,128)(2,1)S(1)} %get-tuple-element.71), channel_id=1, source_target_pairs={{0,1},{1,0},{2,3},{3,2},{4,5},{5,4},{6,7},{7,6},{8,9},{9,8},{10,11... | collective-permute-start | bytes 393224 | tf_op jit(solution)/shard_map/ppermute | solution.py:164
  19.9 23.1 %copy-start.11 = (s32[4,4]{1,0:T(4,128)S(1)}, s32[4,4]{1,0:T(4,128)}, u32[]{:S(2)}) copy-start(s32[4,4]{1,0:T(4,128)} %param.9) | copy-start | bytes 196
  19.9 4.7 %collective-permute-start.5 = (bf16[2,4,16,1024]{3,2,1,0:T(8,128)(2,1)S(1)}, bf16[2,4,16,1024]{3,2,1,0:T(8,128)(2,1)S(1)}, u32[]{:S(2)}, u32[]{:S(2)}) collective-permute-start(bf16[2,4,16,1024]{3,2,1,0:T(8,128)(2,1)S(1)} %pad_maximum_fusion.3), channel_id=1, source_target_pairs={{2,4},{3,5},{4,2},{5,3},{10,12},{11,13},{12,10},{13,11},{18,20},{1... | collective-permute-start | bytes 786440 | tf_op jit(solution)/shard_map/ppermute | solution.py:167
  20.6 8.1 %collective-permute-start.6 = (bf16[2,4,16,1024]{3,2,1,0:T(8,128)(2,1)S(1)}, bf16[2,4,16,1024]{3,2,1,0:T(8,128)(2,1)S(1)}, u32[]{:S(2)}, u32[]{:S(2)}) collective-permute-start(bf16[2,4,16,1024]{3,2,1,0:T(8,128)(2,1)S(1)} %pad_maximum_fusion.3), channel_id=1, source_target_pairs={{0,2},{1,3},{2,0},{3,1},{4,6},{5,7},{6,4},{7,5},{8,10},{9,11},{10,... | collective-permute-start | bytes 786440 | tf_op jit(solution)/shard_map/ppermute | solution.py:167
  24.1 5.0 %collective-permute-start = (bf16[4,16,1024]{2,1,0:T(8,128)(2,1)S(1)}, bf16[4,16,1024]{2,1,0:T(8,128)(2,1)S(1)}, u32[]{:S(2)}, u32[]{:S(2)}) collective-permute-start(bf16[4,16,1024]{2,1,0:T(8,128)(2,1)S(1)} %get-tuple-element.72), channel_id=1, source_target_pairs={{0,1},{1,0},{2,3},{3,2},{4,5},{5,4},{6,7},{7,6},{8,9},{9,8},{10,11... | collective-permute-start | bytes 393224 | tf_op jit(solution)/shard_map/ppermute | solution.py:164
  29.2 5.5 %collective-permute-start.8 = (bf16[2,4,16,1024]{3,2,1,0:T(8,128)(2,1)S(1)}, bf16[2,4,16,1024]{3,2,1,0:T(8,128)(2,1)S(1)}, u32[]{:S(2)}, u32[]{:S(2)}) collective-permute-start(bf16[2,4,16,1024]{3,2,1,0:T(8,128)(2,1)S(1)} %pad_maximum_fusion.4), channel_id=1, source_target_pairs={{2,4},{3,5},{4,2},{5,3},{10,12},{11,13},{12,10},{13,11},{18,20},{1... | collective-permute-start | bytes 786440 | tf_op jit(solution)/shard_map/ppermute | solution.py:167
  29.8 8.6 %collective-permute-start.9 = (bf16[2,4,16,1024]{3,2,1,0:T(8,128)(2,1)S(1)}, bf16[2,4,16,1024]{3,2,1,0:T(8,128)(2,1)S(1)}, u32[]{:S(2)}, u32[]{:S(2)}) collective-permute-start(bf16[2,4,16,1024]{3,2,1,0:T(8,128)(2,1)S(1)} %pad_maximum_fusion.4), channel_id=1, source_target_pairs={{0,2},{1,3},{2,0},{3,1},{4,6},{5,7},{6,4},{7,5},{8,10},{9,11},{10,... | collective-permute-start | bytes 786440 | tf_op jit(solution)/shard_map/ppermute | solution.py:167
  34.1 5.0 %collective-permute-start.7 = (bf16[4,16,1024]{2,1,0:T(8,128)(2,1)S(1)}, bf16[4,16,1024]{2,1,0:T(8,128)(2,1)S(1)}, u32[]{:S(2)}, u32[]{:S(2)}) collective-permute-start(bf16[4,16,1024]{2,1,0:T(8,128)(2,1)S(1)} %get-tuple-element.69), channel_id=1, source_target_pairs={{0,1},{1,0},{2,3},{3,2},{4,5},{5,4},{6,7},{7,6},{8,9},{9,8},{10,11... | collective-permute-start | bytes 393224 | tf_op jit(solution)/shard_map/ppermute | solution.py:164
  39.1 28.7 %copy-start.2 = (bf16[4,16,1024]{2,1,0:T(8,128)(2,1)}, bf16[4,16,1024]{2,1,0:T(8,128)(2,1)S(1)}, u32[]{:S(2)}) copy-start(bf16[4,16,1024]{2,1,0:T(8,128)(2,1)S(1)} %get-tuple-element.50) | copy-start | bytes 393220
  39.2 3.8 %collective-permute-start.10 = (bf16[2,4,16,1024]{3,2,1,0:T(8,128)(2,1)S(1)}, bf16[2,4,16,1024]{3,2,1,0:T(8,128)(2,1)S(1)}, u32[]{:S(2)}, u32[]{:S(2)}) collective-permute-start(bf16[2,4,16,1024]{3,2,1,0:T(8,128)(2,1)S(1)} %pad_maximum_fusion.5), channel_id=1, source_target_pairs={{2,4},{3,5},{4,2},{5,3},{10,12},{11,13},{12,10},{13,11},{18,20},{1... | collective-permute-start | bytes 786440 | tf_op jit(solution)/shard_map/ppermute | solution.py:167
  39.9 7.5 %collective-permute-start.11 = (bf16[2,4,16,1024]{3,2,1,0:T(8,128)(2,1)S(1)}, bf16[2,4,16,1024]{3,2,1,0:T(8,128)(2,1)S(1)}, u32[]{:S(2)}, u32[]{:S(2)}) collective-permute-start(bf16[2,4,16,1024]{3,2,1,0:T(8,128)(2,1)S(1)} %pad_maximum_fusion.5), channel_id=1, source_target_pairs={{0,2},{1,3},{2,0},{3,1},{4,6},{5,7},{6,4},{7,5},{8,10},{9,11},{10,... | collective-permute-start | bytes 786440 | tf_op jit(solution)/shard_map/ppermute | solution.py:167
  48.1 11.7 %collective-permute-start.12 = (bf16[2,4,16,1024]{3,2,1,0:T(8,128)(2,1)}, bf16[2,4,16,1024]{3,2,1,0:T(8,128)(2,1)}, u32[]{:S(2)}, u32[]{:S(2)}) collective-permute-start(bf16[2,4,16,1024]{3,2,1,0:T(8,128)(2,1)} %pad_maximum_fusion.6), channel_id=1, source_target_pairs={{2,4},{3,5},{4,2},{5,3},{10,12},{11,13},{12,10},{13,11},{18,20},{1... | collective-permute-start | bytes 786440 | tf_op jit(solution)/shard_map/ppermute | solution.py:167
  49.5 10.3 %collective-permute-start.13 = (bf16[2,4,16,1024]{3,2,1,0:T(8,128)(2,1)}, bf16[2,4,16,1024]{3,2,1,0:T(8,128)(2,1)}, u32[]{:S(2)}, u32[]{:S(2)}) collective-permute-start(bf16[2,4,16,1024]{3,2,1,0:T(8,128)(2,1)} %pad_maximum_fusion.6), channel_id=1, source_target_pairs={{0,2},{1,3},{2,0},{3,1},{4,6},{5,7},{6,4},{7,5},{8,10},{9,11},{10,... | collective-permute-start | bytes 786440 | tf_op jit(solution)/shard_map/ppermute | solution.py:167
  54.9 1.4 %copy-start.6 = (bf16[1,4,16,1024]{3,2,1,0:T(8,128)(2,1)}, bf16[1,4,16,1024]{3,2,1,0:T(8,128)(2,1)S(1)}, u32[]{:S(2)}) copy-start(bf16[1,4,16,1024]{3,2,1,0:T(8,128)(2,1)S(1)} %get-tuple-element.80) | copy-start | bytes 393220
  54.9 1.4 %copy-start.8 = (bf16[1,4,16,1024]{3,2,1,0:T(8,128)(2,1)}, bf16[1,4,16,1024]{3,2,1,0:T(8,128)(2,1)S(1)}, u32[]{:S(2)}) copy-start(bf16[1,4,16,1024]{3,2,1,0:T(8,128)(2,1)S(1)} %get-tuple-element.89) | copy-start | bytes 393220
  55.7 6.7 %collective-permute-start.14 = (bf16[2,4,16,1024]{3,2,1,0:T(8,128)(2,1)}, bf16[2,4,16,1024]{3,2,1,0:T(8,128)(2,1)}, u32[]{:S(2)}, u32[]{:S(2)}) collective-permute-start(bf16[2,4,16,1024]{3,2,1,0:T(8,128)(2,1)} %pad_maximum_fusion.7), channel_id=1, source_target_pairs={{0,1},{1,0},{2,3},{3,2},{4,5},{5,4},{6,7},{7,6},{8,9},{9,8},{10,11... | collective-permute-start | bytes 786440 | tf_op jit(solution)/shard_map/ppermute | solution.py:164
  56.3 1.8 %copy-start.5 = (bf16[1,4,16,1024]{3,2,1,0:T(8,128)(2,1)S(1)}, bf16[1,4,16,1024]{3,2,1,0:T(8,128)(2,1)}, u32[]{:S(2)}) copy-start(bf16[1,4,16,1024]{3,2,1,0:T(8,128)(2,1)} %get-tuple-element.79) | copy-start | bytes 393220
  56.4 1.8 %copy-start.10 = (bf16[1,4,16,1024]{3,2,1,0:T(8,128)(2,1)S(1)}, bf16[1,4,16,1024]{3,2,1,0:T(8,128)(2,1)}, u32[]{:S(2)}) copy-start(bf16[1,4,16,1024]{3,2,1,0:T(8,128)(2,1)} %get-tuple-element.90) | copy-start | bytes 393220
  56.4 3.4 %copy-start.7 = (bf16[1,4,16,1024]{3,2,1,0:T(8,128)(2,1)S(1)}, bf16[1,4,16,1024]{3,2,1,0:T(8,128)(2,1)}, u32[]{:S(2)}) copy-start(bf16[1,4,16,1024]{3,2,1,0:T(8,128)(2,1)} %copy-done.6) | copy-start | bytes 393220
  56.4 3.4 %copy-start.9 = (bf16[1,4,16,1024]{3,2,1,0:T(8,128)(2,1)S(1)}, bf16[1,4,16,1024]{3,2,1,0:T(8,128)(2,1)}, u32[]{:S(2)}) copy-start(bf16[1,4,16,1024]{3,2,1,0:T(8,128)(2,1)} %copy-done.8) | copy-start | bytes 393220
  58.2 8.6 %collective-permute-start.17 = (bf16[2,4,16,1024]{3,2,1,0:T(8,128)(2,1)S(1)}, bf16[2,4,16,1024]{3,2,1,0:T(8,128)(2,1)S(1)}, u32[]{:S(2)}, u32[]{:S(2)}) collective-permute-start(bf16[2,4,16,1024]{3,2,1,0:T(8,128)(2,1)S(1)} %pad_maximum_fusion.10), channel_id=1, source_target_pairs={{0,1},{1,0},{2,3},{3,2},{4,5},{5,4},{6,7},{7,6},{8,9},{9,8},{10,11... | collective-permute-start | bytes 786440 | tf_op jit(solution)/shard_map/ppermute | solution.py:164
  63.5 4.4 %copy-start.3 = (bf16[1,4,16,1024]{3,2,1,0:T(8,128)(2,1)}, bf16[1,4,16,1024]{3,2,1,0:T(8,128)(2,1)S(1)}, u32[]{:S(2)}) copy-start(bf16[1,4,16,1024]{3,2,1,0:T(8,128)(2,1)S(1)} %get-tuple-element.65) | copy-start | bytes 393220
  63.5 4.4 %copy-start.4 = (bf16[1,4,16,1024]{3,2,1,0:T(8,128)(2,1)}, bf16[1,4,16,1024]{3,2,1,0:T(8,128)(2,1)S(1)}, u32[]{:S(2)}) copy-start(bf16[1,4,16,1024]{3,2,1,0:T(8,128)(2,1)S(1)} %get-tuple-element.66) | copy-start | bytes 393220
  64.3 5.4 %collective-permute-start.15 = (bf16[2,4,16,1024]{3,2,1,0:T(8,128)(2,1)}, bf16[2,4,16,1024]{3,2,1,0:T(8,128)(2,1)}, u32[]{:S(2)}, u32[]{:S(2)}) collective-permute-start(bf16[2,4,16,1024]{3,2,1,0:T(8,128)(2,1)} %pad_maximum_fusion.9), channel_id=1, source_target_pairs={{2,4},{3,5},{4,2},{5,3},{10,12},{11,13},{12,10},{13,11},{18,20},{1... | collective-permute-start | bytes 786440 | tf_op jit(solution)/shard_map/ppermute | solution.py:167
  65.7 6.7 %collective-permute-start.16 = (bf16[2,4,16,1024]{3,2,1,0:T(8,128)(2,1)}, bf16[2,4,16,1024]{3,2,1,0:T(8,128)(2,1)}, u32[]{:S(2)}, u32[]{:S(2)}) collective-permute-start(bf16[2,4,16,1024]{3,2,1,0:T(8,128)(2,1)} %pad_maximum_fusion.9), channel_id=1, source_target_pairs={{0,2},{1,3},{2,0},{3,1},{4,6},{5,7},{6,4},{7,5},{8,10},{9,11},{10,... | collective-permute-start | bytes 786440 | tf_op jit(solution)/shard_map/ppermute | solution.py:167
  69.7 6.6 %collective-permute-start.20 = (f32[256,1024]{1,0:T(8,128)}, f32[256,1024]{1,0:T(8,128)}, u32[]{:S(2)}, u32[]{:S(2)}) collective-permute-start(f32[256,1024]{1,0:T(8,128)} %fusion.49), channel_id=1, source_target_pairs={{0,8},{8,0},{16,24},{24,16},{1,9},{9,1},{17,25},{25,17},{2,10},{10... | collective-permute-start | bytes 3145736 | tf_op jit(solution)/shard_map/ppermute | solution.py:206
  74.1 8.9 %collective-permute-start.19 = (bf16[2,4,16,1024]{3,2,1,0:T(8,128)(2,1)S(1)}, bf16[2,4,16,1024]{3,2,1,0:T(8,128)(2,1)S(1)}, u32[]{:S(2)}, u32[]{:S(2)}) collective-permute-start(bf16[2,4,16,1024]{3,2,1,0:T(8,128)(2,1)S(1)} %pad_maximum_fusion.11), channel_id=1, source_target_pairs={{0,1},{1,0},{2,3},{3,2},{4,5},{5,4},{6,7},{7,6},{8,9},{9,8},{10,11... | collective-permute-start | bytes 786440 | tf_op jit(solution)/shard_map/ppermute | solution.py:164
  74.7 11.1 %collective-permute-start.18 = (bf16[2,4,16,1024]{3,2,1,0:T(8,128)(2,1)S(1)}, bf16[2,4,16,1024]{3,2,1,0:T(8,128)(2,1)S(1)}, u32[]{:S(2)}, u32[]{:S(2)}) collective-permute-start(bf16[2,4,16,1024]{3,2,1,0:T(8,128)(2,1)S(1)} %pad_maximum_fusion.8), channel_id=1, source_target_pairs={{0,1},{1,0},{2,3},{3,2},{4,5},{5,4},{6,7},{7,6},{8,9},{9,8},{10,11... | collective-permute-start | bytes 786440 | tf_op jit(solution)/shard_map/ppermute | solution.py:164
  78.5 7.6 %collective-permute-start.21 = (s16[129,1024]{1,0:T(8,128)(2,1)S(1)}, s16[129,1024]{1,0:T(8,128)(2,1)S(1)}, u32[]{:S(2)}, u32[]{:S(2)}) collective-permute-start(s16[129,1024]{1,0:T(8,128)(2,1)S(1)} %pad_add_fusion), channel_id=1, source_target_pairs={{0,16},{8,24},{16,0},{24,8},{1,17},{9,25},{17,1},{25,9},{2,18},{10... | collective-permute-start | bytes 792584 | tf_op jit(solution)/shard_map/ppermute | solution.py:213
  89.1 5.5 %collective-permute-start.22 = (f32[256,1024]{1,0:T(8,128)}, f32[256,1024]{1,0:T(8,128)}, u32[]{:S(2)}, u32[]{:S(2)}) collective-permute-start(f32[256,1024]{1,0:T(8,128)} %fusion.50), channel_id=1, source_target_pairs={{0,8},{8,0},{16,24},{24,16},{1,9},{9,1},{17,25},{25,17},{2,10},{10... | collective-permute-start | bytes 3145736 | tf_op jit(solution)/shard_map/ppermute | solution.py:206
  89.1 15.7 %all-to-all-start = ((s16[8,144,128]{2,1,0:T(8,128)(2,1)}), s16[8,144,128]{2,1,0:T(8,128)(2,1)S(1)}, u32[]{:S(2)}, u32[]{:S(2)}) async-start(s16[8,144,128]{2,1,0:T(8,128)(2,1)} %get-tuple-element.37), calls=%async_computation | async-start | bytes 589824 | tf_op jit(solution)/shard_map/all_to_all | solution.py:221
  96.6 15.9 %copy-start.13 = (f32[2,128]{1,0:T(2,128)S(1)}, f32[2,128]{1,0:T(2,128)}, u32[]{:S(2)}) copy-start(f32[2,128]{1,0:T(2,128)} %param.11) | copy-start | bytes 3076
  96.6 16.3 %copy-start = (f32[1024]{0:T(1024)S(1)}, f32[1024]{0:T(1024)}, u32[]{:S(2)}) copy-start(f32[1024]{0:T(1024)} %param.12) | copy-start | bytes 12292
  96.6 16.3 %copy-start.1 = (s32[128]{0:T(128)S(1)}, s32[128]{0:T(128)}, u32[]{:S(2)}) copy-start(s32[128]{0:T(128)} %param.13) | copy-start | bytes 1540
  96.7 8.9 %collective-permute-start.23 = (s16[129,1024]{1,0:T(8,128)(2,1)S(1)}, s16[129,1024]{1,0:T(8,128)(2,1)S(1)}, u32[]{:S(2)}, u32[]{:S(2)}) collective-permute-start(s16[129,1024]{1,0:T(8,128)(2,1)S(1)} %pad_add_fusion.1), channel_id=1, source_target_pairs={{0,16},{8,24},{16,0},{24,8},{1,17},{9,25},{17,1},{25,9},{2,18},{10... | collective-permute-start | bytes 792584 | tf_op jit(solution)/shard_map/ppermute | solution.py:213
  106.8 14.6 %all-to-all-start.1 = ((s16[8,144,128]{2,1,0:T(8,128)(2,1)}), s16[8,144,128]{2,1,0:T(8,128)(2,1)S(1)}, u32[]{:S(2)}, u32[]{:S(2)}) async-start(s16[8,144,128]{2,1,0:T(8,128)(2,1)} %get-tuple-element.40), calls=%async_computation.1 | async-start | bytes 589824 | tf_op jit(solution)/shard_map/all_to_all | solution.py:221

commit v2 on v1

v2 whole, which is shorter than its diff:
```python
import jax
import jax.numpy as jnp
from jax import lax
from jax.experimental import pallas as pl
from jax.experimental.pallas import tpu as pltpu
from jax.sharding import PartitionSpec as P

CHUNKS = 4
PARTS = 2
LEVELS = 32767.0
OCTAVE = 128.0
LANES = 128
TILE_ROWS = 16
WIDE = 4
VMEM = 8 * 1024 * 1024
LONG = pl.CostEstimate(flops=20_000_000_000, bytes_accessed=0, transcendentals=0)


def pick(array, index, axis):
    return lax.dynamic_index_in_dim(array, index, axis, keepdims=False)


def tied(values, *others):
    return lax.optimization_barrier((values, *others))[0]


def codes_of(values):
    top = jnp.max(jnp.abs(values), axis=0, keepdims=True)
    code = jnp.ceil(jnp.log2(jnp.maximum(top, 1e-30)) * OCTAVE)
    scaled = jnp.round(values * (LEVELS * jnp.exp2(code * (-1.0 / OCTAVE))))
    return jnp.clip(scaled, -LEVELS, LEVELS), code


def step_of(code):
    return jnp.exp2(code.astype(jnp.float32) * (1.0 / OCTAVE)) * (1.0 / LEVELS)


def shrink(values):
    scaled, code = codes_of(values)
    return jnp.concatenate([scaled.astype(jnp.int16), code.astype(jnp.int16)], axis=0)


def grow(coded):
    return coded[:-1].astype(jnp.float32) * step_of(coded[-1:])


def times_kernel(a_ref, w_ref, out_ref):
    out_ref[...] = jnp.dot(a_ref[...], w_ref[...], preferred_element_type=jnp.float32)


def times(a, w, aligned):
    if not aligned:
        return jnp.dot(a, w, preferred_element_type=jnp.float32)
    vmem = pl.BlockSpec(memory_space=pltpu.VMEM)
    return pl.pallas_call(
        times_kernel,
        out_shape=jax.ShapeDtypeStruct((a.shape[0], w.shape[1]), jnp.float32),
        in_specs=[vmem, vmem],
        out_specs=vmem,
        cost_estimate=LONG,
        compiler_params=pltpu.CompilerParams(vmem_limit_bytes=VMEM),
        name="times",
    )(a, w)


def settle_kernel(side_ref, here_ref, there_ref, keep_ref, coded_ref):
    side = side_ref[0]
    parts, _, rows, width = here_ref.shape
    lanes = LANES

    for o in range(width // lanes):
        at = slice(o * lanes, (o + 1) * lanes)
        give = []
        for p in range(parts):
            pair = [here_ref[p, k, :, at] + there_ref[p, k, :, at] for k in range(2)]
            keep_ref[p * rows : (p + 1) * rows, at] = jnp.where(side == 0, pair[0], pair[1])
            give.append(jnp.where(side == 0, pair[1], pair[0]))
        scaled, code = codes_of(jnp.concatenate(give, axis=0))
        coded_ref[: parts * rows, at] = scaled.astype(jnp.int32).astype(jnp.int16)
        coded_ref[parts * rows :, at] = jnp.broadcast_to(code, (TILE_ROWS, lanes)).astype(jnp.int32).astype(jnp.int16)


def settle(side, here, there):
    parts, _, rows, width = here.shape
    vmem = pl.BlockSpec(memory_space=pltpu.VMEM)
    return pl.pallas_call(
        settle_kernel,
        out_shape=(
            jax.ShapeDtypeStruct((parts * rows, width), jnp.float32),
            jax.ShapeDtypeStruct((parts * rows + TILE_ROWS, width), jnp.int16),
        ),
        in_specs=[pl.BlockSpec(memory_space=pltpu.SMEM), vmem, vmem],
        out_specs=(vmem, vmem),
        compiler_params=pltpu.CompilerParams(vmem_limit_bytes=VMEM),
        name="settle",
    )(side, here, there)


def merge_kernel(left_ref, keep_ref, coded_ref, total_ref, blocks_ref):
    left = left_ref[0] == 1
    _, rows, _ = keep_ref.shape
    parties, _, lanes = blocks_ref.shape

    for o in range(parties):
        at = slice(o * lanes, (o + 1) * lanes)
        step = step_of(coded_ref[2 * rows : 2 * rows + 1, at].astype(jnp.int32))
        first = keep_ref[0, :, at] + coded_ref[:rows, at].astype(jnp.float32) * step
        second = keep_ref[1, :, at] + coded_ref[rows : 2 * rows, at].astype(jnp.float32) * step
        total = jnp.concatenate([jnp.where(left, first, second), jnp.where(left, second, first)], axis=0)
        total_ref[:, at] = total
        scaled, code = codes_of(total)
        blocks_ref[o, : 2 * rows] = scaled.astype(jnp.int32).astype(jnp.int16)
        blocks_ref[o, 2 * rows :] = jnp.broadcast_to(code, (TILE_ROWS, lanes)).astype(jnp.int32).astype(jnp.int16)


def merge(left, left_word, keep, coded, parties, aligned):
    _, rows, width = keep.shape
    lanes = width // parties
    if not aligned:
        total = keep + grow(coded).reshape(keep.shape)
        total = jnp.where(left, total, total[::-1]).reshape(2 * rows, width)
        coded = shrink(total)
        return total, jnp.stack([coded[:, o * lanes : (o + 1) * lanes] for o in range(parties)])
    vmem = pl.BlockSpec(memory_space=pltpu.VMEM)
    return pl.pallas_call(
        merge_kernel,
        out_shape=(
            jax.ShapeDtypeStruct((2 * rows, width), jnp.float32),
            jax.ShapeDtypeStruct((parties, 2 * rows + TILE_ROWS, lanes), jnp.int16),
        ),
        in_specs=[pl.BlockSpec(memory_space=pltpu.SMEM), vmem, vmem],
        out_specs=(vmem, vmem),
        cost_estimate=LONG,
        compiler_params=pltpu.CompilerParams(vmem_limit_bytes=VMEM),
        name="merge",
    )(left_word, keep, coded)


def finish_kernel(part, total_ref, blocks_ref, swap_ref, vir_ref, occ_ref, *rest):
    out_ref = rest[-1]
    batches, _, _, count, _ = out_ref.shape
    wide, padded, lanes = blocks_ref.shape
    rows = padded - TILE_ROWS
    half = occ_ref.shape[1] // 2
    swap = jnp.broadcast_to(swap_ref[...], (rows, lanes))
    occ = [jnp.transpose(jnp.broadcast_to(occ_ref[b : b + 1], (lanes, 2 * half))) for b in range(batches)]
    occ = [occ[b][h * half + part * count : h * half + (part + 1) * count] for h in range(2) for b in range(batches)]
    occ = jnp.concatenate(occ, axis=0)

    for o in range(wide):
        at = slice(o * lanes, (o + 1) * lanes)
        facing = blocks_ref[o, :rows].astype(jnp.float32) * step_of(blocks_ref[o, rows : rows + 1].astype(jnp.int32))
        both = total_ref[:, at] + jnp.take_along_axis(facing, swap, axis=1)
        both = both / (vir_ref[:, at] - occ)
        for h in range(2):
            for b in range(batches):
                first = (h * batches + b) * count
                out_ref[b, h, 0, :, at] = both[first : first + count]


def finish(total, blocks, swap_within, vir_energy, occ_energy, out, part, parts):
    rows, width = total.shape
    parties, padded, lanes = blocks.shape
    batches = occ_energy.shape[0]
    count = rows // 2 // batches
    wide = min(WIDE, parties)
    args = [total, blocks, swap_within.reshape(1, lanes), vir_energy.reshape(1, width), occ_energy]
    specs = [
        pl.BlockSpec((rows, wide * lanes), lambda i: (0, i)),
        pl.BlockSpec((wide, padded, lanes), lambda i: (i, 0, 0)),
        pl.BlockSpec((1, lanes), lambda i: (0, 0)),
        pl.BlockSpec((1, wide * lanes), lambda i: (0, i)),
        pl.BlockSpec(occ_energy.shape, lambda i: (0, 0)),
    ]
    alias = {}
    if out is not None:
        alias = {len(args): 0}
        args.append(out)
        specs.append(pl.BlockSpec(memory_space=pl.ANY))
    return pl.pallas_call(
        lambda *refs: finish_kernel(part, *refs),
        grid=(parties // wide,),
        out_shape=jax.ShapeDtypeStruct((batches, 2, parts, count, width), jnp.float32),
        in_specs=specs,
        out_specs=pl.BlockSpec((batches, 2, 1, count, wide * lanes), lambda i: (0, 0, part, 0, i)),
        input_output_aliases=alias,
        cost_estimate=LONG,
        compiler_params=pltpu.CompilerParams(vmem_limit_bytes=VMEM),
        name="finish",
    )(*args)


def on_device(integrals, amplitudes, tile_live, batch_owner, occ_energy, vir_energy, swap_within):
    parties, groups = lax.axis_size("outpair"), lax.axis_size("inpair")
    nz, bits = parties // 2, groups.bit_length() - 1
    batches = batch_owner.shape[0]
    _, rows, depth = amplitudes.shape
    width = integrals.shape[1]
    lanes = width // parties
    share = rows // groups
    half = share // 2
    parts, chunks = (PARTS, CHUNKS) if half % (16 * CHUNKS) == 0 else (1, 1)
    deep = half // chunks
    aligned = lanes % LANES == 0 and share % LANES == 0 and bits == 2
    beside = [(o, o ^ 1) for o in range(parties)]
    even = [(o, o ^ 2) for o in range(parties) if (o ^ 2) < parties]
    odd = [(o, ((o // 2 + 1) ^ 1) * 2 - 2 + o % 2) for o in range(parties)]
    odd = [(o, t) for o, t in odd if 0 <= t < parties]

    def swap_x(values):
        return lax.ppermute(values, "outpair", beside)

    def shift(values):
        return lax.ppermute(values, "outpair", odd), lax.ppermute(values, "outpair", even)

    def cut(a, c):
        return a[:, c * deep : (c + 1) * deep]

    me, place = lax.axis_index("outpair").astype(jnp.uint32), lax.axis_index("inpair").astype(jnp.uint32)
    x, z = me & 1, me >> 1
    stored = amplitudes[0].reshape(groups, 2, half, depth)
    other = pick(stored, 1 - x, 1)
    came = [swap_x(cut(other, c)) for c in range(chunks)]

    owner = [batch_owner[b].astype(jnp.uint32) for b in range(batches)]
    scalars = dict(
        x=x,
        left=x == 0,
        own=[z == o >> 1 for o in owner],
        mine=[x == o & 1 for o in owner],
        from_even=[(z > o >> 1) == (z & 1 == 1) for o in owner],
        far=[jnp.where(z > o >> 1, z - (o >> 1), (o >> 1) - z) for o in owner],
        side=[place >> k & 1 for k in range(bits)],
        not_side=[1 - (place >> k & 1) for k in range(bits)],
        left_word=(x == 0).astype(jnp.int32).reshape(1),
        side_word=(place >> 1 & 1).astype(jnp.int32).reshape(1),
    )
    tall_tile, wide_tile = integrals.shape[0] // tile_live.shape[0], width // tile_live.shape[1]
    flags = jnp.repeat(tile_live.astype(jnp.bfloat16), wide_tile, 1)[:, None, :]
    live = (integrals.reshape(-1, tall_tile, width) * flags).reshape(integrals.shape)
    mine = pick(stored, x, 1)
    came[0], live, mine, scalars = lax.optimization_barrier((came[0], live, mine, scalars))
    left, own, from_even, distance = scalars["left"], scalars["own"], scalars["from_even"], scalars["far"]
    side, not_side = scalars["side"], scalars["not_side"]

    source = [[jnp.where(m, cut(mine, c), came[c]) for m in scalars["mine"]] for c in range(chunks)]
    held, near, far = [], [], []
    keeps, sent, coded = {}, {}, {}

    def sum_part(p, n, f):
        tall = jnp.stack([jnp.concatenate(n, axis=2), jnp.concatenate(f, axis=2)])
        count = tall.shape[3]
        tall = tall.reshape(2 * batches, groups // 2, 2, count, depth)
        away = pick(tall, not_side[0], 2).reshape(-1, depth)
        stay = pick(tall, side[0], 2).reshape(-1, depth)
        there = lax.ppermute(times(away, live, aligned), "inpair", [(g, g ^ 1) for g in range(groups)])
        here = times(stay, live, aligned)
        across = lambda k: [(g, g ^ (1 << k)) for g in range(groups)]
        if aligned:
            shape = (2 * batches, 2, count, width)
            keep, sent[p] = settle(scalars["side_word"], here.reshape(shape), there.reshape(shape))
            coded[p] = lax.ppermute(sent[p], "inpair", across(1))
        else:
            total = (here + there).reshape(2 * batches, groups // 2, count, width)
            for k in range(1, bits):
                split = total.reshape(2 * batches, total.shape[1] // 2, 2, count, width)
                keep, give = pick(split, side[k], 2), pick(split, not_side[k], 2)
                sent[p] = shrink(give.reshape(-1, width))
                coded[p] = lax.ppermute(sent[p], "inpair", across(k))
                if k + 1 < bits:
                    total = keep + grow(coded[p]).reshape(keep.shape)
        keeps[p] = keep.reshape(2, batches * count, width)
        return sent[p]

    moved = None
    for step in range(chunks + nz - 1):
        now = source[min(step, chunks - 1)]
        if step:
            others = list(far[-1:])
            if parts > 1 and step == chunks + nz - 2:
                others.append(sum_part(0, near[: chunks // 2], far[: chunks // 2]))
            by_odd, by_even = tied(moved, *others)
            now = [
                jnp.where(own[b], now[b], jnp.where(from_even[b], by_even[b], by_odd[b])) for b in range(batches)
            ]
        held.append(jnp.stack(now))
        if step >= nz - 1:
            window = held[step - nz + 1 : step + 1]
            got = [pick(jnp.stack([h[b] for h in window]), distance[b], 0) for b in range(batches)]
            near.append(jnp.stack(got))
        if step >= nz - 1:
            far.append(swap_x(near[-1]))
        if step < chunks + nz - 2:
            moved = shift(tied(held[-1], *near[-1:]))

    word = scalars["left_word"]
    merged = {}
    if parts > 1:
        merged[0] = merge(left, word, keeps[0], coded[0], parties, aligned)
        n, f = tied((near[chunks // 2 :], far[chunks // 2 :]), merged[0])
    else:
        n, f = near, far
    sum_part(parts - 1, n, f)
    merged[parts - 1] = merge(left, word, keeps[parts - 1], coded[parts - 1], parties, aligned)
    order = range(parts)

    out, parted = None, []
    for p in order:
        total, blocks = merged[p]
        blocks = lax.all_to_all(blocks, "outpair", split_axis=0, concat_axis=0, tiled=True)
        if aligned:
            out = finish(total, blocks, swap_within, vir_energy, occ_energy, out, p, parts)
            continue
        facing = jnp.concatenate([jnp.take(grow(blocks[o]), swap_within, axis=1) for o in range(parties)], axis=1)
        parted.append((total + facing).reshape(2, batches, -1, width))
    if aligned:
        return out.reshape(batches, share, width)
    whole = jnp.transpose(jnp.concatenate(parted, axis=2), (1, 0, 2, 3)).reshape(batches, share, width)
    return whole / (vir_energy[None, None, :] - occ_energy[:, :, None])


def solution(mesh):
    return jax.shard_map(
        on_device,
        mesh=mesh,
        in_specs=(
            P("inpair", "outpair"),
            P("outpair", None, "inpair"),
            P("inpair", "outpair"),
            P(),
            P(None, "inpair"),
            P("outpair"),
            P(),
        ),
        out_specs=P(None, "inpair", "outpair"),
        check_vma=False,
    )
```

time: 124 us -> 115 us (0.927)
  waiting for transfers between devices: 41.9 us -> 50.3 us
  other arithmetic: 10.1 us -> 2 us
  matrix products: 7.23 us -> 0 us
  between operations: 5.83 us -> 1.73 us
  Pallas kernels: 5.89 us -> 7.52 us
    ppermute x4, waiting for transfers between devices: 0.8 us -> 13.6 us  [the longest x2 9.72 us: sum_part(): coded[p] = lax.ppermute(sent[p], 'inpair', across(1))]
    dot_general x4 -> x0, matrix products: 7.23 us -> none  [on_device(): dot = lambda a, w: jnp.dot(a, w, preferred_element_type=jnp.float32)]
    all_to_all x2, starting transfers between devices: 11.2 us -> 7.04 us  [on_device(): lax.all_to_all(blocks, 'outpair', split_axis=0, concat_axis=0, tiled=True)]
    another operation x13, other arithmetic: 4.14 us -> 0.45 us  [on_device(): held.append(jnp.stack(now))]
    ppermute x8, starting transfers between devices: 9.04 us -> 12.4 us  [swap_x(): return lax.ppermute(values, 'outpair', beside)]
    ppermute x6, starting transfers between devices: 20.7 us -> 23.8 us  [shift(): lax.ppermute(values, 'outpair', even)]
    ppermute x6, waiting for transfers between devices: 18.5 us -> 16.2 us  [shift(): lax.ppermute(values, 'outpair', even)]
    pallas_call x2 -> x8, Pallas kernels: 3.46 us -> 5.66 us  [the longest x4 2.88 us: times(): pl.pallas_call(times_kernel, out_shape=jax.ShapeDtypeStruct((a.shape[0],...]
  transfers between devices with their start and end apart: 26 -> 26, of which waited for: 13 -> 17; matrix products, arithmetic and copies ran while one was open for 13% -> 1% of each run, Pallas kernels for 1% -> 5%
where the time goes in v2:
time: 115 us; the launch traced here: 114 us
  starting transfers between devices  50.6 us (44%)
  waiting for transfers between devices  50.3 us (44%)
  Pallas kernels  7.52 us (7%)
  local copies, waits for them, and re-layouts  2.37 us (2%)
  other arithmetic  2 us (2%)
  between operations  1.73 us (2%)
    ppermute x6, starting transfers between devices, shift(): lax.ppermute(values, 'outpair', even)  23.8 us
    ppermute x6, waiting for transfers between devices, shift(): lax.ppermute(values, 'outpair', even)  16.2 us
    all_to_all x2, waiting for transfers between devices, on_device(): lax.all_to_all(blocks, 'outpair', split_axis=0, concat_axis=0, tiled=True)  12.8 us
    ppermute x8, starting transfers between devices, swap_x(): return lax.ppermute(values, 'outpair', beside)  12.4 us
    ppermute x2, waiting for transfers between devices, sum_part(): coded[p] = lax.ppermute(sent[p], 'inpair', across(1))  9.72 us
    ppermute x8, waiting for transfers between devices, swap_x(): return lax.ppermute(values, 'outpair', beside)  7.65 us
    all_to_all x2, starting transfers between devices, on_device(): lax.all_to_all(blocks, 'outpair', split_axis=0, concat_axis=0, tiled=True)  7.04 us
    ppermute x6, starting transfers between devices, shift(): lax.ppermute(values, 'outpair', odd)  4.05 us
  transfers between devices with their start and end apart: 26, of which 17 were waited for; matrix products, arithmetic and copies ran while one was open for 1% of the time, Pallas kernels for 5%

profile of v2, /device:TPU:0, one launch (start us, length us, event | category | flops | bytes accessed | tf_op | source)
XLA Modules:
  0.0 114.4 jit_solution(2520361135002440690)
XLA Ops:
  0.0 1.5 %dynamic-slice_bitcast_fusion = (bf16[4,64,1024]{2,1,0:T(8,128)(2,1)S(1)}, bf16[4,64,1024]{2,1,0:T(8,128)(2,1)S(1)}) fusion(bf16[4,2,64,1024]{3,2,1,0:T(8,128)(2,1)} %bitcast.135, u32[]{:T(128)S(6)} %and.30, u32[]{:T(128)S(6)} %sub.19), kind=kLoop, calls=%fused_computation.39 | loop fusion | bytes 2097160 | tf_op jit(solution)/shard_map/jit(dynamic_index_in_dim)/squeeze | solution.py:20
  1.5 3.0 %collective-permute-start = (bf16[4,16,1024]{2,1,0:T(8,128)(2,1)S(1)}, bf16[4,16,1024]{2,1,0:T(8,128)(2,1)S(1)}, u32[]{:S(2)}, u32[]{:S(2)}) collective-permute-start(bf16[4,16,1024]{2,1,0:T(8,128)(2,1)S(1)} %get-tuple-element.116), channel_id=1, source_target_pairs={{0,1},{1,0},{2,3},{3,2},{4,5},{5,4},{6,7},{7,6},{8,9},{9,8},{10,11... | collective-permute-start | bytes 393224 | tf_op jit(solution)/shard_map/ppermute | solution.py:211
  4.5 0.6 fusion.37
  6.5 0.1 bitcast_multiply_fusion.w_ref
  6.7 1.3 %collective-permute-done = bf16[4,16,1024]{2,1,0:T(8,128)(2,1)S(1)} collective-permute-done((bf16[4,16,1024]{2,1,0:T(8,128)(2,1)S(1)}, bf16[4,16,1024]{2,1,0:T(8,128)(2,1)S(1)}, u32[]{:S(2)}, u32[]{:S(2)}) %collective-permute-start) | collective-permute-done | bytes 131104 | tf_op jit(solution)/shard_map/ppermute | solution.py:211
  8.1 0.7 collective-permute-start.3
  8.8 4.7 %collective-permute-start.4 = (bf16[2,4,16,1024]{3,2,1,0:T(8,128)(2,1)S(1)}, bf16[2,4,16,1024]{3,2,1,0:T(8,128)(2,1)S(1)}, u32[]{:S(2)}, u32[]{:S(2)}) collective-permute-start(bf16[2,4,16,1024]{3,2,1,0:T(8,128)(2,1)S(1)} %pad_maximum_fusion.2), channel_id=1, source_target_pairs={{0,2},{1,3},{2,0},{3,1},{4,6},{5,7},{6,4},{7,5},{8,10},{9,11},{10,... | collective-permute-start | bytes 786440 | tf_op jit(solution)/shard_map/ppermute | solution.py:214
  13.5 1.5 %collective-permute-start.2 = (bf16[4,16,1024]{2,1,0:T(8,128)(2,1)S(1)}, bf16[4,16,1024]{2,1,0:T(8,128)(2,1)S(1)}, u32[]{:S(2)}, u32[]{:S(2)}) collective-permute-start(bf16[4,16,1024]{2,1,0:T(8,128)(2,1)S(1)} %get-tuple-element.114), channel_id=1, source_target_pairs={{0,1},{1,0},{2,3},{3,2},{4,5},{5,4},{6,7},{7,6},{8,9},{9,8},{10,11... | collective-permute-start | bytes 393224 | tf_op jit(solution)/shard_map/ppermute | solution.py:211
  15.0 3.7 %collective-permute-done.4 = bf16[2,4,16,1024]{3,2,1,0:T(8,128)(2,1)S(1)} collective-permute-done((bf16[2,4,16,1024]{3,2,1,0:T(8,128)(2,1)S(1)}, bf16[2,4,16,1024]{3,2,1,0:T(8,128)(2,1)S(1)}, u32[]{:S(2)}, u32[]{:S(2)}) %collective-permute-start.4) | collective-permute-done | bytes 262176 | tf_op jit(solution)/shard_map/ppermute | solution.py:214
  18.7 0.7 collective-permute-start.5
  19.4 3.5 %collective-permute-start.6 = (bf16[2,4,16,1024]{3,2,1,0:T(8,128)(2,1)S(1)}, bf16[2,4,16,1024]{3,2,1,0:T(8,128)(2,1)S(1)}, u32[]{:S(2)}, u32[]{:S(2)}) collective-permute-start(bf16[2,4,16,1024]{3,2,1,0:T(8,128)(2,1)S(1)} %pad_maximum_fusion.3), channel_id=1, source_target_pairs={{0,2},{1,3},{2,0},{3,1},{4,6},{5,7},{6,4},{7,5},{8,10},{9,11},{10,... | collective-permute-start | bytes 786440 | tf_op jit(solution)/shard_map/ppermute | solution.py:214
  22.9 1.5 %collective-permute-start.1 = (bf16[4,16,1024]{2,1,0:T(8,128)(2,1)S(1)}, bf16[4,16,1024]{2,1,0:T(8,128)(2,1)S(1)}, u32[]{:S(2)}, u32[]{:S(2)}) collective-permute-start(bf16[4,16,1024]{2,1,0:T(8,128)(2,1)S(1)} %get-tuple-element.115), channel_id=1, source_target_pairs={{0,1},{1,0},{2,3},{3,2},{4,5},{5,4},{6,7},{7,6},{8,9},{9,8},{10,11... | collective-permute-start | bytes 393224 | tf_op jit(solution)/shard_map/ppermute | solution.py:211
  24.4 2.9 %collective-permute-done.6 = bf16[2,4,16,1024]{3,2,1,0:T(8,128)(2,1)S(1)} collective-permute-done((bf16[2,4,16,1024]{3,2,1,0:T(8,128)(2,1)S(1)}, bf16[2,4,16,1024]{3,2,1,0:T(8,128)(2,1)S(1)}, u32[]{:S(2)}, u32[]{:S(2)}) %collective-permute-start.6) | collective-permute-done | bytes 262176 | tf_op jit(solution)/shard_map/ppermute | solution.py:214
  27.3 0.6 collective-permute-done.1
  28.0 0.7 collective-permute-start.8
  28.6 4.3 %collective-permute-start.9 = (bf16[2,4,16,1024]{3,2,1,0:T(8,128)(2,1)S(1)}, bf16[2,4,16,1024]{3,2,1,0:T(8,128)(2,1)S(1)}, u32[]{:S(2)}, u32[]{:S(2)}) collective-permute-start(bf16[2,4,16,1024]{3,2,1,0:T(8,128)(2,1)S(1)} %pad_maximum_fusion.4), channel_id=1, source_target_pairs={{0,2},{1,3},{2,0},{3,1},{4,6},{5,7},{6,4},{7,5},{8,10},{9,11},{10,... | collective-permute-start | bytes 786440 | tf_op jit(solution)/shard_map/ppermute | solution.py:214
  32.9 1.5 %collective-permute-start.7 = (bf16[4,16,1024]{2,1,0:T(8,128)(2,1)S(1)}, bf16[4,16,1024]{2,1,0:T(8,128)(2,1)S(1)}, u32[]{:S(2)}, u32[]{:S(2)}) collective-permute-start(bf16[4,16,1024]{2,1,0:T(8,128)(2,1)S(1)} %get-tuple-element.113), channel_id=1, source_target_pairs={{0,1},{1,0},{2,3},{3,2},{4,5},{5,4},{6,7},{7,6},{8,9},{9,8},{10,11... | collective-permute-start | bytes 393224 | tf_op jit(solution)/shard_map/ppermute | solution.py:211
  34.4 2.9 %collective-permute-done.9 = bf16[2,4,16,1024]{3,2,1,0:T(8,128)(2,1)S(1)} collective-permute-done((bf16[2,4,16,1024]{3,2,1,0:T(8,128)(2,1)S(1)}, bf16[2,4,16,1024]{3,2,1,0:T(8,128)(2,1)S(1)}, u32[]{:S(2)}, u32[]{:S(2)}) %collective-permute-start.9) | collective-permute-done | bytes 262176 | tf_op jit(solution)/shard_map/ppermute | solution.py:214
  37.3 0.6 collective-permute-done.7
  37.9 0.1 fusion.23
  38.1 0.1 fusion.20
  38.3 0.7 collective-permute-start.10
  39.0 3.2 %collective-permute-start.11 = (bf16[2,4,16,1024]{3,2,1,0:T(8,128)(2,1)S(1)}, bf16[2,4,16,1024]{3,2,1,0:T(8,128)(2,1)S(1)}, u32[]{:S(2)}, u32[]{:S(2)}) collective-permute-start(bf16[2,4,16,1024]{3,2,1,0:T(8,128)(2,1)S(1)} %pad_maximum_fusion.5), channel_id=1, source_target_pairs={{0,2},{1,3},{2,0},{3,1},{4,6},{5,7},{6,4},{7,5},{8,10},{9,11},{10,... | collective-permute-start | bytes 786440 | tf_op jit(solution)/shard_map/ppermute | solution.py:214
  42.1 1.5 %collective-permute-start.12 = (bf16[2,4,16,1024]{3,2,1,0:T(8,128)(2,1)S(1)}, bf16[2,4,16,1024]{3,2,1,0:T(8,128)(2,1)S(1)}, u32[]{:S(2)}, u32[]{:S(2)}) collective-permute-start(bf16[2,4,16,1024]{3,2,1,0:T(8,128)(2,1)S(1)} %pad_maximum_fusion.6), channel_id=1, source_target_pairs={{0,1},{1,0},{2,3},{3,2},{4,5},{5,4},{6,7},{7,6},{8,9},{9,8},{10,11... | collective-permute-start | bytes 786440 | tf_op jit(solution)/shard_map/ppermute | solution.py:211
  43.6 2.9 %collective-permute-done.11 = bf16[2,4,16,1024]{3,2,1,0:T(8,128)(2,1)S(1)} collective-permute-done((bf16[2,4,16,1024]{3,2,1,0:T(8,128)(2,1)S(1)}, bf16[2,4,16,1024]{3,2,1,0:T(8,128)(2,1)S(1)}, u32[]{:S(2)}, u32[]{:S(2)}) %collective-permute-start.11) | collective-permute-done | bytes 262176 | tf_op jit(solution)/shard_map/ppermute | solution.py:214
  46.5 4.0 %collective-permute-done.12 = bf16[2,4,16,1024]{3,2,1,0:T(8,128)(2,1)S(1)} collective-permute-done((bf16[2,4,16,1024]{3,2,1,0:T(8,128)(2,1)S(1)}, bf16[2,4,16,1024]{3,2,1,0:T(8,128)(2,1)S(1)}, u32[]{:S(2)}, u32[]{:S(2)}) %collective-permute-start.12) | collective-permute-done | bytes 262176 | tf_op jit(solution)/shard_map/ppermute | solution.py:211
  50.5 0.1 fusion.17
  50.6 0.1 fusion.14
  50.8 1.6 %collective-permute-start.15 = (bf16[2,4,16,1024]{3,2,1,0:T(8,128)(2,1)S(1)}, bf16[2,4,16,1024]{3,2,1,0:T(8,128)(2,1)S(1)}, u32[]{:S(2)}, u32[]{:S(2)}) collective-permute-start(bf16[2,4,16,1024]{3,2,1,0:T(8,128)(2,1)S(1)} %pad_maximum_fusion.8), channel_id=1, source_target_pairs={{0,1},{1,0},{2,3},{3,2},{4,5},{5,4},{6,7},{7,6},{8,9},{9,8},{10,11... | collective-permute-start | bytes 786440 | tf_op jit(solution)/shard_map/ppermute | solution.py:211
  52.4 0.7 collective-permute-start.13
  53.0 3.4 %collective-permute-start.14 = (bf16[2,4,16,1024]{3,2,1,0:T(8,128)(2,1)S(1)}, bf16[2,4,16,1024]{3,2,1,0:T(8,128)(2,1)S(1)}, u32[]{:S(2)}, u32[]{:S(2)}) collective-permute-start(bf16[2,4,16,1024]{3,2,1,0:T(8,128)(2,1)S(1)} %pad_maximum_fusion.7), channel_id=1, source_target_pairs={{0,2},{1,3},{2,0},{3,1},{4,6},{5,7},{6,4},{7,5},{8,10},{9,11},{10,... | collective-permute-start | bytes 786440 | tf_op jit(solution)/shard_map/ppermute | solution.py:214
  56.5 0.8 collective-permute-done.15
  57.3 4.0 %collective-permute-done.14 = bf16[2,4,16,1024]{3,2,1,0:T(8,128)(2,1)S(1)} collective-permute-done((bf16[2,4,16,1024]{3,2,1,0:T(8,128)(2,1)S(1)}, bf16[2,4,16,1024]{3,2,1,0:T(8,128)(2,1)S(1)}, u32[]{:S(2)}, u32[]{:S(2)}) %collective-permute-start.14) | collective-permute-done | bytes 262176 | tf_op jit(solution)/shard_map/ppermute | solution.py:214
  61.3 0.1 fusion.11
  61.5 0.1 fusion.8
  61.7 0.7 collective-permute-start.16
  62.3 4.8 %collective-permute-start.17 = (bf16[2,4,16,1024]{3,2,1,0:T(8,128)(2,1)S(1)}, bf16[2,4,16,1024]{3,2,1,0:T(8,128)(2,1)S(1)}, u32[]{:S(2)}, u32[]{:S(2)}) collective-permute-start(bf16[2,4,16,1024]{3,2,1,0:T(8,128)(2,1)S(1)} %pad_maximum_fusion.10), channel_id=1, source_target_pairs={{0,2},{1,3},{2,0},{3,1},{4,6},{5,7},{6,4},{7,5},{8,10},{9,11},{10,... | collective-permute-start | bytes 786440 | tf_op jit(solution)/shard_map/ppermute | solution.py:214
  67.1 0.5 collective-permute-start.18
  67.7 0.1 pad_maximum_fusion
  67.8 0.1 constant_dynamic-slice_fusion.2
  67.9 0.7 times.5
  68.7 0.7 times.4
  69.4 1.9 %collective-permute-done.19 = f32[256,1024]{1,0:T(8,128)S(1)} collective-permute-done((f32[256,1024]{1,0:T(8,128)S(1)}, f32[256,1024]{1,0:T(8,128)S(1)}, u32[]{:S(2)}, u32[]{:S(2)}) %collective-permute-start.19) | collective-permute-done | bytes 1048608 | tf_op jit(solution)/shard_map/ppermute | solution.py:256
  71.3 0.3 settle.2
  71.6 1.6 %collective-permute-start.21 = (s16[144,1024]{1,0:T(8,128)(2,1)S(1)}, s16[144,1024]{1,0:T(8,128)(2,1)S(1)}, u32[]{:S(2)}, u32[]{:S(2)}) collective-permute-start(s16[144,1024]{1,0:T(8,128)(2,1)S(1)} %get-tuple-element.75), channel_id=1, source_target_pairs={{0,16},{8,24},{16,0},{24,8},{1,17},{9,25},{17,1},{25,9},{2,18},{10... | collective-permute-start | bytes 884744 | tf_op jit(solution)/shard_map/ppermute | solution.py:262
  73.2 0.3 collective-permute-done.18
  73.5 0.2 fusion.2
  73.8 1.3 %collective-permute-start.20 = (bf16[2,4,16,1024]{3,2,1,0:T(8,128)(2,1)S(1)}, bf16[2,4,16,1024]{3,2,1,0:T(8,128)(2,1)S(1)}, u32[]{:S(2)}, u32[]{:S(2)}) collective-permute-start(bf16[2,4,16,1024]{3,2,1,0:T(8,128)(2,1)S(1)} %pad_maximum_fusion.11), channel_id=1, source_target_pairs={{0,1},{1,0},{2,3},{3,2},{4,5},{5,4},{6,7},{7,6},{8,9},{9,8},{10,11... | collective-permute-start | bytes 786440 | tf_op jit(solution)/shard_map/ppermute | solution.py:211
  75.1 5.6 %collective-permute-done.21.coded_ref = s16[144,1024]{1,0:T(8,128)(2,1)S(1)} collective-permute-done((s16[144,1024]{1,0:T(8,128)(2,1)S(1)}, s16[144,1024]{1,0:T(8,128)(2,1)S(1)}, u32[]{:S(2)}, u32[]{:S(2)}) %collective-permute-start.21) | collective-permute-done | bytes 294944 | tf_op jit(solution)/shard_map/ppermute | solution.py:262
  80.7 0.9 merge.2
  81.8 0.1 pad_maximum_fusion.1
  82.0 0.7 times.7
  82.8 0.7 times.6
  83.5 1.9 %collective-permute-done.22 = f32[256,1024]{1,0:T(8,128)S(1)} collective-permute-done((f32[256,1024]{1,0:T(8,128)S(1)}, f32[256,1024]{1,0:T(8,128)S(1)}, u32[]{:S(2)}, u32[]{:S(2)}) %collective-permute-start.22) | collective-permute-done | bytes 1048608 | tf_op jit(solution)/shard_map/ppermute | solution.py:256
  85.4 0.2 settle.3
  85.6 1.6 %collective-permute-start.23 = (s16[144,1024]{1,0:T(8,128)(2,1)S(1)}, s16[144,1024]{1,0:T(8,128)(2,1)S(1)}, u32[]{:S(2)}, u32[]{:S(2)}) collective-permute-start(s16[144,1024]{1,0:T(8,128)(2,1)S(1)} %get-tuple-element.86), channel_id=1, source_target_pairs={{0,16},{8,24},{16,0},{24,8},{1,17},{9,25},{17,1},{25,9},{2,18},{10... | collective-permute-start | bytes 884744 | tf_op jit(solution)/shard_map/ppermute | solution.py:262
  87.2 3.4 %all-to-all-start.1 = ((s16[8,144,128]{2,1,0:T(8,128)(2,1)}), s16[8,144,128]{2,1,0:T(8,128)(2,1)S(1)}, u32[]{:S(2)}, u32[]{:S(2)}) async-start(s16[8,144,128]{2,1,0:T(8,128)(2,1)} %get-tuple-element.80), calls=%async_computation.1 | async-start | bytes 589824 | tf_op jit(solution)/shard_map/all_to_all | solution.py:310
  90.7 4.1 %collective-permute-done.23.coded_ref = s16[144,1024]{1,0:T(8,128)(2,1)S(1)} collective-permute-done((s16[144,1024]{1,0:T(8,128)(2,1)S(1)}, s16[144,1024]{1,0:T(8,128)(2,1)S(1)}, u32[]{:S(2)}, u32[]{:S(2)}) %collective-permute-start.23) | collective-permute-done | bytes 294944 | tf_op jit(solution)/shard_map/ppermute | solution.py:262
  94.8 0.9 merge.3
  95.7 4.8 %all-to-all-done.1.refs_1_ = s16[8,144,128]{2,1,0:T(8,128)(2,1)S(1)} async-done(((s16[8,144,128]{2,1,0:T(8,128)(2,1)}), s16[8,144,128]{2,1,0:T(8,128)(2,1)S(1)}, u32[]{:S(2)}, u32[]{:S(2)}) %all-to-all-start.1) | async-done | bytes 294944 | tf_op jit(solution)/shard_map/all_to_all | solution.py:310
  100.5 3.6 %all-to-all-start = ((s16[8,144,128]{2,1,0:T(8,128)(2,1)}), s16[8,144,128]{2,1,0:T(8,128)(2,1)S(1)}, u32[]{:S(2)}, u32[]{:S(2)}) async-start(s16[8,144,128]{2,1,0:T(8,128)(2,1)} %get-tuple-element.88), calls=%async_computation | async-start | bytes 589824 | tf_op jit(solution)/shard_map/all_to_all | solution.py:310
  104.1 1.2 %finish.2.refs_5_ = f32[2,2,2,32,1024]{4,3,2,1,0:T(8,128)} custom-call(f32[128,1024]{1,0:T(8,128)S(1)} %get-tuple-element.79.refs_0_, s16[8,144,128]{2,1,0:T(8,128)(2,1)S(1)} %all-to-all-done.1.refs_1_, s32[1,128]{1,0:T(1,128)S(1)} %bitcast.131, f32[1,1024]{1,0:T(1,128)S(1)} %bitcast.129, f32[2,128]{1,0:T(2,128)S(1)} %copy-done.1), custom_call_target="tpu_custom_call" | custom-call | flops 20000000000 | tf_op jit(solution)/shard_map/finish/pallas_call | solution.py:180
  105.3 8.0 %all-to-all-done.refs_1_ = s16[8,144,128]{2,1,0:T(8,128)(2,1)S(1)} async-done(((s16[8,144,128]{2,1,0:T(8,128)(2,1)}), s16[8,144,128]{2,1,0:T(8,128)(2,1)S(1)}, u32[]{:S(2)}, u32[]{:S(2)}) %all-to-all-start) | async-done | bytes 294944 | tf_op jit(solution)/shard_map/all_to_all | solution.py:310
  113.3 1.1 %finish.3 = f32[2,2,2,32,1024]{4,3,2,1,0:T(8,128)} custom-call(f32[128,1024]{1,0:T(8,128)S(1)} %get-tuple-element.87.refs_0_, s16[8,144,128]{2,1,0:T(8,128)(2,1)S(1)} %all-to-all-done.refs_1_, s32[1,128]{1,0:T(1,128)S(1)} %bitcast.132, f32[1,1024]{1,0:T(1,128)S(1)} %bitcast.130, f32[2,128]{1,0:T(2,128)S(1)} %copy-done.1, ...), custom_call_target="tpu_custom_call", output_to_operand_aliasing={{}: (5, {})} | custom-call | flops 20000000000 | tf_op jit(solution)/shard_map/finish/pallas_call | solution.py:180
  (49 shorter events, 1.1 us)
Async XLA Ops:
  0.0 4.5 %copy-start.5 = (s32[2]{0:T(128)S(1)}, s32[2]{0:T(128)}, u32[]{:S(2)}) copy-start(s32[2]{0:T(128)} %param.10) | copy-start | bytes 28
  0.0 6.4 %copy-start.4 = (s32[4,4]{1,0:T(4,128)S(1)}, s32[4,4]{1,0:T(4,128)}, u32[]{:S(2)}) copy-start(s32[4,4]{1,0:T(4,128)} %param.9) | copy-start | bytes 196
  0.0 6.5 %copy-start.3 = (bf16[1024,1024]{1,0:T(8,128)(2,1)S(1)}, bf16[1024,1024]{1,0:T(8,128)(2,1)}, u32[]{:S(2)}) copy-start(bf16[1024,1024]{1,0:T(8,128)(2,1)} %param.7) | copy-start | bytes 6291460
  1.5 6.5 %collective-permute-start = (bf16[4,16,1024]{2,1,0:T(8,128)(2,1)S(1)}, bf16[4,16,1024]{2,1,0:T(8,128)(2,1)S(1)}, u32[]{:S(2)}, u32[]{:S(2)}) collective-permute-start(bf16[4,16,1024]{2,1,0:T(8,128)(2,1)S(1)} %get-tuple-element.116), channel_id=1, source_target_pairs={{0,1},{1,0},{2,3},{3,2},{4,5},{5,4},{6,7},{7,6},{8,9},{9,8},{10,11... | collective-permute-start | bytes 393224 | tf_op jit(solution)/shard_map/ppermute | solution.py:211
  8.1 6.9 %collective-permute-start.3 = (bf16[2,4,16,1024]{3,2,1,0:T(8,128)(2,1)S(1)}, bf16[2,4,16,1024]{3,2,1,0:T(8,128)(2,1)S(1)}, u32[]{:S(2)}, u32[]{:S(2)}) collective-permute-start(bf16[2,4,16,1024]{3,2,1,0:T(8,128)(2,1)S(1)} %pad_maximum_fusion.2), channel_id=1, source_target_pairs={{2,4},{3,5},{4,2},{5,3},{10,12},{11,13},{12,10},{13,11},{18,20},{1... | collective-permute-start | bytes 786440 | tf_op jit(solution)/shard_map/ppermute | solution.py:214
  8.8 9.9 %collective-permute-start.4 = (bf16[2,4,16,1024]{3,2,1,0:T(8,128)(2,1)S(1)}, bf16[2,4,16,1024]{3,2,1,0:T(8,128)(2,1)S(1)}, u32[]{:S(2)}, u32[]{:S(2)}) collective-permute-start(bf16[2,4,16,1024]{3,2,1,0:T(8,128)(2,1)S(1)} %pad_maximum_fusion.2), channel_id=1, source_target_pairs={{0,2},{1,3},{2,0},{3,1},{4,6},{5,7},{6,4},{7,5},{8,10},{9,11},{10,... | collective-permute-start | bytes 786440 | tf_op jit(solution)/shard_map/ppermute | solution.py:214
  13.5 5.2 %collective-permute-start.2 = (bf16[4,16,1024]{2,1,0:T(8,128)(2,1)S(1)}, bf16[4,16,1024]{2,1,0:T(8,128)(2,1)S(1)}, u32[]{:S(2)}, u32[]{:S(2)}) collective-permute-start(bf16[4,16,1024]{2,1,0:T(8,128)(2,1)S(1)} %get-tuple-element.114), channel_id=1, source_target_pairs={{0,1},{1,0},{2,3},{3,2},{4,5},{5,4},{6,7},{7,6},{8,9},{9,8},{10,11... | collective-permute-start | bytes 393224 | tf_op jit(solution)/shard_map/ppermute | solution.py:211
  18.7 5.7 %collective-permute-start.5 = (bf16[2,4,16,1024]{3,2,1,0:T(8,128)(2,1)S(1)}, bf16[2,4,16,1024]{3,2,1,0:T(8,128)(2,1)S(1)}, u32[]{:S(2)}, u32[]{:S(2)}) collective-permute-start(bf16[2,4,16,1024]{3,2,1,0:T(8,128)(2,1)S(1)} %pad_maximum_fusion.3), channel_id=1, source_target_pairs={{2,4},{3,5},{4,2},{5,3},{10,12},{11,13},{12,10},{13,11},{18,20},{1... | collective-permute-start | bytes 786440 | tf_op jit(solution)/shard_map/ppermute | solution.py:214
  19.4 7.8 %collective-permute-start.6 = (bf16[2,4,16,1024]{3,2,1,0:T(8,128)(2,1)S(1)}, bf16[2,4,16,1024]{3,2,1,0:T(8,128)(2,1)S(1)}, u32[]{:S(2)}, u32[]{:S(2)}) collective-permute-start(bf16[2,4,16,1024]{3,2,1,0:T(8,128)(2,1)S(1)} %pad_maximum_fusion.3), channel_id=1, source_target_pairs={{0,2},{1,3},{2,0},{3,1},{4,6},{5,7},{6,4},{7,5},{8,10},{9,11},{10,... | collective-permute-start | bytes 786440 | tf_op jit(solution)/shard_map/ppermute | solution.py:214
  22.9 5.0 %collective-permute-start.1 = (bf16[4,16,1024]{2,1,0:T(8,128)(2,1)S(1)}, bf16[4,16,1024]{2,1,0:T(8,128)(2,1)S(1)}, u32[]{:S(2)}, u32[]{:S(2)}) collective-permute-start(bf16[4,16,1024]{2,1,0:T(8,128)(2,1)S(1)} %get-tuple-element.115), channel_id=1, source_target_pairs={{0,1},{1,0},{2,3},{3,2},{4,5},{5,4},{6,7},{7,6},{8,9},{9,8},{10,11... | collective-permute-start | bytes 393224 | tf_op jit(solution)/shard_map/ppermute | solution.py:211
  28.0 6.5 %collective-permute-start.8 = (bf16[2,4,16,1024]{3,2,1,0:T(8,128)(2,1)S(1)}, bf16[2,4,16,1024]{3,2,1,0:T(8,128)(2,1)S(1)}, u32[]{:S(2)}, u32[]{:S(2)}) collective-permute-start(bf16[2,4,16,1024]{3,2,1,0:T(8,128)(2,1)S(1)} %pad_maximum_fusion.4), channel_id=1, source_target_pairs={{2,4},{3,5},{4,2},{5,3},{10,12},{11,13},{12,10},{13,11},{18,20},{1... | collective-permute-start | bytes 786440 | tf_op jit(solution)/shard_map/ppermute | solution.py:214
  28.6 8.6 %collective-permute-start.9 = (bf16[2,4,16,1024]{3,2,1,0:T(8,128)(2,1)S(1)}, bf16[2,4,16,1024]{3,2,1,0:T(8,128)(2,1)S(1)}, u32[]{:S(2)}, u32[]{:S(2)}) collective-permute-start(bf16[2,4,16,1024]{3,2,1,0:T(8,128)(2,1)S(1)} %pad_maximum_fusion.4), channel_id=1, source_target_pairs={{0,2},{1,3},{2,0},{3,1},{4,6},{5,7},{6,4},{7,5},{8,10},{9,11},{10,... | collective-permute-start | bytes 786440 | tf_op jit(solution)/shard_map/ppermute | solution.py:214
  32.9 5.0 %collective-permute-start.7 = (bf16[4,16,1024]{2,1,0:T(8,128)(2,1)S(1)}, bf16[4,16,1024]{2,1,0:T(8,128)(2,1)S(1)}, u32[]{:S(2)}, u32[]{:S(2)}) collective-permute-start(bf16[4,16,1024]{2,1,0:T(8,128)(2,1)S(1)} %get-tuple-element.113), channel_id=1, source_target_pairs={{0,1},{1,0},{2,3},{3,2},{4,5},{5,4},{6,7},{7,6},{8,9},{9,8},{10,11... | collective-permute-start | bytes 393224 | tf_op jit(solution)/shard_map/ppermute | solution.py:211
  38.3 5.3 %collective-permute-start.10 = (bf16[2,4,16,1024]{3,2,1,0:T(8,128)(2,1)S(1)}, bf16[2,4,16,1024]{3,2,1,0:T(8,128)(2,1)S(1)}, u32[]{:S(2)}, u32[]{:S(2)}) collective-permute-start(bf16[2,4,16,1024]{3,2,1,0:T(8,128)(2,1)S(1)} %pad_maximum_fusion.5), channel_id=1, source_target_pairs={{2,4},{3,5},{4,2},{5,3},{10,12},{11,13},{12,10},{13,11},{18,20},{1... | collective-permute-start | bytes 786440 | tf_op jit(solution)/shard_map/ppermute | solution.py:214
  39.0 7.5 %collective-permute-start.11 = (bf16[2,4,16,1024]{3,2,1,0:T(8,128)(2,1)S(1)}, bf16[2,4,16,1024]{3,2,1,0:T(8,128)(2,1)S(1)}, u32[]{:S(2)}, u32[]{:S(2)}) collective-permute-start(bf16[2,4,16,1024]{3,2,1,0:T(8,128)(2,1)S(1)} %pad_maximum_fusion.5), channel_id=1, source_target_pairs={{0,2},{1,3},{2,0},{3,1},{4,6},{5,7},{6,4},{7,5},{8,10},{9,11},{10,... | collective-permute-start | bytes 786440 | tf_op jit(solution)/shard_map/ppermute | solution.py:214
  42.1 8.3 %collective-permute-start.12 = (bf16[2,4,16,1024]{3,2,1,0:T(8,128)(2,1)S(1)}, bf16[2,4,16,1024]{3,2,1,0:T(8,128)(2,1)S(1)}, u32[]{:S(2)}, u32[]{:S(2)}) collective-permute-start(bf16[2,4,16,1024]{3,2,1,0:T(8,128)(2,1)S(1)} %pad_maximum_fusion.6), channel_id=1, source_target_pairs={{0,1},{1,0},{2,3},{3,2},{4,5},{5,4},{6,7},{7,6},{8,9},{9,8},{10,11... | collective-permute-start | bytes 786440 | tf_op jit(solution)/shard_map/ppermute | solution.py:211
  50.8 6.5 %collective-permute-start.15 = (bf16[2,4,16,1024]{3,2,1,0:T(8,128)(2,1)S(1)}, bf16[2,4,16,1024]{3,2,1,0:T(8,128)(2,1)S(1)}, u32[]{:S(2)}, u32[]{:S(2)}) collective-permute-start(bf16[2,4,16,1024]{3,2,1,0:T(8,128)(2,1)S(1)} %pad_maximum_fusion.8), channel_id=1, source_target_pairs={{0,1},{1,0},{2,3},{3,2},{4,5},{5,4},{6,7},{7,6},{8,9},{9,8},{10,11... | collective-permute-start | bytes 786440 | tf_op jit(solution)/shard_map/ppermute | solution.py:211
  52.4 4.9 %collective-permute-start.13 = (bf16[2,4,16,1024]{3,2,1,0:T(8,128)(2,1)S(1)}, bf16[2,4,16,1024]{3,2,1,0:T(8,128)(2,1)S(1)}, u32[]{:S(2)}, u32[]{:S(2)}) collective-permute-start(bf16[2,4,16,1024]{3,2,1,0:T(8,128)(2,1)S(1)} %pad_maximum_fusion.7), channel_id=1, source_target_pairs={{2,4},{3,5},{4,2},{5,3},{10,12},{11,13},{12,10},{13,11},{18,20},{1... | collective-permute-start | bytes 786440 | tf_op jit(solution)/shard_map/ppermute | solution.py:214
  53.0 8.3 %collective-permute-start.14 = (bf16[2,4,16,1024]{3,2,1,0:T(8,128)(2,1)S(1)}, bf16[2,4,16,1024]{3,2,1,0:T(8,128)(2,1)S(1)}, u32[]{:S(2)}, u32[]{:S(2)}) collective-permute-start(bf16[2,4,16,1024]{3,2,1,0:T(8,128)(2,1)S(1)} %pad_maximum_fusion.7), channel_id=1, source_target_pairs={{0,2},{1,3},{2,0},{3,1},{4,6},{5,7},{6,4},{7,5},{8,10},{9,11},{10,... | collective-permute-start | bytes 786440 | tf_op jit(solution)/shard_map/ppermute | solution.py:214
  61.7 11.5 %collective-permute-start.16 = (bf16[2,4,16,1024]{3,2,1,0:T(8,128)(2,1)S(1)}, bf16[2,4,16,1024]{3,2,1,0:T(8,128)(2,1)S(1)}, u32[]{:S(2)}, u32[]{:S(2)}) collective-permute-start(bf16[2,4,16,1024]{3,2,1,0:T(8,128)(2,1)S(1)} %pad_maximum_fusion.10), channel_id=1, source_target_pairs={{2,4},{3,5},{4,2},{5,3},{10,12},{11,13},{12,10},{13,11},{18,20},{1... | collective-permute-start | bytes 786440 | tf_op jit(solution)/shard_map/ppermute | solution.py:214
  62.3 10.9 %collective-permute-start.17 = (bf16[2,4,16,1024]{3,2,1,0:T(8,128)(2,1)S(1)}, bf16[2,4,16,1024]{3,2,1,0:T(8,128)(2,1)S(1)}, u32[]{:S(2)}, u32[]{:S(2)}) collective-permute-start(bf16[2,4,16,1024]{3,2,1,0:T(8,128)(2,1)S(1)} %pad_maximum_fusion.10), channel_id=1, source_target_pairs={{0,2},{1,3},{2,0},{3,1},{4,6},{5,7},{6,4},{7,5},{8,10},{9,11},{10,... | collective-permute-start | bytes 786440 | tf_op jit(solution)/shard_map/ppermute | solution.py:214
  67.1 6.4 %collective-permute-start.18 = (bf16[2,4,16,1024]{3,2,1,0:T(8,128)(2,1)S(1)}, bf16[2,4,16,1024]{3,2,1,0:T(8,128)(2,1)S(1)}, u32[]{:S(2)}, u32[]{:S(2)}) collective-permute-start(bf16[2,4,16,1024]{3,2,1,0:T(8,128)(2,1)S(1)} %pad_maximum_fusion.9), channel_id=1, source_target_pairs={{0,1},{1,0},{2,3},{3,2},{4,5},{5,4},{6,7},{7,6},{8,9},{9,8},{10,11... | collective-permute-start | bytes 786440 | tf_op jit(solution)/shard_map/ppermute | solution.py:211
  68.6 2.7 %collective-permute-start.19 = (f32[256,1024]{1,0:T(8,128)S(1)}, f32[256,1024]{1,0:T(8,128)S(1)}, u32[]{:S(2)}, u32[]{:S(2)}) collective-permute-start(f32[256,1024]{1,0:T(8,128)S(1)} %times.5), channel_id=1, source_target_pairs={{0,8},{8,0},{16,24},{24,16},{1,9},{9,1},{17,25},{25,17},{2,10},{10... | collective-permute-start | bytes 3145736 | tf_op jit(solution)/shard_map/ppermute | solution.py:256
  71.6 9.1 %collective-permute-start.21 = (s16[144,1024]{1,0:T(8,128)(2,1)S(1)}, s16[144,1024]{1,0:T(8,128)(2,1)S(1)}, u32[]{:S(2)}, u32[]{:S(2)}) collective-permute-start(s16[144,1024]{1,0:T(8,128)(2,1)S(1)} %get-tuple-element.75), channel_id=1, source_target_pairs={{0,16},{8,24},{16,0},{24,8},{1,17},{9,25},{17,1},{25,9},{2,18},{10... | collective-permute-start | bytes 884744 | tf_op jit(solution)/shard_map/ppermute | solution.py:262
  73.8 7.9 %collective-permute-start.20 = (bf16[2,4,16,1024]{3,2,1,0:T(8,128)(2,1)S(1)}, bf16[2,4,16,1024]{3,2,1,0:T(8,128)(2,1)S(1)}, u32[]{:S(2)}, u32[]{:S(2)}) collective-permute-start(bf16[2,4,16,1024]{3,2,1,0:T(8,128)(2,1)S(1)} %pad_maximum_fusion.11), channel_id=1, source_target_pairs={{0,1},{1,0},{2,3},{3,2},{4,5},{5,4},{6,7},{7,6},{8,9},{9,8},{10,11... | collective-permute-start | bytes 786440 | tf_op jit(solution)/shard_map/ppermute | solution.py:211
  82.7 2.7 %collective-permute-start.22 = (f32[256,1024]{1,0:T(8,128)S(1)}, f32[256,1024]{1,0:T(8,128)S(1)}, u32[]{:S(2)}, u32[]{:S(2)}) collective-permute-start(f32[256,1024]{1,0:T(8,128)S(1)} %times.7), channel_id=1, source_target_pairs={{0,8},{8,0},{16,24},{24,16},{1,9},{9,1},{17,25},{25,17},{2,10},{10... | collective-permute-start | bytes 3145736 | tf_op jit(solution)/shard_map/ppermute | solution.py:256
  85.6 9.1 %collective-permute-start.23 = (s16[144,1024]{1,0:T(8,128)(2,1)S(1)}, s16[144,1024]{1,0:T(8,128)(2,1)S(1)}, u32[]{:S(2)}, u32[]{:S(2)}) collective-permute-start(s16[144,1024]{1,0:T(8,128)(2,1)S(1)} %get-tuple-element.86), channel_id=1, source_target_pairs={{0,16},{8,24},{16,0},{24,8},{1,17},{9,25},{17,1},{25,9},{2,18},{10... | collective-permute-start | bytes 884744 | tf_op jit(solution)/shard_map/ppermute | solution.py:262
  87.2 13.2 %all-to-all-start.1 = ((s16[8,144,128]{2,1,0:T(8,128)(2,1)}), s16[8,144,128]{2,1,0:T(8,128)(2,1)S(1)}, u32[]{:S(2)}, u32[]{:S(2)}) async-start(s16[8,144,128]{2,1,0:T(8,128)(2,1)} %get-tuple-element.80), calls=%async_computation.1 | async-start | bytes 589824 | tf_op jit(solution)/shard_map/all_to_all | solution.py:310
  94.8 9.3 %copy-start = (f32[1024]{0:T(1024)S(1)}, f32[1024]{0:T(1024)}, u32[]{:S(2)}) copy-start(f32[1024]{0:T(1024)} %param.12) | copy-start | bytes 12292
  94.8 9.3 %copy-start.1 = (f32[2,128]{1,0:T(2,128)S(1)}, f32[2,128]{1,0:T(2,128)}, u32[]{:S(2)}) copy-start(f32[2,128]{1,0:T(2,128)} %refs_4_.3) | copy-start | bytes 3076
  94.8 9.3 %copy-start.2 = (s32[128]{0:T(128)S(1)}, s32[128]{0:T(128)}, u32[]{:S(2)}) copy-start(s32[128]{0:T(128)} %param.13) | copy-start | bytes 1540
  100.5 12.8 %all-to-all-start = ((s16[8,144,128]{2,1,0:T(8,128)(2,1)}), s16[8,144,128]{2,1,0:T(8,128)(2,1)S(1)}, u32[]{:S(2)}, u32[]{:S(2)}) async-start(s16[8,144,128]{2,1,0:T(8,128)(2,1)} %get-tuple-element.88), calls=%async_computation | async-start | bytes 589824 | tf_op jit(solution)/shard_map/all_to_all | solution.py:310

commit v3 on v2

--- a/solution.py
+++ b/solution.py
@@ -5,14 +5,15 @@
 from jax.experimental.pallas import tpu as pltpu
 from jax.sharding import PartitionSpec as P
 
-CHUNKS = 4
-PARTS = 2
+CHUNKS = 2
+STREAMS = 2
 LEVELS = 32767.0
 OCTAVE = 128.0
 LANES = 128
 TILE_ROWS = 16
 WIDE = 4
 VMEM = 8 * 1024 * 1024
+SHORT = pl.CostEstimate(flops=1_000_000, bytes_accessed=0, transcendentals=0)
 LONG = pl.CostEstimate(flops=20_000_000_000, bytes_accessed=0, transcendentals=0)
 
 
@@ -44,11 +45,102 @@
     return coded[:-1].astype(jnp.float32) * step_of(coded[-1:])
 
 
+def step_kernel(where_ref, mine_ref, came_ref, odd_ref, even_ref, out_ref):
+    for b in range(out_ref.shape[0]):
+        own, column, side = where_ref[b, 0] == 1, where_ref[b, 1] == 1, where_ref[b, 2] == 1
+
+        @pl.when(own & column)
+        def _():
+            out_ref[b] = mine_ref[...]
+
+        @pl.when(own & ~column)
+        def _():
+            out_ref[b] = came_ref[...]
+
+        @pl.when(~own & side)
+        def _():
+            out_ref[b] = even_ref[b]
+
+        @pl.when(~own & ~side)
+        def _():
+            out_ref[b] = odd_ref[b]
+
+
+def step_on(where, mine, came, by_odd, by_even, cost):
+    vmem = pl.BlockSpec(memory_space=pltpu.VMEM)
+    return pl.pallas_call(
+        step_kernel,
+        out_shape=jax.ShapeDtypeStruct(by_odd.shape, by_odd.dtype),
+        in_specs=[pl.BlockSpec(memory_space=pltpu.SMEM)] + [vmem] * 4,
+        out_specs=vmem,
+        cost_estimate=cost,
+        compiler_params=pltpu.CompilerParams(vmem_limit_bytes=VMEM),
+        name="step_on",
+    )(where, mine, came, by_odd, by_even)
+
+
+def flops(n):
+    return pl.CostEstimate(flops=n, bytes_accessed=0, transcendentals=0)
+
+
+def cost_of(step, q):
+    return LONG if step < 4 or q == 1 else SHORT
+
+
+def begin_kernel(where_ref, mine_ref, came_ref, out_ref):
+    for b in range(out_ref.shape[0]):
+        column = where_ref[b, 1] == 1
+
+        @pl.when(column)
+        def _():
+            out_ref[b] = mine_ref[...]
+
+        @pl.when(~column)
+        def _():
+            out_ref[b] = came_ref[...]
+
+
+def begin(where, mine, came):
+    vmem = pl.BlockSpec(memory_space=pltpu.VMEM)
+    return pl.pallas_call(
+        begin_kernel,
+        out_shape=jax.ShapeDtypeStruct((where.shape[0], *mine.shape), mine.dtype),
+        in_specs=[pl.BlockSpec(memory_space=pltpu.SMEM), vmem, vmem],
+        out_specs=vmem,
+        cost_estimate=LONG,
+        compiler_params=pltpu.CompilerParams(vmem_limit_bytes=VMEM),
+        name="begin",
+    )(where, mine, came)
+
+
+def choose_kernel(away_ref, *refs):
+    out_ref = refs[-1]
+    for b in range(out_ref.shape[0]):
+        for k, ref in enumerate(refs[:-1]):
+
+            @pl.when(away_ref[b] == k)
+            def _():
+                out_ref[b] = ref[b]
+
+
+def choose(away, window):
+    vmem = pl.BlockSpec(memory_space=pltpu.VMEM)
+    return pl.pallas_call(
+        choose_kernel,
+        out_shape=jax.ShapeDtypeStruct(window[0].shape, window[0].dtype),
+        in_specs=[pl.BlockSpec(memory_space=pltpu.SMEM)] + [vmem] * len(window),
+        out_specs=vmem,
+        cost_estimate=SHORT,
+        compiler_params=pltpu.CompilerParams(vmem_limit_bytes=VMEM),
+        name="choose",
+    )(away, *window)
+
+
 def times_kernel(a_ref, w_ref, out_ref):
     out_ref[...] = jnp.dot(a_ref[...], w_ref[...], preferred_element_type=jnp.float32)
 
 
-def times(a, w, aligned):
+def times(a, w, aligned, cost):
     if not aligned:
         return jnp.dot(a, w, preferred_element_type=jnp.float32)
     vmem = pl.BlockSpec(memory_space=pltpu.VMEM)
@@ -57,7 +149,7 @@
         out_shape=jax.ShapeDtypeStruct((a.shape[0], w.shape[1]), jnp.float32),
         in_specs=[vmem, vmem],
         out_specs=vmem,
-        cost_estimate=LONG,
+        cost_estimate=cost,
         compiler_params=pltpu.CompilerParams(vmem_limit_bytes=VMEM),
         name="times",
     )(a, w)
@@ -199,8 +291,9 @@
     lanes = width // parties
     share = rows // groups
     half = share // 2
-    parts, chunks = (PARTS, CHUNKS) if half % (16 * CHUNKS) == 0 else (1, 1)
-    deep = half // chunks
+    streams, chunks = (STREAMS, CHUNKS) if half % (16 * STREAMS * CHUNKS) == 0 else (1, 1)
+    parts = chunks
+    deep = half // (streams * chunks)
     aligned = lanes % LANES == 0 and share % LANES == 0 and bits == 2
     beside = [(o, o ^ 1) for o in range(parties)]
     even = [(o, o ^ 2) for o in range(parties) if (o ^ 2) < parties]
@@ -213,14 +306,15 @@
     def shift(values):
         return lax.ppermute(values, "outpair", odd), lax.ppermute(values, "outpair", even)
 
-    def cut(a, c):
-        return a[:, c * deep : (c + 1) * deep]
+    def cut(a, q, c):
+        return a[:, (c * streams + q) * deep : (c * streams + q + 1) * deep]
 
     me, place = lax.axis_index("outpair").astype(jnp.uint32), lax.axis_index("inpair").astype(jnp.uint32)
     x, z = me & 1, me >> 1
     stored = amplitudes[0].reshape(groups, 2, half, depth)
     other = pick(stored, 1 - x, 1)
-    came = [swap_x(cut(other, c)) for c in range(chunks)]
+    came = [[swap_x(cut(other, q, 0)) for q in range(streams)]]
+    came += [swap_x(tied(jnp.stack([cut(other, q, c) for q in range(streams)]), came[0][0])) for c in range(1, chunks)]
 
     owner = [batch_owner[b].astype(jnp.uint32) for b in range(batches)]
     scalars = dict(
@@ -232,6 +326,13 @@
         far=[jnp.where(z > o >> 1, z - (o >> 1), (o >> 1) - z) for o in owner],
         side=[place >> k & 1 for k in range(bits)],
         not_side=[1 - (place >> k & 1) for k in range(bits)],
+        where=jnp.stack(
+            [
+                jnp.stack([z == o >> 1, x == o & 1, (z > o >> 1) == (z & 1 == 1)]).astype(jnp.int32)
+                for o in owner
+            ]
+        ),
+        away=jnp.stack([jnp.where(z > o >> 1, z - (o >> 1), (o >> 1) - z).astype(jnp.int32) for o in owner]),
         left_word=(x == 0).astype(jnp.int32).reshape(1),
         side_word=(place >> 1 & 1).astype(jnp.int32).reshape(1),
     )
@@ -239,12 +340,10 @@
     flags = jnp.repeat(tile_live.astype(jnp.bfloat16), wide_tile, 1)[:, None, :]
     live = (integrals.reshape(-1, tall_tile, width) * flags).reshape(integrals.shape)
     mine = pick(stored, x, 1)
-    came[0], live, mine, scalars = lax.optimization_barrier((came[0], live, mine, scalars))
+    came[0][0], live, mine, scalars = lax.optimization_barrier((came[0][0], live, mine, scalars))
     left, own, from_even, distance = scalars["left"], scalars["own"], scalars["from_even"], scalars["far"]
     side, not_side = scalars["side"], scalars["not_side"]
 
-    source = [[jnp.where(m, cut(mine, c), came[c]) for m in scalars["mine"]] for c in range(chunks)]
-    held, near, far = [], [], []
     keeps, sent, coded = {}, {}, {}
 
     def sum_part(p, n, f):
@@ -253,8 +352,8 @@
         tall = tall.reshape(2 * batches, groups // 2, 2, count, depth)
         away = pick(tall, not_side[0], 2).reshape(-1, depth)
         stay = pick(tall, side[0], 2).reshape(-1, depth)
-        there = lax.ppermute(times(away, live, aligned), "inpair", [(g, g ^ 1) for g in range(groups)])
-        here = times(stay, live, aligned)
+        there = lax.ppermute(times(away, live, aligned, LONG if p else SHORT), "inpair", [(g, g ^ 1) for g in range(groups)])
+        here = times(stay, live, aligned, LONG if p else SHORT)
         across = lambda k: [(g, g ^ (1 << k)) for g in range(groups)]
         if aligned:
             shape = (2 * batches, 2, count, width)
@@ -272,36 +371,48 @@
         keeps[p] = keep.reshape(2, batches * count, width)
         return sent[p]
 
-    moved = None
-    for step in range(chunks + nz - 1):
-        now = source[min(step, chunks - 1)]
-        if step:
-            others = list(far[-1:])
-            if parts > 1 and step == chunks + nz - 2:
-                others.append(sum_part(0, near[: chunks // 2], far[: chunks // 2]))
-            by_odd, by_even = tied(moved, *others)
-            now = [
-                jnp.where(own[b], now[b], jnp.where(from_even[b], by_even[b], by_odd[b])) for b in range(batches)
-            ]
-        held.append(jnp.stack(now))
-        if step >= nz - 1:
-            window = held[step - nz + 1 : step + 1]
-            got = [pick(jnp.stack([h[b] for h in window]), distance[b], 0) for b in range(batches)]
-            near.append(jnp.stack(got))
-        if step >= nz - 1:
-            far.append(swap_x(near[-1]))
-        if step < chunks + nz - 2:
-            moved = shift(tied(held[-1], *near[-1:]))
+    def advance(q, c, by_odd, by_even, cost):
+        if aligned:
+            return step_on(scalars["where"], cut(mine, q, c), came[c][q], by_odd, by_even, cost)
+        own_chunk = [jnp.where(m, cut(mine, q, c), came[c][q]) for m in scalars["mine"]]
+        return jnp.stack(
+            [jnp.where(own[b], own_chunk[b], jnp.where(from_even[b], by_even[b], by_odd[b])) for b in range(batches)]
+        )
+
+    def settled(window):
+        if aligned:
+            return choose(scalars["away"], window)
+        return jnp.stack([pick(jnp.stack([h[b] for h in window]), distance[b], 0) for b in range(batches)])
+
+    held = []
+    near, far = [[] for _ in range(streams)], [[] for _ in range(streams)]
+    for q in range(streams):
+        if aligned:
+            start = begin(scalars["where"], cut(mine, q, 0), came[0][q])
+        else:
+            start = jnp.stack([jnp.where(m, cut(mine, q, 0), came[0][q]) for m in scalars["mine"]])
+        held.append([start])
+    moved = [shift(h[0]) for h in held]
+    for step in range(1, chunks + nz - 1):
+        for q in range(streams):
+            arrived = moved[q]
+            held[q].append(advance(q, min(step, chunks - 1), *arrived, cost_of(step, q)))
+            if step < chunks + nz - 2:
+                moved[q] = shift(held[q][-1])
+            if step >= nz - 1:
+                near[q].append(settled(held[q][step - nz + 1 : step + 1]))
+                far[q].append(swap_x(near[q][-1]))
 
     word = scalars["left_word"]
     merged = {}
-    if parts > 1:
-        merged[0] = merge(left, word, keeps[0], coded[0], parties, aligned)
-        n, f = tied((near[chunks // 2 :], far[chunks // 2 :]), merged[0])
-    else:
-        n, f = near, far
-    sum_part(parts - 1, n, f)
-    merged[parts - 1] = merge(left, word, keeps[parts - 1], coded[parts - 1], parties, aligned)
+    for p in range(parts):
+        n, f = [near[q][p] for q in range(streams)], [far[q][p] for q in range(streams)]
+        if p:
+            n, f = tied((n, f), *[sent[k] for k in range(p)])
+        sum_part(p, n, f)
+    for p in range(parts):
+        back = tied(coded[p], *[sent[k] for k in range(p + 1, parts)])
+        merged[p] = merge(left, word, keeps[p], back, parties, aligned)
     order = range(parts)
 
     out, parted = None, []

time: 115 us -> 110 us (0.957)
  waiting for transfers between devices: 50.3 us -> 30.6 us
  Pallas kernels: 7.52 us -> 16 us
  starting transfers between devices: 50.6 us -> 58.2 us
  other arithmetic: 2 us -> 0.69 us
    ppermute x6 -> x8, waiting for transfers between devices: 16.2 us -> 2.15 us  [shift(): lax.ppermute(values, 'outpair', even)]
    ppermute x2, waiting for transfers between devices: 9.72 us -> 1.01 us  [sum_part(): coded[p] = lax.ppermute(sent[p], 'inpair', across(1))]
    pallas_call x0 -> x14, Pallas kernels: none -> 8.5 us  [the longest x8 4.87 us: step_on(): pl.pallas_call(step_kernel, out_shape=jax.ShapeDtypeStruct(by_odd.shape,...]
    ppermute x6 -> x8, starting transfers between devices: 23.8 us -> 29.3 us  [shift(): lax.ppermute(values, 'outpair', even)]
    all_to_all x2, waiting for transfers between devices: 12.8 us -> 15.7 us  [on_device(): lax.all_to_all(blocks, 'outpair', split_axis=0, concat_axis=0, tiled=True)]
    ppermute x8 -> x7, waiting for transfers between devices: 7.65 us -> 9.82 us  [swap_x(): return lax.ppermute(values, 'outpair', beside)]
    all_to_all x2, starting transfers between devices: 7.04 us -> 9.18 us  [on_device(): lax.all_to_all(blocks, 'outpair', split_axis=0, concat_axis=0, tiled=True)]
    ppermute x2, waiting for transfers between devices: 3.84 us -> 1.93 us  [sum_part(): lax.ppermute(times(away, live, aligned, LONG if p else SHORT), 'inpair',...]
  transfers between devices with their start and end apart: 26 -> 29, of which waited for: 17 -> 10; matrix products, arithmetic and copies ran while one was open for 1% -> 1% of each run, Pallas kernels for 5% -> 14%
where the time goes in v3:
time: 110 us
  starting transfers between devices  58.2 us (53%)
  waiting for transfers between devices  30.6 us (28%)
  Pallas kernels  16 us (15%)
  local copies, waits for them, and re-layouts  2.36 us (2%)
  between operations  1.72 us (2%)
    ppermute x8, starting transfers between devices, shift(): lax.ppermute(values, 'outpair', even)  29.3 us
    all_to_all x2, waiting for transfers between devices, on_device(): lax.all_to_all(blocks, 'outpair', split_axis=0, concat_axis=0, tiled=True)  15.7 us
    ppermute x7, starting transfers between devices, swap_x(): return lax.ppermute(values, 'outpair', beside)  11.1 us
    ppermute x7, waiting for transfers between devices, swap_x(): return lax.ppermute(values, 'outpair', beside)  9.82 us
    all_to_all x2, starting transfers between devices, on_device(): lax.all_to_all(blocks, 'outpair', split_axis=0, concat_axis=0, tiled=True)  9.18 us
    ppermute x8, starting transfers between devices, shift(): lax.ppermute(values, 'outpair', odd)  5.33 us
    pallas_call x8, Pallas kernels, step_on(): pl.pallas_call(step_kernel, out_shape=jax.ShapeDtypeStruct(by_odd.shape,...  4.87 us
    ppermute x2, starting transfers between devices, sum_part(): coded[p] = lax.ppermute(sent[p], 'inpair', across(1))  3.17 us
  transfers between devices with their start and end apart: 29, of which 10 were waited for; matrix products, arithmetic and copies ran while one was open for 1% of the time, Pallas kernels for 14%

profile of v3, /device:TPU:0, one launch (start us, length us, event | category | flops | bytes accessed | tf_op | source)
XLA Modules:
  0.0 109.6 jit_solution(17516003752352908589)
XLA Ops:
  0.0 1.4 %dynamic-slice_bitcast_fusion = (bf16[4,64,1024]{2,1,0:T(8,128)(2,1)S(1)}, bf16[4,64,1024]{2,1,0:T(8,128)(2,1)S(1)}) fusion(bf16[4,2,64,1024]{3,2,1,0:T(8,128)(2,1)} %bitcast.83, u32[]{:T(128)S(6)} %and.34, u32[]{:T(128)S(6)} %sub.23), kind=kLoop, calls=%fused_computation.7 | loop fusion | bytes 2097160 | tf_op jit(solution)/shard_map/jit(dynamic_index_in_dim)/squeeze | solution.py:21
  1.5 3.0 %collective-permute-start.10 = (bf16[4,16,1024]{2,1,0:T(8,128)(2,1)S(1)}, bf16[4,16,1024]{2,1,0:T(8,128)(2,1)S(1)}, u32[]{:S(2)}, u32[]{:S(2)}) collective-permute-start(bf16[4,16,1024]{2,1,0:T(8,128)(2,1)S(1)} %get-tuple-element.57), channel_id=1, source_target_pairs={{0,1},{1,0},{2,3},{3,2},{4,5},{5,4},{6,7},{7,6},{8,9},{9,8},{10,11... | collective-permute-start | bytes 393224 | tf_op jit(solution)/shard_map/ppermute | solution.py:304
  4.6 0.6 fusion.2
  6.6 0.1 bitcast_multiply_fusion.w_ref
  6.8 4.0 %collective-permute-done.came_ref = bf16[4,16,1024]{2,1,0:T(8,128)(2,1)S(1)} collective-permute-done((bf16[4,16,1024]{2,1,0:T(8,128)(2,1)S(1)}, bf16[4,16,1024]{2,1,0:T(8,128)(2,1)S(1)}, u32[]{:S(2)}, u32[]{:S(2)}) %collective-permute-start) | collective-permute-done | bytes 131104 | tf_op jit(solution)/shard_map/ppermute | solution.py:304
  10.9 0.6 begin.2.refs_0_
  11.4 1.9 %collective-permute-start.3 = (bf16[2,4,16,1024]{3,2,1,0:T(8,128)(2,1)S(1)}, bf16[2,4,16,1024]{3,2,1,0:T(8,128)(2,1)S(1)}, u32[]{:S(2)}, u32[]{:S(2)}) collective-permute-start(bf16[2,4,16,1024]{3,2,1,0:T(8,128)(2,1)S(1)} %begin.2.refs_0_), channel_id=1, source_target_pairs={{0,2},{1,3},{2,0},{3,1},{4,6},{5,7},{6,4},{7,5},{8,10},{9,11},{10,... | collective-permute-start | bytes 786440 | tf_op jit(solution)/shard_map/ppermute | solution.py:307
  13.3 0.7 collective-permute-start.2
  14.0 1.6 %collective-permute-start.1 = (bf16[2,4,16,1024]{3,2,1,0:T(8,128)(2,1)S(1)}, bf16[2,4,16,1024]{3,2,1,0:T(8,128)(2,1)S(1)}, u32[]{:S(2)}, u32[]{:S(2)}) collective-permute-start(bf16[2,4,16,1024]{3,2,1,0:T(8,128)(2,1)S(1)} %pad_maximum_fusion.2), channel_id=1, source_target_pairs={{0,1},{1,0},{2,3},{3,2},{4,5},{5,4},{6,7},{7,6},{8,9},{9,8},{10,11... | collective-permute-start | bytes 786440 | tf_op jit(solution)/shard_map/ppermute | solution.py:304
  15.6 0.6 begin.3.refs_0_
  16.2 4.4 %collective-permute-start.12 = (bf16[2,4,16,1024]{3,2,1,0:T(8,128)(2,1)S(1)}, bf16[2,4,16,1024]{3,2,1,0:T(8,128)(2,1)S(1)}, u32[]{:S(2)}, u32[]{:S(2)}) collective-permute-start(bf16[2,4,16,1024]{3,2,1,0:T(8,128)(2,1)S(1)} %begin.3.refs_0_), channel_id=1, source_target_pairs={{0,2},{1,3},{2,0},{3,1},{4,6},{5,7},{6,4},{7,5},{8,10},{9,11},{10,... | collective-permute-start | bytes 786440 | tf_op jit(solution)/shard_map/ppermute | solution.py:307
  20.6 0.7 collective-permute-start.11
  21.3 0.6 step_on.8.refs_0_.refs_1_
  22.0 3.8 %collective-permute-start.5 = (bf16[2,4,16,1024]{3,2,1,0:T(8,128)(2,1)S(1)}, bf16[2,4,16,1024]{3,2,1,0:T(8,128)(2,1)S(1)}, u32[]{:S(2)}, u32[]{:S(2)}) collective-permute-start(bf16[2,4,16,1024]{3,2,1,0:T(8,128)(2,1)S(1)} %step_on.8.refs_0_.refs_1_), channel_id=1, source_target_pairs={{0,2},{1,3},{2,0},{3,1},{4,6},{5,7},{6,4},{7,5},{8,10},{9,11},{10,... | collective-permute-start | bytes 786440 | tf_op jit(solution)/shard_map/ppermute | solution.py:307
  25.8 0.7 collective-permute-start.4
  26.5 0.6 step_on.12.refs_0_.refs_1_
  27.1 4.0 %collective-permute-start.14 = (bf16[2,4,16,1024]{3,2,1,0:T(8,128)(2,1)S(1)}, bf16[2,4,16,1024]{3,2,1,0:T(8,128)(2,1)S(1)}, u32[]{:S(2)}, u32[]{:S(2)}) collective-permute-start(bf16[2,4,16,1024]{3,2,1,0:T(8,128)(2,1)S(1)} %step_on.12.refs_0_.refs_1_), channel_id=1, source_target_pairs={{0,2},{1,3},{2,0},{3,1},{4,6},{5,7},{6,4},{7,5},{8,10},{9,11},{10,... | collective-permute-start | bytes 786440 | tf_op jit(solution)/shard_map/ppermute | solution.py:307
  31.1 0.7 collective-permute-start.13
  31.8 1.2 %collective-permute-done.5.even_ref = bf16[2,4,16,1024]{3,2,1,0:T(8,128)(2,1)S(1)} collective-permute-done((bf16[2,4,16,1024]{3,2,1,0:T(8,128)(2,1)S(1)}, bf16[2,4,16,1024]{3,2,1,0:T(8,128)(2,1)S(1)}, u32[]{:S(2)}, u32[]{:S(2)}) %collective-permute-start.5) | collective-permute-done | bytes 262176 | tf_op jit(solution)/shard_map/ppermute | solution.py:307
  33.0 0.6 step_on.9.refs_1_.refs_2_
  33.6 3.7 %collective-permute-start.7 = (bf16[2,4,16,1024]{3,2,1,0:T(8,128)(2,1)S(1)}, bf16[2,4,16,1024]{3,2,1,0:T(8,128)(2,1)S(1)}, u32[]{:S(2)}, u32[]{:S(2)}) collective-permute-start(bf16[2,4,16,1024]{3,2,1,0:T(8,128)(2,1)S(1)} %step_on.9.refs_1_.refs_2_), channel_id=1, source_target_pairs={{0,2},{1,3},{2,0},{3,1},{4,6},{5,7},{6,4},{7,5},{8,10},{9,11},{10,... | collective-permute-start | bytes 786440 | tf_op jit(solution)/shard_map/ppermute | solution.py:307
  37.4 0.7 collective-permute-start.6
  38.0 0.6 collective-permute-done.14.even_ref
  38.6 0.6 step_on.13.refs_1_.refs_2_
  39.3 3.7 %collective-permute-start.16 = (bf16[2,4,16,1024]{3,2,1,0:T(8,128)(2,1)S(1)}, bf16[2,4,16,1024]{3,2,1,0:T(8,128)(2,1)S(1)}, u32[]{:S(2)}, u32[]{:S(2)}) collective-permute-start(bf16[2,4,16,1024]{3,2,1,0:T(8,128)(2,1)S(1)} %step_on.13.refs_1_.refs_2_), channel_id=1, source_target_pairs={{0,2},{1,3},{2,0},{3,1},{4,6},{5,7},{6,4},{7,5},{8,10},{9,11},{10,... | collective-permute-start | bytes 786440 | tf_op jit(solution)/shard_map/ppermute | solution.py:307
  43.0 0.7 collective-permute-start.15
  43.7 0.3 collective-permute-done.7.even_ref
  44.0 0.6 step_on.10.refs_2_.refs_3_
  44.6 4.3 %collective-permute-start.9 = (bf16[2,4,16,1024]{3,2,1,0:T(8,128)(2,1)S(1)}, bf16[2,4,16,1024]{3,2,1,0:T(8,128)(2,1)S(1)}, u32[]{:S(2)}, u32[]{:S(2)}) collective-permute-start(bf16[2,4,16,1024]{3,2,1,0:T(8,128)(2,1)S(1)} %step_on.10.refs_2_.refs_3_), channel_id=1, source_target_pairs={{0,2},{1,3},{2,0},{3,1},{4,6},{5,7},{6,4},{7,5},{8,10},{9,11},{10,... | collective-permute-start | bytes 786440 | tf_op jit(solution)/shard_map/ppermute | solution.py:307
  48.9 0.7 collective-permute-start.8
  49.6 0.6 choose.6
  50.2 2.4 %collective-permute-start.21 = (bf16[2,4,16,1024]{3,2,1,0:T(8,128)(2,1)S(1)}, bf16[2,4,16,1024]{3,2,1,0:T(8,128)(2,1)S(1)}, u32[]{:S(2)}, u32[]{:S(2)}) collective-permute-start(bf16[2,4,16,1024]{3,2,1,0:T(8,128)(2,1)S(1)} %choose.6), channel_id=1, source_target_pairs={{0,1},{1,0},{2,3},{3,2},{4,5},{5,4},{6,7},{7,6},{8,9},{9,8},{10,11... | collective-permute-start | bytes 786440 | tf_op jit(solution)/shard_map/ppermute | solution.py:304
  52.6 0.6 step_on.14.refs_2_.refs_3_
  53.2 0.6 choose.7
  53.9 3.3 %collective-permute-start.18 = (bf16[2,4,16,1024]{3,2,1,0:T(8,128)(2,1)S(1)}, bf16[2,4,16,1024]{3,2,1,0:T(8,128)(2,1)S(1)}, u32[]{:S(2)}, u32[]{:S(2)}) collective-permute-start(bf16[2,4,16,1024]{3,2,1,0:T(8,128)(2,1)S(1)} %step_on.14.refs_2_.refs_3_), channel_id=1, source_target_pairs={{0,2},{1,3},{2,0},{3,1},{4,6},{5,7},{6,4},{7,5},{8,10},{9,11},{10,... | collective-permute-start | bytes 786440 | tf_op jit(solution)/shard_map/ppermute | solution.py:307
  57.3 0.7 collective-permute-start.17
  58.0 0.6 step_on.11.refs_3_
  58.6 0.6 choose.4
  59.2 1.9 %collective-permute-start.19 = (bf16[2,4,16,1024]{3,2,1,0:T(8,128)(2,1)S(1)}, bf16[2,4,16,1024]{3,2,1,0:T(8,128)(2,1)S(1)}, u32[]{:S(2)}, u32[]{:S(2)}) collective-permute-start(bf16[2,4,16,1024]{3,2,1,0:T(8,128)(2,1)S(1)} %choose.4), channel_id=1, source_target_pairs={{0,1},{1,0},{2,3},{3,2},{4,5},{5,4},{6,7},{7,6},{8,9},{9,8},{10,11... | collective-permute-start | bytes 786440 | tf_op jit(solution)/shard_map/ppermute | solution.py:304
  61.1 1.4 %collective-permute-done.22 = bf16[2,4,16,1024]{3,2,1,0:T(8,128)(2,1)S(1)} collective-permute-done((bf16[2,4,16,1024]{3,2,1,0:T(8,128)(2,1)S(1)}, bf16[2,4,16,1024]{3,2,1,0:T(8,128)(2,1)S(1)}, u32[]{:S(2)}, u32[]{:S(2)}) %collective-permute-start.22) | collective-permute-done | bytes 262176 | tf_op jit(solution)/shard_map/ppermute | solution.py:304
  62.6 0.1 pad_maximum_fusion
  62.8 0.7 times.5
  63.6 0.6 step_on.15.refs_3_
  64.3 0.6 choose.5
  64.9 2.1 %collective-permute-start.20 = (bf16[2,4,16,1024]{3,2,1,0:T(8,128)(2,1)S(1)}, bf16[2,4,16,1024]{3,2,1,0:T(8,128)(2,1)S(1)}, u32[]{:S(2)}, u32[]{:S(2)}) collective-permute-start(bf16[2,4,16,1024]{3,2,1,0:T(8,128)(2,1)S(1)} %choose.5), channel_id=1, source_target_pairs={{0,1},{1,0},{2,3},{3,2},{4,5},{5,4},{6,7},{7,6},{8,9},{9,8},{10,11... | collective-permute-start | bytes 786440 | tf_op jit(solution)/shard_map/ppermute | solution.py:304
  67.0 0.7 times.4
  67.7 0.2 settle.2
  67.9 1.6 %collective-permute-start.26 = (s16[144,1024]{1,0:T(8,128)(2,1)S(1)}, s16[144,1024]{1,0:T(8,128)(2,1)S(1)}, u32[]{:S(2)}, u32[]{:S(2)}) collective-permute-start(s16[144,1024]{1,0:T(8,128)(2,1)S(1)} %get-tuple-element.38), channel_id=1, source_target_pairs={{0,16},{8,24},{16,0},{24,8},{1,17},{9,25},{17,1},{25,9},{2,18},{10... | collective-permute-start | bytes 884744 | tf_op jit(solution)/shard_map/ppermute | solution.py:361
  69.5 4.4 %collective-permute-done.20 = bf16[2,4,16,1024]{3,2,1,0:T(8,128)(2,1)S(1)} collective-permute-done((bf16[2,4,16,1024]{3,2,1,0:T(8,128)(2,1)S(1)}, bf16[2,4,16,1024]{3,2,1,0:T(8,128)(2,1)S(1)}, u32[]{:S(2)}, u32[]{:S(2)}) %collective-permute-start.20) | collective-permute-done | bytes 262176 | tf_op jit(solution)/shard_map/ppermute | solution.py:304
  74.0 0.1 pad_maximum_fusion.1
  74.2 0.7 times.7
  75.0 0.7 times.6
  75.8 1.9 %collective-permute-done.24 = f32[256,1024]{1,0:T(8,128)S(1)} collective-permute-done((f32[256,1024]{1,0:T(8,128)S(1)}, f32[256,1024]{1,0:T(8,128)S(1)}, u32[]{:S(2)}, u32[]{:S(2)}) %collective-permute-start.24) | collective-permute-done | bytes 1048608 | tf_op jit(solution)/shard_map/ppermute | solution.py:355
  77.7 0.2 settle.3
  77.9 1.6 %collective-permute-start.25 = (s16[144,1024]{1,0:T(8,128)(2,1)S(1)}, s16[144,1024]{1,0:T(8,128)(2,1)S(1)}, u32[]{:S(2)}, u32[]{:S(2)}) collective-permute-start(s16[144,1024]{1,0:T(8,128)(2,1)S(1)} %get-tuple-element.44), channel_id=1, source_target_pairs={{0,16},{8,24},{16,0},{24,8},{1,17},{9,25},{17,1},{25,9},{2,18},{10... | collective-permute-start | bytes 884744 | tf_op jit(solution)/shard_map/ppermute | solution.py:361
  79.5 0.9 merge.3
  80.4 5.6 %all-to-all-start.1 = ((s16[8,144,128]{2,1,0:T(8,128)(2,1)}), s16[8,144,128]{2,1,0:T(8,128)(2,1)S(1)}, u32[]{:S(2)}, u32[]{:S(2)}) async-start(s16[8,144,128]{2,1,0:T(8,128)(2,1)} %get-tuple-element.50), calls=%async_computation.1 | async-start | bytes 589824 | tf_op jit(solution)/shard_map/all_to_all | solution.py:421
  86.0 1.0 collective-permute-done.25.coded_ref
  87.0 0.9 merge.2
  88.0 7.7 %all-to-all-done.1.refs_1_ = s16[8,144,128]{2,1,0:T(8,128)(2,1)S(1)} async-done(((s16[8,144,128]{2,1,0:T(8,128)(2,1)}), s16[8,144,128]{2,1,0:T(8,128)(2,1)S(1)}, u32[]{:S(2)}, u32[]{:S(2)}) %all-to-all-start.1) | async-done | bytes 294944 | tf_op jit(solution)/shard_map/all_to_all | solution.py:421
  95.7 3.6 %all-to-all-start = ((s16[8,144,128]{2,1,0:T(8,128)(2,1)}), s16[8,144,128]{2,1,0:T(8,128)(2,1)S(1)}, u32[]{:S(2)}, u32[]{:S(2)}) async-start(s16[8,144,128]{2,1,0:T(8,128)(2,1)} %get-tuple-element.46), calls=%async_computation | async-start | bytes 589824 | tf_op jit(solution)/shard_map/all_to_all | solution.py:421
  99.3 1.2 %finish.2.refs_5_ = f32[2,2,2,32,1024]{4,3,2,1,0:T(8,128)} custom-call(f32[128,1024]{1,0:T(8,128)S(1)} %get-tuple-element.49.refs_0_, s16[8,144,128]{2,1,0:T(8,128)(2,1)S(1)} %all-to-all-done.1.refs_1_, s32[1,128]{1,0:T(1,128)S(1)} %bitcast.79, f32[1,1024]{1,0:T(1,128)S(1)} %bitcast.77, f32[2,128]{1,0:T(2,128)S(1)} %copy-done.1), custom_call_target="tpu_custom_call" | custom-call | flops 20000000000 | tf_op jit(solution)/shard_map/finish/pallas_call | solution.py:272
  100.4 8.0 %all-to-all-done.refs_1_ = s16[8,144,128]{2,1,0:T(8,128)(2,1)S(1)} async-done(((s16[8,144,128]{2,1,0:T(8,128)(2,1)}), s16[8,144,128]{2,1,0:T(8,128)(2,1)S(1)}, u32[]{:S(2)}, u32[]{:S(2)}) %all-to-all-start) | async-done | bytes 294944 | tf_op jit(solution)/shard_map/all_to_all | solution.py:421
  108.4 1.1 %finish.3 = f32[2,2,2,32,1024]{4,3,2,1,0:T(8,128)} custom-call(f32[128,1024]{1,0:T(8,128)S(1)} %get-tuple-element.45.refs_0_, s16[8,144,128]{2,1,0:T(8,128)(2,1)S(1)} %all-to-all-done.refs_1_, s32[1,128]{1,0:T(1,128)S(1)} %bitcast.80, f32[1,1024]{1,0:T(1,128)S(1)} %bitcast.78, f32[2,128]{1,0:T(2,128)S(1)} %copy-done.1, ...), custom_call_target="tpu_custom_call", output_to_operand_aliasing={{}: (5, {})} | custom-call | flops 20000000000 | tf_op jit(solution)/shard_map/finish/pallas_call | solution.py:272
  (49 shorter events, 1.1 us)
Async XLA Ops:
  0.0 4.6 %copy-start.5 = (s32[2]{0:T(128)S(1)}, s32[2]{0:T(128)}, u32[]{:S(2)}) copy-start(s32[2]{0:T(128)} %param.10) | copy-start | bytes 28
  0.0 6.4 %copy-start.4 = (s32[4,4]{1,0:T(4,128)S(1)}, s32[4,4]{1,0:T(4,128)}, u32[]{:S(2)}) copy-start(s32[4,4]{1,0:T(4,128)} %param.9) | copy-start | bytes 196
  0.0 6.6 %copy-start.3 = (bf16[1024,1024]{1,0:T(8,128)(2,1)S(1)}, bf16[1024,1024]{1,0:T(8,128)(2,1)}, u32[]{:S(2)}) copy-start(bf16[1024,1024]{1,0:T(8,128)(2,1)} %param.7) | copy-start | bytes 6291460
  1.5 14.1 %collective-permute-start.10 = (bf16[4,16,1024]{2,1,0:T(8,128)(2,1)S(1)}, bf16[4,16,1024]{2,1,0:T(8,128)(2,1)S(1)}, u32[]{:S(2)}, u32[]{:S(2)}) collective-permute-start(bf16[4,16,1024]{2,1,0:T(8,128)(2,1)S(1)} %get-tuple-element.57), channel_id=1, source_target_pairs={{0,1},{1,0},{2,3},{3,2},{4,5},{5,4},{6,7},{7,6},{8,9},{9,8},{10,11... | collective-permute-start | bytes 393224 | tf_op jit(solution)/shard_map/ppermute | solution.py:304
  4.5 6.3 %collective-permute-start = (bf16[4,16,1024]{2,1,0:T(8,128)(2,1)S(1)}, bf16[4,16,1024]{2,1,0:T(8,128)(2,1)S(1)}, u32[]{:S(2)}, u32[]{:S(2)}) collective-permute-start(bf16[4,16,1024]{2,1,0:T(8,128)(2,1)S(1)} %get-tuple-element.60), channel_id=1, source_target_pairs={{0,1},{1,0},{2,3},{3,2},{4,5},{5,4},{6,7},{7,6},{8,9},{9,8},{10,11... | collective-permute-start | bytes 393224 | tf_op jit(solution)/shard_map/ppermute | solution.py:304
  11.4 9.9 %collective-permute-start.3 = (bf16[2,4,16,1024]{3,2,1,0:T(8,128)(2,1)S(1)}, bf16[2,4,16,1024]{3,2,1,0:T(8,128)(2,1)S(1)}, u32[]{:S(2)}, u32[]{:S(2)}) collective-permute-start(bf16[2,4,16,1024]{3,2,1,0:T(8,128)(2,1)S(1)} %begin.2.refs_0_), channel_id=1, source_target_pairs={{0,2},{1,3},{2,0},{3,1},{4,6},{5,7},{6,4},{7,5},{8,10},{9,11},{10,... | collective-permute-start | bytes 786440 | tf_op jit(solution)/shard_map/ppermute | solution.py:307
  13.3 8.0 %collective-permute-start.2 = (bf16[2,4,16,1024]{3,2,1,0:T(8,128)(2,1)S(1)}, bf16[2,4,16,1024]{3,2,1,0:T(8,128)(2,1)S(1)}, u32[]{:S(2)}, u32[]{:S(2)}) collective-permute-start(bf16[2,4,16,1024]{3,2,1,0:T(8,128)(2,1)S(1)} %begin.2.refs_0_), channel_id=1, source_target_pairs={{2,4},{3,5},{4,2},{5,3},{10,12},{11,13},{12,10},{13,11},{18,20},{1... | collective-permute-start | bytes 786440 | tf_op jit(solution)/shard_map/ppermute | solution.py:307
  14.0 7.3 %collective-permute-start.1 = (bf16[2,4,16,1024]{3,2,1,0:T(8,128)(2,1)S(1)}, bf16[2,4,16,1024]{3,2,1,0:T(8,128)(2,1)S(1)}, u32[]{:S(2)}, u32[]{:S(2)}) collective-permute-start(bf16[2,4,16,1024]{3,2,1,0:T(8,128)(2,1)S(1)} %pad_maximum_fusion.2), channel_id=1, source_target_pairs={{0,1},{1,0},{2,3},{3,2},{4,5},{5,4},{6,7},{7,6},{8,9},{9,8},{10,11... | collective-permute-start | bytes 786440 | tf_op jit(solution)/shard_map/ppermute | solution.py:304
  16.2 10.3 %collective-permute-start.12 = (bf16[2,4,16,1024]{3,2,1,0:T(8,128)(2,1)S(1)}, bf16[2,4,16,1024]{3,2,1,0:T(8,128)(2,1)S(1)}, u32[]{:S(2)}, u32[]{:S(2)}) collective-permute-start(bf16[2,4,16,1024]{3,2,1,0:T(8,128)(2,1)S(1)} %begin.3.refs_0_), channel_id=1, source_target_pairs={{0,2},{1,3},{2,0},{3,1},{4,6},{5,7},{6,4},{7,5},{8,10},{9,11},{10,... | collective-permute-start | bytes 786440 | tf_op jit(solution)/shard_map/ppermute | solution.py:307
  20.6 5.9 %collective-permute-start.11 = (bf16[2,4,16,1024]{3,2,1,0:T(8,128)(2,1)S(1)}, bf16[2,4,16,1024]{3,2,1,0:T(8,128)(2,1)S(1)}, u32[]{:S(2)}, u32[]{:S(2)}) collective-permute-start(bf16[2,4,16,1024]{3,2,1,0:T(8,128)(2,1)S(1)} %begin.3.refs_0_), channel_id=1, source_target_pairs={{2,4},{3,5},{4,2},{5,3},{10,12},{11,13},{12,10},{13,11},{18,20},{1... | collective-permute-start | bytes 786440 | tf_op jit(solution)/shard_map/ppermute | solution.py:307
  22.0 11.1 %collective-permute-start.5 = (bf16[2,4,16,1024]{3,2,1,0:T(8,128)(2,1)S(1)}, bf16[2,4,16,1024]{3,2,1,0:T(8,128)(2,1)S(1)}, u32[]{:S(2)}, u32[]{:S(2)}) collective-permute-start(bf16[2,4,16,1024]{3,2,1,0:T(8,128)(2,1)S(1)} %step_on.8.refs_0_.refs_1_), channel_id=1, source_target_pairs={{0,2},{1,3},{2,0},{3,1},{4,6},{5,7},{6,4},{7,5},{8,10},{9,11},{10,... | collective-permute-start | bytes 786440 | tf_op jit(solution)/shard_map/ppermute | solution.py:307
  25.8 7.2 %collective-permute-start.4 = (bf16[2,4,16,1024]{3,2,1,0:T(8,128)(2,1)S(1)}, bf16[2,4,16,1024]{3,2,1,0:T(8,128)(2,1)S(1)}, u32[]{:S(2)}, u32[]{:S(2)}) collective-permute-start(bf16[2,4,16,1024]{3,2,1,0:T(8,128)(2,1)S(1)} %step_on.8.refs_0_.refs_1_), channel_id=1, source_target_pairs={{2,4},{3,5},{4,2},{5,3},{10,12},{11,13},{12,10},{13,11},{18,20},{1... | collective-permute-start | bytes 786440 | tf_op jit(solution)/shard_map/ppermute | solution.py:307
  27.1 11.5 %collective-permute-start.14 = (bf16[2,4,16,1024]{3,2,1,0:T(8,128)(2,1)S(1)}, bf16[2,4,16,1024]{3,2,1,0:T(8,128)(2,1)S(1)}, u32[]{:S(2)}, u32[]{:S(2)}) collective-permute-start(bf16[2,4,16,1024]{3,2,1,0:T(8,128)(2,1)S(1)} %step_on.12.refs_0_.refs_1_), channel_id=1, source_target_pairs={{0,2},{1,3},{2,0},{3,1},{4,6},{5,7},{6,4},{7,5},{8,10},{9,11},{10,... | collective-permute-start | bytes 786440 | tf_op jit(solution)/shard_map/ppermute | solution.py:307
  31.1 7.5 %collective-permute-start.13 = (bf16[2,4,16,1024]{3,2,1,0:T(8,128)(2,1)S(1)}, bf16[2,4,16,1024]{3,2,1,0:T(8,128)(2,1)S(1)}, u32[]{:S(2)}, u32[]{:S(2)}) collective-permute-start(bf16[2,4,16,1024]{3,2,1,0:T(8,128)(2,1)S(1)} %step_on.12.refs_0_.refs_1_), channel_id=1, source_target_pairs={{2,4},{3,5},{4,2},{5,3},{10,12},{11,13},{12,10},{13,11},{18,20},{1... | collective-permute-start | bytes 786440 | tf_op jit(solution)/shard_map/ppermute | solution.py:307
  33.6 10.3 %collective-permute-start.7 = (bf16[2,4,16,1024]{3,2,1,0:T(8,128)(2,1)S(1)}, bf16[2,4,16,1024]{3,2,1,0:T(8,128)(2,1)S(1)}, u32[]{:S(2)}, u32[]{:S(2)}) collective-permute-start(bf16[2,4,16,1024]{3,2,1,0:T(8,128)(2,1)S(1)} %step_on.9.refs_1_.refs_2_), channel_id=1, source_target_pairs={{0,2},{1,3},{2,0},{3,1},{4,6},{5,7},{6,4},{7,5},{8,10},{9,11},{10,... | collective-permute-start | bytes 786440 | tf_op jit(solution)/shard_map/ppermute | solution.py:307
  37.4 6.6 %collective-permute-start.6 = (bf16[2,4,16,1024]{3,2,1,0:T(8,128)(2,1)S(1)}, bf16[2,4,16,1024]{3,2,1,0:T(8,128)(2,1)S(1)}, u32[]{:S(2)}, u32[]{:S(2)}) collective-permute-start(bf16[2,4,16,1024]{3,2,1,0:T(8,128)(2,1)S(1)} %step_on.9.refs_1_.refs_2_), channel_id=1, source_target_pairs={{2,4},{3,5},{4,2},{5,3},{10,12},{11,13},{12,10},{13,11},{18,20},{1... | collective-permute-start | bytes 786440 | tf_op jit(solution)/shard_map/ppermute | solution.py:307
  39.3 13.3 %collective-permute-start.16 = (bf16[2,4,16,1024]{3,2,1,0:T(8,128)(2,1)S(1)}, bf16[2,4,16,1024]{3,2,1,0:T(8,128)(2,1)S(1)}, u32[]{:S(2)}, u32[]{:S(2)}) collective-permute-start(bf16[2,4,16,1024]{3,2,1,0:T(8,128)(2,1)S(1)} %step_on.13.refs_1_.refs_2_), channel_id=1, source_target_pairs={{0,2},{1,3},{2,0},{3,1},{4,6},{5,7},{6,4},{7,5},{8,10},{9,11},{10,... | collective-permute-start | bytes 786440 | tf_op jit(solution)/shard_map/ppermute | solution.py:307
  43.0 9.6 %collective-permute-start.15 = (bf16[2,4,16,1024]{3,2,1,0:T(8,128)(2,1)S(1)}, bf16[2,4,16,1024]{3,2,1,0:T(8,128)(2,1)S(1)}, u32[]{:S(2)}, u32[]{:S(2)}) collective-permute-start(bf16[2,4,16,1024]{3,2,1,0:T(8,128)(2,1)S(1)} %step_on.13.refs_1_.refs_2_), channel_id=1, source_target_pairs={{2,4},{3,5},{4,2},{5,3},{10,12},{11,13},{12,10},{13,11},{18,20},{1... | collective-permute-start | bytes 786440 | tf_op jit(solution)/shard_map/ppermute | solution.py:307
  44.6 12.7 %collective-permute-start.9 = (bf16[2,4,16,1024]{3,2,1,0:T(8,128)(2,1)S(1)}, bf16[2,4,16,1024]{3,2,1,0:T(8,128)(2,1)S(1)}, u32[]{:S(2)}, u32[]{:S(2)}) collective-permute-start(bf16[2,4,16,1024]{3,2,1,0:T(8,128)(2,1)S(1)} %step_on.10.refs_2_.refs_3_), channel_id=1, source_target_pairs={{0,2},{1,3},{2,0},{3,1},{4,6},{5,7},{6,4},{7,5},{8,10},{9,11},{10,... | collective-permute-start | bytes 786440 | tf_op jit(solution)/shard_map/ppermute | solution.py:307
  48.9 9.0 %collective-permute-start.8 = (bf16[2,4,16,1024]{3,2,1,0:T(8,128)(2,1)S(1)}, bf16[2,4,16,1024]{3,2,1,0:T(8,128)(2,1)S(1)}, u32[]{:S(2)}, u32[]{:S(2)}) collective-permute-start(bf16[2,4,16,1024]{3,2,1,0:T(8,128)(2,1)S(1)} %step_on.10.refs_2_.refs_3_), channel_id=1, source_target_pairs={{2,4},{3,5},{4,2},{5,3},{10,12},{11,13},{12,10},{13,11},{18,20},{1... | collective-permute-start | bytes 786440 | tf_op jit(solution)/shard_map/ppermute | solution.py:307
  50.2 10.9 %collective-permute-start.21 = (bf16[2,4,16,1024]{3,2,1,0:T(8,128)(2,1)S(1)}, bf16[2,4,16,1024]{3,2,1,0:T(8,128)(2,1)S(1)}, u32[]{:S(2)}, u32[]{:S(2)}) collective-permute-start(bf16[2,4,16,1024]{3,2,1,0:T(8,128)(2,1)S(1)} %choose.6), channel_id=1, source_target_pairs={{0,1},{1,0},{2,3},{3,2},{4,5},{5,4},{6,7},{7,6},{8,9},{9,8},{10,11... | collective-permute-start | bytes 786440 | tf_op jit(solution)/shard_map/ppermute | solution.py:304
  53.8 8.7 %collective-permute-start.22 = (bf16[2,4,16,1024]{3,2,1,0:T(8,128)(2,1)S(1)}, bf16[2,4,16,1024]{3,2,1,0:T(8,128)(2,1)S(1)}, u32[]{:S(2)}, u32[]{:S(2)}) collective-permute-start(bf16[2,4,16,1024]{3,2,1,0:T(8,128)(2,1)S(1)} %choose.7), channel_id=1, source_target_pairs={{0,1},{1,0},{2,3},{3,2},{4,5},{5,4},{6,7},{7,6},{8,9},{9,8},{10,11... | collective-permute-start | bytes 786440 | tf_op jit(solution)/shard_map/ppermute | solution.py:304
  53.9 9.7 %collective-permute-start.18 = (bf16[2,4,16,1024]{3,2,1,0:T(8,128)(2,1)S(1)}, bf16[2,4,16,1024]{3,2,1,0:T(8,128)(2,1)S(1)}, u32[]{:S(2)}, u32[]{:S(2)}) collective-permute-start(bf16[2,4,16,1024]{3,2,1,0:T(8,128)(2,1)S(1)} %step_on.14.refs_2_.refs_3_), channel_id=1, source_target_pairs={{0,2},{1,3},{2,0},{3,1},{4,6},{5,7},{6,4},{7,5},{8,10},{9,11},{10,... | collective-permute-start | bytes 786440 | tf_op jit(solution)/shard_map/ppermute | solution.py:307
  57.3 6.4 %collective-permute-start.17 = (bf16[2,4,16,1024]{3,2,1,0:T(8,128)(2,1)S(1)}, bf16[2,4,16,1024]{3,2,1,0:T(8,128)(2,1)S(1)}, u32[]{:S(2)}, u32[]{:S(2)}) collective-permute-start(bf16[2,4,16,1024]{3,2,1,0:T(8,128)(2,1)S(1)} %step_on.14.refs_2_.refs_3_), channel_id=1, source_target_pairs={{2,4},{3,5},{4,2},{5,3},{10,12},{11,13},{12,10},{13,11},{18,20},{1... | collective-permute-start | bytes 786440 | tf_op jit(solution)/shard_map/ppermute | solution.py:307
  59.2 10.3 %collective-permute-start.19 = (bf16[2,4,16,1024]{3,2,1,0:T(8,128)(2,1)S(1)}, bf16[2,4,16,1024]{3,2,1,0:T(8,128)(2,1)S(1)}, u32[]{:S(2)}, u32[]{:S(2)}) collective-permute-start(bf16[2,4,16,1024]{3,2,1,0:T(8,128)(2,1)S(1)} %choose.4), channel_id=1, source_target_pairs={{0,1},{1,0},{2,3},{3,2},{4,5},{5,4},{6,7},{7,6},{8,9},{9,8},{10,11... | collective-permute-start | bytes 786440 | tf_op jit(solution)/shard_map/ppermute | solution.py:304
  63.5 4.2 %collective-permute-start.23 = (f32[256,1024]{1,0:T(8,128)S(1)}, f32[256,1024]{1,0:T(8,128)S(1)}, u32[]{:S(2)}, u32[]{:S(2)}) collective-permute-start(f32[256,1024]{1,0:T(8,128)S(1)} %times.5), channel_id=1, source_target_pairs={{0,8},{8,0},{16,24},{24,16},{1,9},{9,1},{17,25},{25,17},{2,10},{10... | collective-permute-start | bytes 3145736 | tf_op jit(solution)/shard_map/ppermute | solution.py:355
  64.9 9.0 %collective-permute-start.20 = (bf16[2,4,16,1024]{3,2,1,0:T(8,128)(2,1)S(1)}, bf16[2,4,16,1024]{3,2,1,0:T(8,128)(2,1)S(1)}, u32[]{:S(2)}, u32[]{:S(2)}) collective-permute-start(bf16[2,4,16,1024]{3,2,1,0:T(8,128)(2,1)S(1)} %choose.5), channel_id=1, source_target_pairs={{0,1},{1,0},{2,3},{3,2},{4,5},{5,4},{6,7},{7,6},{8,9},{9,8},{10,11... | collective-permute-start | bytes 786440 | tf_op jit(solution)/shard_map/ppermute | solution.py:304
  67.9 11.6 %collective-permute-start.26 = (s16[144,1024]{1,0:T(8,128)(2,1)S(1)}, s16[144,1024]{1,0:T(8,128)(2,1)S(1)}, u32[]{:S(2)}, u32[]{:S(2)}) collective-permute-start(s16[144,1024]{1,0:T(8,128)(2,1)S(1)} %get-tuple-element.38), channel_id=1, source_target_pairs={{0,16},{8,24},{16,0},{24,8},{1,17},{9,25},{17,1},{25,9},{2,18},{10... | collective-permute-start | bytes 884744 | tf_op jit(solution)/shard_map/ppermute | solution.py:361
  75.0 2.7 %collective-permute-start.24 = (f32[256,1024]{1,0:T(8,128)S(1)}, f32[256,1024]{1,0:T(8,128)S(1)}, u32[]{:S(2)}, u32[]{:S(2)}) collective-permute-start(f32[256,1024]{1,0:T(8,128)S(1)} %times.7), channel_id=1, source_target_pairs={{0,8},{8,0},{16,24},{24,16},{1,9},{9,1},{17,25},{25,17},{2,10},{10... | collective-permute-start | bytes 3145736 | tf_op jit(solution)/shard_map/ppermute | solution.py:355
  77.9 9.1 %collective-permute-start.25 = (s16[144,1024]{1,0:T(8,128)(2,1)S(1)}, s16[144,1024]{1,0:T(8,128)(2,1)S(1)}, u32[]{:S(2)}, u32[]{:S(2)}) collective-permute-start(s16[144,1024]{1,0:T(8,128)(2,1)S(1)} %get-tuple-element.44), channel_id=1, source_target_pairs={{0,16},{8,24},{16,0},{24,8},{1,17},{9,25},{17,1},{25,9},{2,18},{10... | collective-permute-start | bytes 884744 | tf_op jit(solution)/shard_map/ppermute | solution.py:361
  80.4 15.2 %all-to-all-start.1 = ((s16[8,144,128]{2,1,0:T(8,128)(2,1)}), s16[8,144,128]{2,1,0:T(8,128)(2,1)S(1)}, u32[]{:S(2)}, u32[]{:S(2)}) async-start(s16[8,144,128]{2,1,0:T(8,128)(2,1)} %get-tuple-element.50), calls=%async_computation.1 | async-start | bytes 589824 | tf_op jit(solution)/shard_map/all_to_all | solution.py:421
  87.0 12.2 %copy-start = (f32[1024]{0:T(1024)S(1)}, f32[1024]{0:T(1024)}, u32[]{:S(2)}) copy-start(f32[1024]{0:T(1024)} %param.12) | copy-start | bytes 12292
  87.0 12.2 %copy-start.1 = (f32[2,128]{1,0:T(2,128)S(1)}, f32[2,128]{1,0:T(2,128)}, u32[]{:S(2)}) copy-start(f32[2,128]{1,0:T(2,128)} %refs_4_.3) | copy-start | bytes 3076
  87.0 12.2 %copy-start.2 = (s32[128]{0:T(128)S(1)}, s32[128]{0:T(128)}, u32[]{:S(2)}) copy-start(s32[128]{0:T(128)} %param.13) | copy-start | bytes 1540
  95.7 12.8 %all-to-all-start = ((s16[8,144,128]{2,1,0:T(8,128)(2,1)}), s16[8,144,128]{2,1,0:T(8,128)(2,1)S(1)}, u32[]{:S(2)}, u32[]{:S(2)}) async-start(s16[8,144,128]{2,1,0:T(8,128)(2,1)} %get-tuple-element.46), calls=%async_computation | async-start | bytes 589824 | tf_op jit(solution)/shard_map/all_to_all | solution.py:421

commit v4 on v3

--- a/solution.py
+++ b/solution.py
@@ -45,9 +45,10 @@
     return coded[:-1].astype(jnp.float32) * step_of(coded[-1:])
 
 
-def step_kernel(where_ref, mine_ref, came_ref, odd_ref, even_ref, out_ref):
+def step_kernel(*refs):
+    mine_ref, came_ref, odd_ref, even_ref, out_ref = refs[-5:]
     for b in range(out_ref.shape[0]):
-        own, column, side = where_ref[b, 0] == 1, where_ref[b, 1] == 1, where_ref[b, 2] == 1
+        own, column, side = [refs[b][0] >> k & 1 == 1 for k in range(3)]
 
         @pl.when(own & column)
         def _():
@@ -66,17 +67,17 @@
             out_ref[b] = odd_ref[b]
 
 
-def step_on(where, mine, came, by_odd, by_even, cost):
+def step_on(words, mine, came, by_odd, by_even, cost):
     vmem = pl.BlockSpec(memory_space=pltpu.VMEM)
     return pl.pallas_call(
         step_kernel,
         out_shape=jax.ShapeDtypeStruct(by_odd.shape, by_odd.dtype),
-        in_specs=[pl.BlockSpec(memory_space=pltpu.SMEM)] + [vmem] * 4,
+        in_specs=[pl.BlockSpec(memory_space=pltpu.SMEM)] * len(words) + [vmem] * 4,
         out_specs=vmem,
         cost_estimate=cost,
         compiler_params=pltpu.CompilerParams(vmem_limit_bytes=VMEM),
         name="step_on",
-    )(where, mine, came, by_odd, by_even)
+    )(*words, mine, came, by_odd, by_even)
 
 
 def flops(n):
@@ -87,9 +88,10 @@
     return LONG if step < 4 or q == 1 else SHORT
 
 
-def begin_kernel(where_ref, mine_ref, came_ref, out_ref):
+def begin_kernel(*refs):
+    mine_ref, came_ref, out_ref = refs[-3:]
     for b in range(out_ref.shape[0]):
-        column = where_ref[b, 1] == 1
+        column = refs[b][0] >> 1 & 1 == 1
 
         @pl.when(column)
         def _():
@@ -100,40 +102,41 @@
             out_ref[b] = came_ref[...]
 
 
-def begin(where, mine, came):
+def begin(words, mine, came):
     vmem = pl.BlockSpec(memory_space=pltpu.VMEM)
     return pl.pallas_call(
         begin_kernel,
-        out_shape=jax.ShapeDtypeStruct((where.shape[0], *mine.shape), mine.dtype),
-        in_specs=[pl.BlockSpec(memory_space=pltpu.SMEM), vmem, vmem],
+        out_shape=jax.ShapeDtypeStruct((len(words), *mine.shape), mine.dtype),
+        in_specs=[pl.BlockSpec(memory_space=pltpu.SMEM)] * len(words) + [vmem] * 2,
         out_specs=vmem,
         cost_estimate=LONG,
         compiler_params=pltpu.CompilerParams(vmem_limit_bytes=VMEM),
         name="begin",
-    )(where, mine, came)
-
-
-def choose_kernel(away_ref, *refs):
+    )(*words, mine, came)
+
+
+def choose_kernel(*refs):
     out_ref = refs[-1]
-    for b in range(out_ref.shape[0]):
-        for k, ref in enumerate(refs[:-1]):
-
-            @pl.when(away_ref[b] == k)
+    batches = out_ref.shape[0]
+    for b in range(batches):
+        for k, ref in enumerate(refs[batches:-1]):
+
+            @pl.when(refs[b][0] >> 3 == k)
             def _():
                 out_ref[b] = ref[b]
 
 
-def choose(away, window):
+def choose(words, window):
     vmem = pl.BlockSpec(memory_space=pltpu.VMEM)
     return pl.pallas_call(
         choose_kernel,
         out_shape=jax.ShapeDtypeStruct(window[0].shape, window[0].dtype),
-        in_specs=[pl.BlockSpec(memory_space=pltpu.SMEM)] + [vmem] * len(window),
+        in_specs=[pl.BlockSpec(memory_space=pltpu.SMEM)] * len(words) + [vmem] * len(window),
         out_specs=vmem,
         cost_estimate=SHORT,
         compiler_params=pltpu.CompilerParams(vmem_limit_bytes=VMEM),
         name="choose",
-    )(away, *window)
+    )(*words, *window)
 
 
 def times_kernel(a_ref, w_ref, out_ref):
@@ -222,7 +225,7 @@
         ),
         in_specs=[pl.BlockSpec(memory_space=pltpu.SMEM), vmem, vmem],
         out_specs=(vmem, vmem),
-        cost_estimate=LONG,
+        cost_estimate=SHORT,
         compiler_params=pltpu.CompilerParams(vmem_limit_bytes=VMEM),
         name="merge",
     )(left_word, keep, coded)
@@ -313,7 +316,8 @@
     x, z = me & 1, me >> 1
     stored = amplitudes[0].reshape(groups, 2, half, depth)
     other = pick(stored, 1 - x, 1)
-    came = [[swap_x(cut(other, q, 0)) for q in range(streams)]]
+    came = [[swap_x(cut(other, 0, 0))]]
+    came[0] += [swap_x(tied(cut(other, q, 0), came[0][0])) for q in range(1, streams)]
     came += [swap_x(tied(jnp.stack([cut(other, q, c) for q in range(streams)]), came[0][0])) for c in range(1, chunks)]
 
     owner = [batch_owner[b].astype(jnp.uint32) for b in range(batches)]
@@ -326,13 +330,15 @@
         far=[jnp.where(z > o >> 1, z - (o >> 1), (o >> 1) - z) for o in owner],
         side=[place >> k & 1 for k in range(bits)],
         not_side=[1 - (place >> k & 1) for k in range(bits)],
-        where=jnp.stack(
-            [
-                jnp.stack([z == o >> 1, x == o & 1, (z > o >> 1) == (z & 1 == 1)]).astype(jnp.int32)
-                for o in owner
-            ]
-        ),
-        away=jnp.stack([jnp.where(z > o >> 1, z - (o >> 1), (o >> 1) - z).astype(jnp.int32) for o in owner]),
+        words=[
+            (
+                (z == o >> 1).astype(jnp.int32)
+                + 2 * (x == o & 1).astype(jnp.int32)
+                + 4 * ((z > o >> 1) == (z & 1 == 1)).astype(jnp.int32)
+                + 8 * jnp.where(z > o >> 1, z - (o >> 1), (o >> 1) - z).astype(jnp.int32)
+            ).reshape(1)
+            for o in owner
+        ],
         left_word=(x == 0).astype(jnp.int32).reshape(1),
         side_word=(place >> 1 & 1).astype(jnp.int32).reshape(1),
     )
@@ -373,7 +379,7 @@
 
     def advance(q, c, by_odd, by_even, cost):
         if aligned:
-            return step_on(scalars["where"], cut(mine, q, c), came[c][q], by_odd, by_even, cost)
+            return step_on(scalars["words"], cut(mine, q, c), came[c][q], by_odd, by_even, cost)
         own_chunk = [jnp.where(m, cut(mine, q, c), came[c][q]) for m in scalars["mine"]]
         return jnp.stack(
             [jnp.where(own[b], own_chunk[b], jnp.where(from_even[b], by_even[b], by_odd[b])) for b in range(batches)]
@@ -381,14 +387,14 @@
 
     def settled(window):
         if aligned:
-            return choose(scalars["away"], window)
+            return choose(scalars["words"], window)
         return jnp.stack([pick(jnp.stack([h[b] for h in window]), distance[b], 0) for b in range(batches)])
 
     held = []
     near, far = [[] for _ in range(streams)], [[] for _ in range(streams)]
     for q in range(streams):
         if aligned:
-            start = begin(scalars["where"], cut(mine, q, 0), came[0][q])
+            start = begin(scalars["words"], cut(mine, q, 0), came[0][q])
         else:
             start = jnp.stack([jnp.where(m, cut(mine, q, 0), came[0][q]) for m in scalars["mine"]])
         held.append([start])

time: 110 us -> 104 us (0.945)
  Pallas kernels: 16 us -> 8.32 us
  starting transfers between devices: 58.2 us -> 60.4 us
    all_to_all x2, waiting for transfers between devices: 15.7 us -> 7.49 us  [on_device(): lax.all_to_all(blocks, 'outpair', split_axis=0, concat_axis=0, tiled=True)]
    ppermute x2, waiting for transfers between devices: 1.01 us -> 7.26 us  [sum_part(): coded[p] = lax.ppermute(sent[p], 'inpair', across(1))]
    pallas_call x8, Pallas kernels: 4.87 us -> 0.45 us  [step_on(): pl.pallas_call(step_kernel, out_shape=jax.ShapeDtypeStruct(by_odd.shape,...]
    ppermute x8, starting transfers between devices: 29.3 us -> 32.4 us  [shift(): lax.ppermute(values, 'outpair', even)]
    pallas_call x4, Pallas kernels: 2.46 us -> 0.32 us  [choose(): pl.pallas_call(choose_kernel, out_shape=jax.ShapeDtypeStruct(window[0].sh...]
    ppermute x7, starting transfers between devices: 11.1 us -> 9.4 us  [swap_x(): return lax.ppermute(values, 'outpair', beside)]
    ppermute x7, waiting for transfers between devices: 9.82 us -> 11.4 us  [swap_x(): return lax.ppermute(values, 'outpair', beside)]
    ppermute x2, waiting for transfers between devices: 1.93 us -> 3.2 us  [sum_part(): lax.ppermute(times(away, live, aligned, LONG if p else SHORT), 'inpair',...]
  transfers between devices with their start and end apart: 29 -> 29, of which waited for: 10 -> 14; matrix products, arithmetic and copies ran while one was open for 1% -> 1% of each run, Pallas kernels for 14% -> 6%
where the time goes in v4:
time: 104 us
  starting transfers between devices  60.4 us (58%)
  waiting for transfers between devices  30.3 us (29%)
  Pallas kernels  8.32 us (8%)
  local copies, waits for them, and re-layouts  2.43 us (2%)
  between operations  1.72 us (2%)
    ppermute x8, starting transfers between devices, shift(): lax.ppermute(values, 'outpair', even)  32.4 us
    ppermute x7, waiting for transfers between devices, swap_x(): return lax.ppermute(values, 'outpair', beside)  11.4 us
    all_to_all x2, starting transfers between devices, on_device(): lax.all_to_all(blocks, 'outpair', split_axis=0, concat_axis=0, tiled=True)  10.1 us
    ppermute x7, starting transfers between devices, swap_x(): return lax.ppermute(values, 'outpair', beside)  9.4 us
    all_to_all x2, waiting for transfers between devices, on_device(): lax.all_to_all(blocks, 'outpair', split_axis=0, concat_axis=0, tiled=True)  7.49 us
    ppermute x2, waiting for transfers between devices, sum_part(): coded[p] = lax.ppermute(sent[p], 'inpair', across(1))  7.26 us
    ppermute x8, starting transfers between devices, shift(): lax.ppermute(values, 'outpair', odd)  5.32 us
    ppermute x2, waiting for transfers between devices, sum_part(): lax.ppermute(times(away, live, aligned, LONG if p else SHORT), 'inpair',...  3.2 us
  transfers between devices with their start and end apart: 29, of which 14 were waited for; matrix products, arithmetic and copies ran while one was open for 1% of the time, Pallas kernels for 6%

profile of v4, /device:TPU:0, one launch (start us, length us, event | category | flops | bytes accessed | tf_op | source)
XLA Modules:
  0.0 103.7 jit_solution(8853766255491705213)
XLA Ops:
  0.0 1.5 %dynamic-slice_bitcast_fusion = (bf16[4,64,1024]{2,1,0:T(8,128)(2,1)S(1)}, bf16[4,64,1024]{2,1,0:T(8,128)(2,1)S(1)}) fusion(bf16[4,2,64,1024]{3,2,1,0:T(8,128)(2,1)} %bitcast.77, u32[]{:T(128)S(6)} %and.34, u32[]{:T(128)S(6)} %sub.23), kind=kLoop, calls=%fused_computation.7 | loop fusion | bytes 2097160 | tf_op jit(solution)/shard_map/jit(dynamic_index_in_dim)/squeeze | solution.py:21
  1.5 3.0 %collective-permute-start = (bf16[4,16,1024]{2,1,0:T(8,128)(2,1)S(1)}, bf16[4,16,1024]{2,1,0:T(8,128)(2,1)S(1)}, u32[]{:S(2)}, u32[]{:S(2)}) collective-permute-start(bf16[4,16,1024]{2,1,0:T(8,128)(2,1)S(1)} %get-tuple-element.62), channel_id=1, source_target_pairs={{0,1},{1,0},{2,3},{3,2},{4,5},{5,4},{6,7},{7,6},{8,9},{9,8},{10,11... | collective-permute-start | bytes 393224 | tf_op jit(solution)/shard_map/ppermute | solution.py:307
  4.5 0.1 broadcast_bitcast_fusion
  4.6 0.6 fusion.2
  6.5 0.1 bitcast_multiply_fusion.w_ref
  6.7 1.4 %collective-permute-done.refs_3_ = bf16[4,16,1024]{2,1,0:T(8,128)(2,1)S(1)} collective-permute-done((bf16[4,16,1024]{2,1,0:T(8,128)(2,1)S(1)}, bf16[4,16,1024]{2,1,0:T(8,128)(2,1)S(1)}, u32[]{:S(2)}, u32[]{:S(2)}) %collective-permute-start) | collective-permute-done | bytes 131104 | tf_op jit(solution)/shard_map/ppermute | solution.py:307
  8.0 1.7 %collective-permute-start.10 = (bf16[4,16,1024]{2,1,0:T(8,128)(2,1)S(1)}, bf16[4,16,1024]{2,1,0:T(8,128)(2,1)S(1)}, u32[]{:S(2)}, u32[]{:S(2)}) collective-permute-start(bf16[4,16,1024]{2,1,0:T(8,128)(2,1)S(1)} %get-tuple-element.36), channel_id=1, source_target_pairs={{0,1},{1,0},{2,3},{3,2},{4,5},{5,4},{6,7},{7,6},{8,9},{9,8},{10,11... | collective-permute-start | bytes 393224 | tf_op jit(solution)/shard_map/ppermute | solution.py:307
  9.9 1.6 %collective-permute-start.3 = (bf16[2,4,16,1024]{3,2,1,0:T(8,128)(2,1)S(1)}, bf16[2,4,16,1024]{3,2,1,0:T(8,128)(2,1)S(1)}, u32[]{:S(2)}, u32[]{:S(2)}) collective-permute-start(bf16[2,4,16,1024]{3,2,1,0:T(8,128)(2,1)S(1)} %begin.2.refs_2_), channel_id=1, source_target_pairs={{0,2},{1,3},{2,0},{3,1},{4,6},{5,7},{6,4},{7,5},{8,10},{9,11},{10,... | collective-permute-start | bytes 786440 | tf_op jit(solution)/shard_map/ppermute | solution.py:310
  11.5 0.7 collective-permute-start.2
  12.2 0.6 collective-permute-start.1
  12.8 0.5 collective-permute-done.10.refs_3_
  13.3 3.9 %collective-permute-start.12 = (bf16[2,4,16,1024]{3,2,1,0:T(8,128)(2,1)S(1)}, bf16[2,4,16,1024]{3,2,1,0:T(8,128)(2,1)S(1)}, u32[]{:S(2)}, u32[]{:S(2)}) collective-permute-start(bf16[2,4,16,1024]{3,2,1,0:T(8,128)(2,1)S(1)} %begin.3.refs_2_), channel_id=1, source_target_pairs={{0,2},{1,3},{2,0},{3,1},{4,6},{5,7},{6,4},{7,5},{8,10},{9,11},{10,... | collective-permute-start | bytes 786440 | tf_op jit(solution)/shard_map/ppermute | solution.py:310
  17.3 0.7 collective-permute-start.11
  17.9 0.9 collective-permute-done.1
  19.0 4.4 %collective-permute-start.5 = (bf16[2,4,16,1024]{3,2,1,0:T(8,128)(2,1)S(1)}, bf16[2,4,16,1024]{3,2,1,0:T(8,128)(2,1)S(1)}, u32[]{:S(2)}, u32[]{:S(2)}) collective-permute-start(bf16[2,4,16,1024]{3,2,1,0:T(8,128)(2,1)S(1)} %step_on.8.refs_2_.refs_3_), channel_id=1, source_target_pairs={{0,2},{1,3},{2,0},{3,1},{4,6},{5,7},{6,4},{7,5},{8,10},{9,11},{10,... | collective-permute-start | bytes 786440 | tf_op jit(solution)/shard_map/ppermute | solution.py:310
  23.4 0.7 collective-permute-start.4
  24.2 4.7 %collective-permute-start.14 = (bf16[2,4,16,1024]{3,2,1,0:T(8,128)(2,1)S(1)}, bf16[2,4,16,1024]{3,2,1,0:T(8,128)(2,1)S(1)}, u32[]{:S(2)}, u32[]{:S(2)}) collective-permute-start(bf16[2,4,16,1024]{3,2,1,0:T(8,128)(2,1)S(1)} %step_on.12.refs_2_.refs_3_), channel_id=1, source_target_pairs={{0,2},{1,3},{2,0},{3,1},{4,6},{5,7},{6,4},{7,5},{8,10},{9,11},{10,... | collective-permute-start | bytes 786440 | tf_op jit(solution)/shard_map/ppermute | solution.py:310
  28.9 0.7 collective-permute-start.13
  29.6 0.1 collective-permute-done.5.refs_5_
  29.8 5.4 %collective-permute-start.7 = (bf16[2,4,16,1024]{3,2,1,0:T(8,128)(2,1)S(1)}, bf16[2,4,16,1024]{3,2,1,0:T(8,128)(2,1)S(1)}, u32[]{:S(2)}, u32[]{:S(2)}) collective-permute-start(bf16[2,4,16,1024]{3,2,1,0:T(8,128)(2,1)S(1)} %step_on.9.refs_3_.refs_4_), channel_id=1, source_target_pairs={{0,2},{1,3},{2,0},{3,1},{4,6},{5,7},{6,4},{7,5},{8,10},{9,11},{10,... | collective-permute-start | bytes 786440 | tf_op jit(solution)/shard_map/ppermute | solution.py:310
  35.2 0.7 collective-permute-start.6
  35.8 0.2 collective-permute-done.14.refs_5_
  36.1 4.7 %collective-permute-start.16 = (bf16[2,4,16,1024]{3,2,1,0:T(8,128)(2,1)S(1)}, bf16[2,4,16,1024]{3,2,1,0:T(8,128)(2,1)S(1)}, u32[]{:S(2)}, u32[]{:S(2)}) collective-permute-start(bf16[2,4,16,1024]{3,2,1,0:T(8,128)(2,1)S(1)} %step_on.13.refs_3_.refs_4_), channel_id=1, source_target_pairs={{0,2},{1,3},{2,0},{3,1},{4,6},{5,7},{6,4},{7,5},{8,10},{9,11},{10,... | collective-permute-start | bytes 786440 | tf_op jit(solution)/shard_map/ppermute | solution.py:310
  40.8 0.7 collective-permute-start.15
  41.4 0.6 collective-permute-done.7.refs_5_
  42.1 4.3 %collective-permute-start.9 = (bf16[2,4,16,1024]{3,2,1,0:T(8,128)(2,1)S(1)}, bf16[2,4,16,1024]{3,2,1,0:T(8,128)(2,1)S(1)}, u32[]{:S(2)}, u32[]{:S(2)}) collective-permute-start(bf16[2,4,16,1024]{3,2,1,0:T(8,128)(2,1)S(1)} %step_on.10.refs_4_.refs_5_), channel_id=1, source_target_pairs={{0,2},{1,3},{2,0},{3,1},{4,6},{5,7},{6,4},{7,5},{8,10},{9,11},{10,... | collective-permute-start | bytes 786440 | tf_op jit(solution)/shard_map/ppermute | solution.py:310
  46.4 0.7 collective-permute-start.8
  47.1 0.1 choose.6
  47.2 0.5 collective-permute-start.21
  47.7 0.1 choose.7
  47.8 1.7 %collective-permute-start.22 = (bf16[2,4,16,1024]{3,2,1,0:T(8,128)(2,1)S(1)}, bf16[2,4,16,1024]{3,2,1,0:T(8,128)(2,1)S(1)}, u32[]{:S(2)}, u32[]{:S(2)}) collective-permute-start(bf16[2,4,16,1024]{3,2,1,0:T(8,128)(2,1)S(1)} %choose.7), channel_id=1, source_target_pairs={{0,1},{1,0},{2,3},{3,2},{4,5},{5,4},{6,7},{7,6},{8,9},{9,8},{10,11... | collective-permute-start | bytes 786440 | tf_op jit(solution)/shard_map/ppermute | solution.py:307
  49.5 3.3 %collective-permute-start.18 = (bf16[2,4,16,1024]{3,2,1,0:T(8,128)(2,1)S(1)}, bf16[2,4,16,1024]{3,2,1,0:T(8,128)(2,1)S(1)}, u32[]{:S(2)}, u32[]{:S(2)}) collective-permute-start(bf16[2,4,16,1024]{3,2,1,0:T(8,128)(2,1)S(1)} %step_on.14.refs_4_.refs_5_), channel_id=1, source_target_pairs={{0,2},{1,3},{2,0},{3,1},{4,6},{5,7},{6,4},{7,5},{8,10},{9,11},{10,... | collective-permute-start | bytes 786440 | tf_op jit(solution)/shard_map/ppermute | solution.py:310
  52.8 0.7 collective-permute-start.17
  53.6 0.1 choose.4
  53.7 1.4 %collective-permute-start.19 = (bf16[2,4,16,1024]{3,2,1,0:T(8,128)(2,1)S(1)}, bf16[2,4,16,1024]{3,2,1,0:T(8,128)(2,1)S(1)}, u32[]{:S(2)}, u32[]{:S(2)}) collective-permute-start(bf16[2,4,16,1024]{3,2,1,0:T(8,128)(2,1)S(1)} %choose.4), channel_id=1, source_target_pairs={{0,1},{1,0},{2,3},{3,2},{4,5},{5,4},{6,7},{7,6},{8,9},{9,8},{10,11... | collective-permute-start | bytes 786440 | tf_op jit(solution)/shard_map/ppermute | solution.py:307
  55.1 0.9 collective-permute-done.21
  56.0 3.2 %collective-permute-done.22 = bf16[2,4,16,1024]{3,2,1,0:T(8,128)(2,1)S(1)} collective-permute-done((bf16[2,4,16,1024]{3,2,1,0:T(8,128)(2,1)S(1)}, bf16[2,4,16,1024]{3,2,1,0:T(8,128)(2,1)S(1)}, u32[]{:S(2)}, u32[]{:S(2)}) %collective-permute-start.22) | collective-permute-done | bytes 262176 | tf_op jit(solution)/shard_map/ppermute | solution.py:307
  59.2 0.1 pad_maximum_fusion
  59.4 0.1 constant_dynamic-slice_fusion.2
  59.5 0.7 times.5
  60.4 0.1 choose.5
  60.4 0.5 collective-permute-start.20
  60.9 0.7 times.4
  61.6 1.3 %collective-permute-done.23 = f32[256,1024]{1,0:T(8,128)S(1)} collective-permute-done((f32[256,1024]{1,0:T(8,128)S(1)}, f32[256,1024]{1,0:T(8,128)S(1)}, u32[]{:S(2)}, u32[]{:S(2)}) %collective-permute-start.23) | collective-permute-done | bytes 1048608 | tf_op jit(solution)/shard_map/ppermute | solution.py:361
  62.9 0.2 settle.2
  63.1 1.6 %collective-permute-start.26 = (s16[144,1024]{1,0:T(8,128)(2,1)S(1)}, s16[144,1024]{1,0:T(8,128)(2,1)S(1)}, u32[]{:S(2)}, u32[]{:S(2)}) collective-permute-start(s16[144,1024]{1,0:T(8,128)(2,1)S(1)} %get-tuple-element.40), channel_id=1, source_target_pairs={{0,16},{8,24},{16,0},{24,8},{1,17},{9,25},{17,1},{25,9},{2,18},{10... | collective-permute-start | bytes 884744 | tf_op jit(solution)/shard_map/ppermute | solution.py:367
  64.7 4.5 %collective-permute-done.20 = bf16[2,4,16,1024]{3,2,1,0:T(8,128)(2,1)S(1)} collective-permute-done((bf16[2,4,16,1024]{3,2,1,0:T(8,128)(2,1)S(1)}, bf16[2,4,16,1024]{3,2,1,0:T(8,128)(2,1)S(1)}, u32[]{:S(2)}, u32[]{:S(2)}) %collective-permute-start.20) | collective-permute-done | bytes 262176 | tf_op jit(solution)/shard_map/ppermute | solution.py:307
  69.2 0.1 maximum_bitcast_fusion.2
  69.3 0.1 pad_maximum_fusion.1
  69.4 0.1 constant_dynamic-slice_fusion
  69.5 0.7 times.7
  70.3 0.7 times.6
  71.0 1.9 %collective-permute-done.24 = f32[256,1024]{1,0:T(8,128)S(1)} collective-permute-done((f32[256,1024]{1,0:T(8,128)S(1)}, f32[256,1024]{1,0:T(8,128)S(1)}, u32[]{:S(2)}, u32[]{:S(2)}) %collective-permute-start.24) | collective-permute-done | bytes 1048608 | tf_op jit(solution)/shard_map/ppermute | solution.py:361
  73.0 0.2 settle.3
  73.2 0.9 merge.3
  74.1 4.5 %all-to-all-start.1 = ((s16[8,144,128]{2,1,0:T(8,128)(2,1)}), s16[8,144,128]{2,1,0:T(8,128)(2,1)S(1)}, u32[]{:S(2)}, u32[]{:S(2)}) async-start(s16[8,144,128]{2,1,0:T(8,128)(2,1)} %get-tuple-element.52), calls=%async_computation.1 | async-start | bytes 589824 | tf_op jit(solution)/shard_map/all_to_all | solution.py:427
  78.7 1.5 %collective-permute-start.25 = (s16[144,1024]{1,0:T(8,128)(2,1)S(1)}, s16[144,1024]{1,0:T(8,128)(2,1)S(1)}, u32[]{:S(2)}, u32[]{:S(2)}) collective-permute-start(s16[144,1024]{1,0:T(8,128)(2,1)S(1)} %get-tuple-element.46), channel_id=1, source_target_pairs={{0,16},{8,24},{16,0},{24,8},{1,17},{9,25},{17,1},{25,9},{2,18},{10... | collective-permute-start | bytes 884744 | tf_op jit(solution)/shard_map/ppermute | solution.py:367
  80.2 7.3 %collective-permute-done.25.coded_ref = s16[144,1024]{1,0:T(8,128)(2,1)S(1)} collective-permute-done((s16[144,1024]{1,0:T(8,128)(2,1)S(1)}, s16[144,1024]{1,0:T(8,128)(2,1)S(1)}, u32[]{:S(2)}, u32[]{:S(2)}) %collective-permute-start.25) | collective-permute-done | bytes 294944 | tf_op jit(solution)/shard_map/ppermute | solution.py:367
  87.4 0.9 merge.2
  88.4 0.2 all-to-all-done.1.refs_1_
  88.5 5.6 %all-to-all-start = ((s16[8,144,128]{2,1,0:T(8,128)(2,1)}), s16[8,144,128]{2,1,0:T(8,128)(2,1)S(1)}, u32[]{:S(2)}, u32[]{:S(2)}) async-start(s16[8,144,128]{2,1,0:T(8,128)(2,1)} %get-tuple-element.48), calls=%async_computation | async-start | bytes 589824 | tf_op jit(solution)/shard_map/all_to_all | solution.py:427
  94.1 1.2 %finish.2.refs_5_ = f32[2,2,2,32,1024]{4,3,2,1,0:T(8,128)} custom-call(f32[128,1024]{1,0:T(8,128)S(1)} %get-tuple-element.51.refs_0_, s16[8,144,128]{2,1,0:T(8,128)(2,1)S(1)} %all-to-all-done.1.refs_1_, s32[1,128]{1,0:T(1,128)S(1)} %bitcast.73, f32[1,1024]{1,0:T(1,128)S(1)} %bitcast.71, f32[2,128]{1,0:T(2,128)S(1)} %copy-done.1), custom_call_target="tpu_custom_call" | custom-call | flops 20000000000 | tf_op jit(solution)/shard_map/finish/pallas_call | solution.py:275
  95.3 7.3 %all-to-all-done.refs_1_ = s16[8,144,128]{2,1,0:T(8,128)(2,1)S(1)} async-done(((s16[8,144,128]{2,1,0:T(8,128)(2,1)}), s16[8,144,128]{2,1,0:T(8,128)(2,1)S(1)}, u32[]{:S(2)}, u32[]{:S(2)}) %all-to-all-start) | async-done | bytes 294944 | tf_op jit(solution)/shard_map/all_to_all | solution.py:427
  102.6 1.1 %finish.3 = f32[2,2,2,32,1024]{4,3,2,1,0:T(8,128)} custom-call(f32[128,1024]{1,0:T(8,128)S(1)} %get-tuple-element.47.refs_0_, s16[8,144,128]{2,1,0:T(8,128)(2,1)S(1)} %all-to-all-done.refs_1_, s32[1,128]{1,0:T(1,128)S(1)} %bitcast.74, f32[1,1024]{1,0:T(1,128)S(1)} %bitcast.72, f32[2,128]{1,0:T(2,128)S(1)} %copy-done.1, ...), custom_call_target="tpu_custom_call", output_to_operand_aliasing={{}: (5, {})} | custom-call | flops 20000000000 | tf_op jit(solution)/shard_map/finish/pallas_call | solution.py:275
  (47 shorter events, 1.0 us)
Async XLA Ops:
  0.0 4.5 %copy-start.4 = (s32[4,4]{1,0:T(4,128)S(1)}, s32[4,4]{1,0:T(4,128)}, u32[]{:S(2)}) copy-start(s32[4,4]{1,0:T(4,128)} %param.9) | copy-start | bytes 196
  0.0 4.6 %copy-start.5 = (s32[2]{0:T(128)S(1)}, s32[2]{0:T(128)}, u32[]{:S(2)}) copy-start(s32[2]{0:T(128)} %param.10) | copy-start | bytes 28
  0.0 6.5 %copy-start.3 = (bf16[1024,1024]{1,0:T(8,128)(2,1)S(1)}, bf16[1024,1024]{1,0:T(8,128)(2,1)}, u32[]{:S(2)}) copy-start(bf16[1024,1024]{1,0:T(8,128)(2,1)} %param.7) | copy-start | bytes 6291460
  1.5 6.5 %collective-permute-start = (bf16[4,16,1024]{2,1,0:T(8,128)(2,1)S(1)}, bf16[4,16,1024]{2,1,0:T(8,128)(2,1)S(1)}, u32[]{:S(2)}, u32[]{:S(2)}) collective-permute-start(bf16[4,16,1024]{2,1,0:T(8,128)(2,1)S(1)} %get-tuple-element.62), channel_id=1, source_target_pairs={{0,1},{1,0},{2,3},{3,2},{4,5},{5,4},{6,7},{7,6},{8,9},{9,8},{10,11... | collective-permute-start | bytes 393224 | tf_op jit(solution)/shard_map/ppermute | solution.py:307
  8.0 5.3 %collective-permute-start.10 = (bf16[4,16,1024]{2,1,0:T(8,128)(2,1)S(1)}, bf16[4,16,1024]{2,1,0:T(8,128)(2,1)S(1)}, u32[]{:S(2)}, u32[]{:S(2)}) collective-permute-start(bf16[4,16,1024]{2,1,0:T(8,128)(2,1)S(1)} %get-tuple-element.36), channel_id=1, source_target_pairs={{0,1},{1,0},{2,3},{3,2},{4,5},{5,4},{6,7},{7,6},{8,9},{9,8},{10,11... | collective-permute-start | bytes 393224 | tf_op jit(solution)/shard_map/ppermute | solution.py:307
  9.9 9.0 %collective-permute-start.3 = (bf16[2,4,16,1024]{3,2,1,0:T(8,128)(2,1)S(1)}, bf16[2,4,16,1024]{3,2,1,0:T(8,128)(2,1)S(1)}, u32[]{:S(2)}, u32[]{:S(2)}) collective-permute-start(bf16[2,4,16,1024]{3,2,1,0:T(8,128)(2,1)S(1)} %begin.2.refs_2_), channel_id=1, source_target_pairs={{0,2},{1,3},{2,0},{3,1},{4,6},{5,7},{6,4},{7,5},{8,10},{9,11},{10,... | collective-permute-start | bytes 786440 | tf_op jit(solution)/shard_map/ppermute | solution.py:310
  11.5 7.4 %collective-permute-start.2 = (bf16[2,4,16,1024]{3,2,1,0:T(8,128)(2,1)S(1)}, bf16[2,4,16,1024]{3,2,1,0:T(8,128)(2,1)S(1)}, u32[]{:S(2)}, u32[]{:S(2)}) collective-permute-start(bf16[2,4,16,1024]{3,2,1,0:T(8,128)(2,1)S(1)} %begin.2.refs_2_), channel_id=1, source_target_pairs={{2,4},{3,5},{4,2},{5,3},{10,12},{11,13},{12,10},{13,11},{18,20},{1... | collective-permute-start | bytes 786440 | tf_op jit(solution)/shard_map/ppermute | solution.py:310
  12.2 6.7 %collective-permute-start.1 = (bf16[2,4,16,1024]{3,2,1,0:T(8,128)(2,1)S(1)}, bf16[2,4,16,1024]{3,2,1,0:T(8,128)(2,1)S(1)}, u32[]{:S(2)}, u32[]{:S(2)}) collective-permute-start(bf16[2,4,16,1024]{3,2,1,0:T(8,128)(2,1)S(1)} %pad_maximum_fusion.2), channel_id=1, source_target_pairs={{0,1},{1,0},{2,3},{3,2},{4,5},{5,4},{6,7},{7,6},{8,9},{9,8},{10,11... | collective-permute-start | bytes 786440 | tf_op jit(solution)/shard_map/ppermute | solution.py:307
  13.3 10.8 %collective-permute-start.12 = (bf16[2,4,16,1024]{3,2,1,0:T(8,128)(2,1)S(1)}, bf16[2,4,16,1024]{3,2,1,0:T(8,128)(2,1)S(1)}, u32[]{:S(2)}, u32[]{:S(2)}) collective-permute-start(bf16[2,4,16,1024]{3,2,1,0:T(8,128)(2,1)S(1)} %begin.3.refs_2_), channel_id=1, source_target_pairs={{0,2},{1,3},{2,0},{3,1},{4,6},{5,7},{6,4},{7,5},{8,10},{9,11},{10,... | collective-permute-start | bytes 786440 | tf_op jit(solution)/shard_map/ppermute | solution.py:310
  17.3 6.8 %collective-permute-start.11 = (bf16[2,4,16,1024]{3,2,1,0:T(8,128)(2,1)S(1)}, bf16[2,4,16,1024]{3,2,1,0:T(8,128)(2,1)S(1)}, u32[]{:S(2)}, u32[]{:S(2)}) collective-permute-start(bf16[2,4,16,1024]{3,2,1,0:T(8,128)(2,1)S(1)} %begin.3.refs_2_), channel_id=1, source_target_pairs={{2,4},{3,5},{4,2},{5,3},{10,12},{11,13},{12,10},{13,11},{18,20},{1... | collective-permute-start | bytes 786440 | tf_op jit(solution)/shard_map/ppermute | solution.py:310
  19.0 10.7 %collective-permute-start.5 = (bf16[2,4,16,1024]{3,2,1,0:T(8,128)(2,1)S(1)}, bf16[2,4,16,1024]{3,2,1,0:T(8,128)(2,1)S(1)}, u32[]{:S(2)}, u32[]{:S(2)}) collective-permute-start(bf16[2,4,16,1024]{3,2,1,0:T(8,128)(2,1)S(1)} %step_on.8.refs_2_.refs_3_), channel_id=1, source_target_pairs={{0,2},{1,3},{2,0},{3,1},{4,6},{5,7},{6,4},{7,5},{8,10},{9,11},{10,... | collective-permute-start | bytes 786440 | tf_op jit(solution)/shard_map/ppermute | solution.py:310
  23.4 6.3 %collective-permute-start.4 = (bf16[2,4,16,1024]{3,2,1,0:T(8,128)(2,1)S(1)}, bf16[2,4,16,1024]{3,2,1,0:T(8,128)(2,1)S(1)}, u32[]{:S(2)}, u32[]{:S(2)}) collective-permute-start(bf16[2,4,16,1024]{3,2,1,0:T(8,128)(2,1)S(1)} %step_on.8.refs_2_.refs_3_), channel_id=1, source_target_pairs={{2,4},{3,5},{4,2},{5,3},{10,12},{11,13},{12,10},{13,11},{18,20},{1... | collective-permute-start | bytes 786440 | tf_op jit(solution)/shard_map/ppermute | solution.py:310
  24.2 11.8 %collective-permute-start.14 = (bf16[2,4,16,1024]{3,2,1,0:T(8,128)(2,1)S(1)}, bf16[2,4,16,1024]{3,2,1,0:T(8,128)(2,1)S(1)}, u32[]{:S(2)}, u32[]{:S(2)}) collective-permute-start(bf16[2,4,16,1024]{3,2,1,0:T(8,128)(2,1)S(1)} %step_on.12.refs_2_.refs_3_), channel_id=1, source_target_pairs={{0,2},{1,3},{2,0},{3,1},{4,6},{5,7},{6,4},{7,5},{8,10},{9,11},{10,... | collective-permute-start | bytes 786440 | tf_op jit(solution)/shard_map/ppermute | solution.py:310
  28.9 7.1 %collective-permute-start.13 = (bf16[2,4,16,1024]{3,2,1,0:T(8,128)(2,1)S(1)}, bf16[2,4,16,1024]{3,2,1,0:T(8,128)(2,1)S(1)}, u32[]{:S(2)}, u32[]{:S(2)}) collective-permute-start(bf16[2,4,16,1024]{3,2,1,0:T(8,128)(2,1)S(1)} %step_on.12.refs_2_.refs_3_), channel_id=1, source_target_pairs={{2,4},{3,5},{4,2},{5,3},{10,12},{11,13},{12,10},{13,11},{18,20},{1... | collective-permute-start | bytes 786440 | tf_op jit(solution)/shard_map/ppermute | solution.py:310
  29.8 12.3 %collective-permute-start.7 = (bf16[2,4,16,1024]{3,2,1,0:T(8,128)(2,1)S(1)}, bf16[2,4,16,1024]{3,2,1,0:T(8,128)(2,1)S(1)}, u32[]{:S(2)}, u32[]{:S(2)}) collective-permute-start(bf16[2,4,16,1024]{3,2,1,0:T(8,128)(2,1)S(1)} %step_on.9.refs_3_.refs_4_), channel_id=1, source_target_pairs={{0,2},{1,3},{2,0},{3,1},{4,6},{5,7},{6,4},{7,5},{8,10},{9,11},{10,... | collective-permute-start | bytes 786440 | tf_op jit(solution)/shard_map/ppermute | solution.py:310
  35.2 6.9 %collective-permute-start.6 = (bf16[2,4,16,1024]{3,2,1,0:T(8,128)(2,1)S(1)}, bf16[2,4,16,1024]{3,2,1,0:T(8,128)(2,1)S(1)}, u32[]{:S(2)}, u32[]{:S(2)}) collective-permute-start(bf16[2,4,16,1024]{3,2,1,0:T(8,128)(2,1)S(1)} %step_on.9.refs_3_.refs_4_), channel_id=1, source_target_pairs={{2,4},{3,5},{4,2},{5,3},{10,12},{11,13},{12,10},{13,11},{18,20},{1... | collective-permute-start | bytes 786440 | tf_op jit(solution)/shard_map/ppermute | solution.py:310
  36.1 11.6 %collective-permute-start.16 = (bf16[2,4,16,1024]{3,2,1,0:T(8,128)(2,1)S(1)}, bf16[2,4,16,1024]{3,2,1,0:T(8,128)(2,1)S(1)}, u32[]{:S(2)}, u32[]{:S(2)}) collective-permute-start(bf16[2,4,16,1024]{3,2,1,0:T(8,128)(2,1)S(1)} %step_on.13.refs_3_.refs_4_), channel_id=1, source_target_pairs={{0,2},{1,3},{2,0},{3,1},{4,6},{5,7},{6,4},{7,5},{8,10},{9,11},{10,... | collective-permute-start | bytes 786440 | tf_op jit(solution)/shard_map/ppermute | solution.py:310
  40.8 6.9 %collective-permute-start.15 = (bf16[2,4,16,1024]{3,2,1,0:T(8,128)(2,1)S(1)}, bf16[2,4,16,1024]{3,2,1,0:T(8,128)(2,1)S(1)}, u32[]{:S(2)}, u32[]{:S(2)}) collective-permute-start(bf16[2,4,16,1024]{3,2,1,0:T(8,128)(2,1)S(1)} %step_on.13.refs_3_.refs_4_), channel_id=1, source_target_pairs={{2,4},{3,5},{4,2},{5,3},{10,12},{11,13},{12,10},{13,11},{18,20},{1... | collective-permute-start | bytes 786440 | tf_op jit(solution)/shard_map/ppermute | solution.py:310
  42.1 10.7 %collective-permute-start.9 = (bf16[2,4,16,1024]{3,2,1,0:T(8,128)(2,1)S(1)}, bf16[2,4,16,1024]{3,2,1,0:T(8,128)(2,1)S(1)}, u32[]{:S(2)}, u32[]{:S(2)}) collective-permute-start(bf16[2,4,16,1024]{3,2,1,0:T(8,128)(2,1)S(1)} %step_on.10.refs_4_.refs_5_), channel_id=1, source_target_pairs={{0,2},{1,3},{2,0},{3,1},{4,6},{5,7},{6,4},{7,5},{8,10},{9,11},{10,... | collective-permute-start | bytes 786440 | tf_op jit(solution)/shard_map/ppermute | solution.py:310
  46.4 7.1 %collective-permute-start.8 = (bf16[2,4,16,1024]{3,2,1,0:T(8,128)(2,1)S(1)}, bf16[2,4,16,1024]{3,2,1,0:T(8,128)(2,1)S(1)}, u32[]{:S(2)}, u32[]{:S(2)}) collective-permute-start(bf16[2,4,16,1024]{3,2,1,0:T(8,128)(2,1)S(1)} %step_on.10.refs_4_.refs_5_), channel_id=1, source_target_pairs={{2,4},{3,5},{4,2},{5,3},{10,12},{11,13},{12,10},{13,11},{18,20},{1... | collective-permute-start | bytes 786440 | tf_op jit(solution)/shard_map/ppermute | solution.py:310
  47.2 8.8 %collective-permute-start.21 = (bf16[2,4,16,1024]{3,2,1,0:T(8,128)(2,1)S(1)}, bf16[2,4,16,1024]{3,2,1,0:T(8,128)(2,1)S(1)}, u32[]{:S(2)}, u32[]{:S(2)}) collective-permute-start(bf16[2,4,16,1024]{3,2,1,0:T(8,128)(2,1)S(1)} %choose.6), channel_id=1, source_target_pairs={{0,1},{1,0},{2,3},{3,2},{4,5},{5,4},{6,7},{7,6},{8,9},{9,8},{10,11... | collective-permute-start | bytes 786440 | tf_op jit(solution)/shard_map/ppermute | solution.py:307
  47.8 11.4 %collective-permute-start.22 = (bf16[2,4,16,1024]{3,2,1,0:T(8,128)(2,1)S(1)}, bf16[2,4,16,1024]{3,2,1,0:T(8,128)(2,1)S(1)}, u32[]{:S(2)}, u32[]{:S(2)}) collective-permute-start(bf16[2,4,16,1024]{3,2,1,0:T(8,128)(2,1)S(1)} %choose.7), channel_id=1, source_target_pairs={{0,1},{1,0},{2,3},{3,2},{4,5},{5,4},{6,7},{7,6},{8,9},{9,8},{10,11... | collective-permute-start | bytes 786440 | tf_op jit(solution)/shard_map/ppermute | solution.py:307
  49.5 10.8 %collective-permute-start.18 = (bf16[2,4,16,1024]{3,2,1,0:T(8,128)(2,1)S(1)}, bf16[2,4,16,1024]{3,2,1,0:T(8,128)(2,1)S(1)}, u32[]{:S(2)}, u32[]{:S(2)}) collective-permute-start(bf16[2,4,16,1024]{3,2,1,0:T(8,128)(2,1)S(1)} %step_on.14.refs_4_.refs_5_), channel_id=1, source_target_pairs={{0,2},{1,3},{2,0},{3,1},{4,6},{5,7},{6,4},{7,5},{8,10},{9,11},{10,... | collective-permute-start | bytes 786440 | tf_op jit(solution)/shard_map/ppermute | solution.py:310
  52.8 7.5 %collective-permute-start.17 = (bf16[2,4,16,1024]{3,2,1,0:T(8,128)(2,1)S(1)}, bf16[2,4,16,1024]{3,2,1,0:T(8,128)(2,1)S(1)}, u32[]{:S(2)}, u32[]{:S(2)}) collective-permute-start(bf16[2,4,16,1024]{3,2,1,0:T(8,128)(2,1)S(1)} %step_on.14.refs_4_.refs_5_), channel_id=1, source_target_pairs={{2,4},{3,5},{4,2},{5,3},{10,12},{11,13},{12,10},{13,11},{18,20},{1... | collective-permute-start | bytes 786440 | tf_op jit(solution)/shard_map/ppermute | solution.py:310
  53.7 11.1 %collective-permute-start.19 = (bf16[2,4,16,1024]{3,2,1,0:T(8,128)(2,1)S(1)}, bf16[2,4,16,1024]{3,2,1,0:T(8,128)(2,1)S(1)}, u32[]{:S(2)}, u32[]{:S(2)}) collective-permute-start(bf16[2,4,16,1024]{3,2,1,0:T(8,128)(2,1)S(1)} %choose.4), channel_id=1, source_target_pairs={{0,1},{1,0},{2,3},{3,2},{4,5},{5,4},{6,7},{7,6},{8,9},{9,8},{10,11... | collective-permute-start | bytes 786440 | tf_op jit(solution)/shard_map/ppermute | solution.py:307
  60.2 2.7 %collective-permute-start.23 = (f32[256,1024]{1,0:T(8,128)S(1)}, f32[256,1024]{1,0:T(8,128)S(1)}, u32[]{:S(2)}, u32[]{:S(2)}) collective-permute-start(f32[256,1024]{1,0:T(8,128)S(1)} %times.5), channel_id=1, source_target_pairs={{0,8},{8,0},{16,24},{24,16},{1,9},{9,1},{17,25},{25,17},{2,10},{10... | collective-permute-start | bytes 3145736 | tf_op jit(solution)/shard_map/ppermute | solution.py:361
  60.4 8.7 %collective-permute-start.20 = (bf16[2,4,16,1024]{3,2,1,0:T(8,128)(2,1)S(1)}, bf16[2,4,16,1024]{3,2,1,0:T(8,128)(2,1)S(1)}, u32[]{:S(2)}, u32[]{:S(2)}) collective-permute-start(bf16[2,4,16,1024]{3,2,1,0:T(8,128)(2,1)S(1)} %choose.5), channel_id=1, source_target_pairs={{0,1},{1,0},{2,3},{3,2},{4,5},{5,4},{6,7},{7,6},{8,9},{9,8},{10,11... | collective-permute-start | bytes 786440 | tf_op jit(solution)/shard_map/ppermute | solution.py:307
  63.1 10.1 %collective-permute-start.26 = (s16[144,1024]{1,0:T(8,128)(2,1)S(1)}, s16[144,1024]{1,0:T(8,128)(2,1)S(1)}, u32[]{:S(2)}, u32[]{:S(2)}) collective-permute-start(s16[144,1024]{1,0:T(8,128)(2,1)S(1)} %get-tuple-element.40), channel_id=1, source_target_pairs={{0,16},{8,24},{16,0},{24,8},{1,17},{9,25},{17,1},{25,9},{2,18},{10... | collective-permute-start | bytes 884744 | tf_op jit(solution)/shard_map/ppermute | solution.py:367
  70.2 2.7 %collective-permute-start.24 = (f32[256,1024]{1,0:T(8,128)S(1)}, f32[256,1024]{1,0:T(8,128)S(1)}, u32[]{:S(2)}, u32[]{:S(2)}) collective-permute-start(f32[256,1024]{1,0:T(8,128)S(1)} %times.7), channel_id=1, source_target_pairs={{0,8},{8,0},{16,24},{24,16},{1,9},{9,1},{17,25},{25,17},{2,10},{10... | collective-permute-start | bytes 3145736 | tf_op jit(solution)/shard_map/ppermute | solution.py:361
  73.0 21.1 %copy-start = (f32[1024]{0:T(1024)S(1)}, f32[1024]{0:T(1024)}, u32[]{:S(2)}) copy-start(f32[1024]{0:T(1024)} %param.12) | copy-start | bytes 12292
  73.0 21.1 %copy-start.1 = (f32[2,128]{1,0:T(2,128)S(1)}, f32[2,128]{1,0:T(2,128)}, u32[]{:S(2)}) copy-start(f32[2,128]{1,0:T(2,128)} %refs_4_.3) | copy-start | bytes 3076
  73.0 21.1 %copy-start.2 = (s32[128]{0:T(128)S(1)}, s32[128]{0:T(128)}, u32[]{:S(2)}) copy-start(s32[128]{0:T(128)} %param.13) | copy-start | bytes 1540
  74.1 14.4 %all-to-all-start.1 = ((s16[8,144,128]{2,1,0:T(8,128)(2,1)}), s16[8,144,128]{2,1,0:T(8,128)(2,1)S(1)}, u32[]{:S(2)}, u32[]{:S(2)}) async-start(s16[8,144,128]{2,1,0:T(8,128)(2,1)} %get-tuple-element.52), calls=%async_computation.1 | async-start | bytes 589824 | tf_op jit(solution)/shard_map/all_to_all | solution.py:427
  78.7 8.8 %collective-permute-start.25 = (s16[144,1024]{1,0:T(8,128)(2,1)S(1)}, s16[144,1024]{1,0:T(8,128)(2,1)S(1)}, u32[]{:S(2)}, u32[]{:S(2)}) collective-permute-start(s16[144,1024]{1,0:T(8,128)(2,1)S(1)} %get-tuple-element.46), channel_id=1, source_target_pairs={{0,16},{8,24},{16,0},{24,8},{1,17},{9,25},{17,1},{25,9},{2,18},{10... | collective-permute-start | bytes 884744 | tf_op jit(solution)/shard_map/ppermute | solution.py:367
  88.5 14.1 %all-to-all-start = ((s16[8,144,128]{2,1,0:T(8,128)(2,1)}), s16[8,144,128]{2,1,0:T(8,128)(2,1)S(1)}, u32[]{:S(2)}, u32[]{:S(2)}) async-start(s16[8,144,128]{2,1,0:T(8,128)(2,1)} %get-tuple-element.48), calls=%async_computation | async-start | bytes 589824 | tf_op jit(solution)/shard_map/all_to_all | solution.py:427

commit v5 on v4

--- a/solution.py
+++ b/solution.py
@@ -316,7 +316,10 @@
     x, z = me & 1, me >> 1
     stored = amplitudes[0].reshape(groups, 2, half, depth)
     other = pick(stored, 1 - x, 1)
-    came = [[swap_x(cut(other, 0, 0))]]
+    zero = jnp.uint32(0)
+    first = lax.dynamic_slice(stored, (zero, 1 - x, zero, zero), (groups, 1, deep, depth))[:, 0]
+    came = [[swap_x(first)]]
+    other = pick(tied(stored, first), 1 - x, 1)
     came[0] += [swap_x(tied(cut(other, q, 0), came[0][0])) for q in range(1, streams)]
     came += [swap_x(tied(jnp.stack([cut(other, q, c) for q in range(streams)]), came[0][0])) for c in range(1, chunks)]
 
@@ -346,7 +349,7 @@
     flags = jnp.repeat(tile_live.astype(jnp.bfloat16), wide_tile, 1)[:, None, :]
     live = (integrals.reshape(-1, tall_tile, width) * flags).reshape(integrals.shape)
     mine = pick(stored, x, 1)
-    came[0][0], live, mine, scalars = lax.optimization_barrier((came[0][0], live, mine, scalars))
+    came[0][0], mine, scalars = lax.optimization_barrier((came[0][0], mine, scalars))
     left, own, from_even, distance = scalars["left"], scalars["own"], scalars["from_even"], scalars["far"]
     side, not_side = scalars["side"], scalars["not_side"]
 

time: 104 us -> 104 us (level)
    squeeze x1 -> x2, local copies, waits for them, and re-layouts: 1.45 us -> 0.07 us  [pick(): return lax.dynamic_index_in_dim(array, index, axis, keepdims=False)]
    unnamed x14 -> x18, local copies, waits for them, and re-layouts: 0.1 us -> 1.33 us
  transfers between devices with their start and end apart: 29 -> 29, of which waited for: 14 -> 13; matrix products, arithmetic and copies ran while one was open for 1% -> 2% of each run, Pallas kernels for 6% -> 6%
where the time goes in v5:
time: 104 us; the launch traced here: 103 us
  starting transfers between devices  60.6 us (58%)
  waiting for transfers between devices  29.4 us (28%)
  Pallas kernels  8.31 us (8%)
  local copies, waits for them, and re-layouts  2.27 us (2%)
  between operations  1.77 us (2%)
  other arithmetic  1.11 us (1%)
    ppermute x8, starting transfers between devices, shift(): lax.ppermute(values, 'outpair', even)  33.2 us
    ppermute x7, waiting for transfers between devices, swap_x(): return lax.ppermute(values, 'outpair', beside)  10.6 us
    all_to_all x2, starting transfers between devices, on_device(): lax.all_to_all(blocks, 'outpair', split_axis=0, concat_axis=0, tiled=True)  10.1 us
    ppermute x7, starting transfers between devices, swap_x(): return lax.ppermute(values, 'outpair', beside)  8.77 us
    all_to_all x2, waiting for transfers between devices, on_device(): lax.all_to_all(blocks, 'outpair', split_axis=0, concat_axis=0, tiled=True)  7.5 us
    ppermute x2, waiting for transfers between devices, sum_part(): coded[p] = lax.ppermute(sent[p], 'inpair', across(1))  7.25 us
    ppermute x8, starting transfers between devices, shift(): lax.ppermute(values, 'outpair', odd)  5.33 us
    ppermute x2, waiting for transfers between devices, sum_part(): lax.ppermute(times(away, live, aligned, LONG if p else SHORT), 'inpair',...  3.19 us
  transfers between devices with their start and end apart: 29, of which 13 were waited for; matrix products, arithmetic and copies ran while one was open for 2% of the time, Pallas kernels for 6%

profile of v5, /device:TPU:0, one launch (start us, length us, event | category | flops | bytes accessed | tf_op | source)
XLA Modules:
  0.0 103.5 jit_solution(10740126577594661366)
XLA Ops:
  0.0 1.2 %copy-done = bf16[1,512,1024]{2,1,0:T(8,128)(2,1)S(1)} copy-done((bf16[1,512,1024]{2,1,0:T(8,128)(2,1)S(1)}, bf16[1,512,1024]{2,1,0:T(8,128)(2,1)}, u32[]{:S(2)}) %copy-start) | copy-done | bytes 1048600
  1.2 3.0 %collective-permute-start = (bf16[4,16,1024]{2,1,0:T(8,128)(2,1)S(1)}, bf16[4,16,1024]{2,1,0:T(8,128)(2,1)S(1)}, u32[]{:S(2)}, u32[]{:S(2)}) collective-permute-start(bf16[4,16,1024]{2,1,0:T(8,128)(2,1)S(1)} %dynamic-slice_bitcast_fusion.2), channel_id=1, source_target_pairs={{0,1},{1,0},{2,3},{3,2},{4,5},{5,4},{6,7},{7,6},{8,9},{9,8},{10,11... | collective-permute-start | bytes 393224 | tf_op jit(solution)/shard_map/ppermute | solution.py:307
  4.4 0.6 fusion.2
  6.3 0.6 convert_element_type.46
  6.9 0.9 collective-permute-done.refs_3_
  7.7 1.7 %collective-permute-start.10 = (bf16[4,16,1024]{2,1,0:T(8,128)(2,1)S(1)}, bf16[4,16,1024]{2,1,0:T(8,128)(2,1)S(1)}, u32[]{:S(2)}, u32[]{:S(2)}) collective-permute-start(bf16[4,16,1024]{2,1,0:T(8,128)(2,1)S(1)} %get-tuple-element.37), channel_id=1, source_target_pairs={{0,1},{1,0},{2,3},{3,2},{4,5},{5,4},{6,7},{7,6},{8,9},{9,8},{10,11... | collective-permute-start | bytes 393224 | tf_op jit(solution)/shard_map/ppermute | solution.py:307
  9.6 1.6 %collective-permute-start.3 = (bf16[2,4,16,1024]{3,2,1,0:T(8,128)(2,1)S(1)}, bf16[2,4,16,1024]{3,2,1,0:T(8,128)(2,1)S(1)}, u32[]{:S(2)}, u32[]{:S(2)}) collective-permute-start(bf16[2,4,16,1024]{3,2,1,0:T(8,128)(2,1)S(1)} %begin.2.refs_2_), channel_id=1, source_target_pairs={{0,2},{1,3},{2,0},{3,1},{4,6},{5,7},{6,4},{7,5},{8,10},{9,11},{10,... | collective-permute-start | bytes 786440 | tf_op jit(solution)/shard_map/ppermute | solution.py:310
  11.2 0.7 collective-permute-start.2
  11.9 0.6 collective-permute-start.1
  12.5 0.5 collective-permute-done.10.refs_3_
  13.0 3.9 %collective-permute-start.12 = (bf16[2,4,16,1024]{3,2,1,0:T(8,128)(2,1)S(1)}, bf16[2,4,16,1024]{3,2,1,0:T(8,128)(2,1)S(1)}, u32[]{:S(2)}, u32[]{:S(2)}) collective-permute-start(bf16[2,4,16,1024]{3,2,1,0:T(8,128)(2,1)S(1)} %begin.3.refs_2_), channel_id=1, source_target_pairs={{0,2},{1,3},{2,0},{3,1},{4,6},{5,7},{6,4},{7,5},{8,10},{9,11},{10,... | collective-permute-start | bytes 786440 | tf_op jit(solution)/shard_map/ppermute | solution.py:310
  17.0 0.7 collective-permute-start.11
  17.7 0.9 collective-permute-done.1
  18.7 4.5 %collective-permute-start.5 = (bf16[2,4,16,1024]{3,2,1,0:T(8,128)(2,1)S(1)}, bf16[2,4,16,1024]{3,2,1,0:T(8,128)(2,1)S(1)}, u32[]{:S(2)}, u32[]{:S(2)}) collective-permute-start(bf16[2,4,16,1024]{3,2,1,0:T(8,128)(2,1)S(1)} %step_on.8.refs_2_.refs_3_), channel_id=1, source_target_pairs={{0,2},{1,3},{2,0},{3,1},{4,6},{5,7},{6,4},{7,5},{8,10},{9,11},{10,... | collective-permute-start | bytes 786440 | tf_op jit(solution)/shard_map/ppermute | solution.py:310
  23.1 0.7 collective-permute-start.4
  23.9 4.7 %collective-permute-start.14 = (bf16[2,4,16,1024]{3,2,1,0:T(8,128)(2,1)S(1)}, bf16[2,4,16,1024]{3,2,1,0:T(8,128)(2,1)S(1)}, u32[]{:S(2)}, u32[]{:S(2)}) collective-permute-start(bf16[2,4,16,1024]{3,2,1,0:T(8,128)(2,1)S(1)} %step_on.12.refs_2_.refs_3_), channel_id=1, source_target_pairs={{0,2},{1,3},{2,0},{3,1},{4,6},{5,7},{6,4},{7,5},{8,10},{9,11},{10,... | collective-permute-start | bytes 786440 | tf_op jit(solution)/shard_map/ppermute | solution.py:310
  28.6 0.7 collective-permute-start.13
  29.3 0.1 collective-permute-done.5.refs_5_
  29.4 5.4 %collective-permute-start.7 = (bf16[2,4,16,1024]{3,2,1,0:T(8,128)(2,1)S(1)}, bf16[2,4,16,1024]{3,2,1,0:T(8,128)(2,1)S(1)}, u32[]{:S(2)}, u32[]{:S(2)}) collective-permute-start(bf16[2,4,16,1024]{3,2,1,0:T(8,128)(2,1)S(1)} %step_on.9.refs_3_.refs_4_), channel_id=1, source_target_pairs={{0,2},{1,3},{2,0},{3,1},{4,6},{5,7},{6,4},{7,5},{8,10},{9,11},{10,... | collective-permute-start | bytes 786440 | tf_op jit(solution)/shard_map/ppermute | solution.py:310
  34.9 0.7 collective-permute-start.6
  35.5 0.2 collective-permute-done.14.refs_5_
  35.8 4.7 %collective-permute-start.16 = (bf16[2,4,16,1024]{3,2,1,0:T(8,128)(2,1)S(1)}, bf16[2,4,16,1024]{3,2,1,0:T(8,128)(2,1)S(1)}, u32[]{:S(2)}, u32[]{:S(2)}) collective-permute-start(bf16[2,4,16,1024]{3,2,1,0:T(8,128)(2,1)S(1)} %step_on.13.refs_3_.refs_4_), channel_id=1, source_target_pairs={{0,2},{1,3},{2,0},{3,1},{4,6},{5,7},{6,4},{7,5},{8,10},{9,11},{10,... | collective-permute-start | bytes 786440 | tf_op jit(solution)/shard_map/ppermute | solution.py:310
  40.5 0.7 collective-permute-start.15
  41.2 0.6 collective-permute-done.7.refs_5_
  41.8 4.3 %collective-permute-start.9 = (bf16[2,4,16,1024]{3,2,1,0:T(8,128)(2,1)S(1)}, bf16[2,4,16,1024]{3,2,1,0:T(8,128)(2,1)S(1)}, u32[]{:S(2)}, u32[]{:S(2)}) collective-permute-start(bf16[2,4,16,1024]{3,2,1,0:T(8,128)(2,1)S(1)} %step_on.10.refs_4_.refs_5_), channel_id=1, source_target_pairs={{0,2},{1,3},{2,0},{3,1},{4,6},{5,7},{6,4},{7,5},{8,10},{9,11},{10,... | collective-permute-start | bytes 786440 | tf_op jit(solution)/shard_map/ppermute | solution.py:310
  46.1 0.7 collective-permute-start.8
  46.8 0.1 choose.6
  46.9 0.5 collective-permute-start.21
  47.4 0.1 choose.7
  47.5 1.7 %collective-permute-start.22 = (bf16[2,4,16,1024]{3,2,1,0:T(8,128)(2,1)S(1)}, bf16[2,4,16,1024]{3,2,1,0:T(8,128)(2,1)S(1)}, u32[]{:S(2)}, u32[]{:S(2)}) collective-permute-start(bf16[2,4,16,1024]{3,2,1,0:T(8,128)(2,1)S(1)} %choose.7), channel_id=1, source_target_pairs={{0,1},{1,0},{2,3},{3,2},{4,5},{5,4},{6,7},{7,6},{8,9},{9,8},{10,11... | collective-permute-start | bytes 786440 | tf_op jit(solution)/shard_map/ppermute | solution.py:307
  49.2 0.1 broadcast_bitcast_fusion
  49.3 0.1 bitcast_multiply_fusion.w_ref
  49.4 4.0 %collective-permute-start.18 = (bf16[2,4,16,1024]{3,2,1,0:T(8,128)(2,1)S(1)}, bf16[2,4,16,1024]{3,2,1,0:T(8,128)(2,1)S(1)}, u32[]{:S(2)}, u32[]{:S(2)}) collective-permute-start(bf16[2,4,16,1024]{3,2,1,0:T(8,128)(2,1)S(1)} %step_on.14.refs_4_.refs_5_), channel_id=1, source_target_pairs={{0,2},{1,3},{2,0},{3,1},{4,6},{5,7},{6,4},{7,5},{8,10},{9,11},{10,... | collective-permute-start | bytes 786440 | tf_op jit(solution)/shard_map/ppermute | solution.py:310
  53.4 0.7 collective-permute-start.17
  54.2 0.1 choose.4
  54.3 0.8 collective-permute-start.19
  55.1 3.8 %collective-permute-done.22 = bf16[2,4,16,1024]{3,2,1,0:T(8,128)(2,1)S(1)} collective-permute-done((bf16[2,4,16,1024]{3,2,1,0:T(8,128)(2,1)S(1)}, bf16[2,4,16,1024]{3,2,1,0:T(8,128)(2,1)S(1)}, u32[]{:S(2)}, u32[]{:S(2)}) %collective-permute-start.22) | collective-permute-done | bytes 262176 | tf_op jit(solution)/shard_map/ppermute | solution.py:307
  59.0 0.1 pad_maximum_fusion
  59.1 0.1 constant_dynamic-slice_fusion.2
  59.2 0.7 times.5
  60.1 0.1 choose.5
  60.2 0.5 collective-permute-start.20
  60.6 0.7 times.4
  61.4 1.3 %collective-permute-done.23 = f32[256,1024]{1,0:T(8,128)S(1)} collective-permute-done((f32[256,1024]{1,0:T(8,128)S(1)}, f32[256,1024]{1,0:T(8,128)S(1)}, u32[]{:S(2)}, u32[]{:S(2)}) %collective-permute-start.23) | collective-permute-done | bytes 1048608 | tf_op jit(solution)/shard_map/ppermute | solution.py:364
  62.6 0.2 settle.2
  62.9 1.6 %collective-permute-start.26 = (s16[144,1024]{1,0:T(8,128)(2,1)S(1)}, s16[144,1024]{1,0:T(8,128)(2,1)S(1)}, u32[]{:S(2)}, u32[]{:S(2)}) collective-permute-start(s16[144,1024]{1,0:T(8,128)(2,1)S(1)} %get-tuple-element.40), channel_id=1, source_target_pairs={{0,16},{8,24},{16,0},{24,8},{1,17},{9,25},{17,1},{25,9},{2,18},{10... | collective-permute-start | bytes 884744 | tf_op jit(solution)/shard_map/ppermute | solution.py:370
  64.5 4.5 %collective-permute-done.20 = bf16[2,4,16,1024]{3,2,1,0:T(8,128)(2,1)S(1)} collective-permute-done((bf16[2,4,16,1024]{3,2,1,0:T(8,128)(2,1)S(1)}, bf16[2,4,16,1024]{3,2,1,0:T(8,128)(2,1)S(1)}, u32[]{:S(2)}, u32[]{:S(2)}) %collective-permute-start.20) | collective-permute-done | bytes 262176 | tf_op jit(solution)/shard_map/ppermute | solution.py:307
  68.9 0.1 maximum_bitcast_fusion.2
  69.0 0.1 pad_maximum_fusion.1
  69.1 0.1 constant_dynamic-slice_fusion
  69.2 0.7 times.7
  70.0 0.7 times.6
  70.8 1.9 %collective-permute-done.24 = f32[256,1024]{1,0:T(8,128)S(1)} collective-permute-done((f32[256,1024]{1,0:T(8,128)S(1)}, f32[256,1024]{1,0:T(8,128)S(1)}, u32[]{:S(2)}, u32[]{:S(2)}) %collective-permute-start.24) | collective-permute-done | bytes 1048608 | tf_op jit(solution)/shard_map/ppermute | solution.py:364
  72.7 0.2 settle.3
  72.9 0.9 merge.3
  73.9 4.5 %all-to-all-start.1 = ((s16[8,144,128]{2,1,0:T(8,128)(2,1)}), s16[8,144,128]{2,1,0:T(8,128)(2,1)S(1)}, u32[]{:S(2)}, u32[]{:S(2)}) async-start(s16[8,144,128]{2,1,0:T(8,128)(2,1)} %get-tuple-element.52), calls=%async_computation.1 | async-start | bytes 589824 | tf_op jit(solution)/shard_map/all_to_all | solution.py:430
  78.4 1.5 %collective-permute-start.25 = (s16[144,1024]{1,0:T(8,128)(2,1)S(1)}, s16[144,1024]{1,0:T(8,128)(2,1)S(1)}, u32[]{:S(2)}, u32[]{:S(2)}) collective-permute-start(s16[144,1024]{1,0:T(8,128)(2,1)S(1)} %get-tuple-element.46), channel_id=1, source_target_pairs={{0,16},{8,24},{16,0},{24,8},{1,17},{9,25},{17,1},{25,9},{2,18},{10... | collective-permute-start | bytes 884744 | tf_op jit(solution)/shard_map/ppermute | solution.py:370
  79.9 7.2 %collective-permute-done.25.coded_ref = s16[144,1024]{1,0:T(8,128)(2,1)S(1)} collective-permute-done((s16[144,1024]{1,0:T(8,128)(2,1)S(1)}, s16[144,1024]{1,0:T(8,128)(2,1)S(1)}, u32[]{:S(2)}, u32[]{:S(2)}) %collective-permute-start.25) | collective-permute-done | bytes 294944 | tf_op jit(solution)/shard_map/ppermute | solution.py:370
  87.2 0.9 merge.2
  88.1 0.2 all-to-all-done.1.refs_1_
  88.3 5.5 %all-to-all-start = ((s16[8,144,128]{2,1,0:T(8,128)(2,1)}), s16[8,144,128]{2,1,0:T(8,128)(2,1)S(1)}, u32[]{:S(2)}, u32[]{:S(2)}) async-start(s16[8,144,128]{2,1,0:T(8,128)(2,1)} %get-tuple-element.48), calls=%async_computation | async-start | bytes 589824 | tf_op jit(solution)/shard_map/all_to_all | solution.py:430
  93.8 1.2 %finish.2.refs_5_ = f32[2,2,2,32,1024]{4,3,2,1,0:T(8,128)} custom-call(f32[128,1024]{1,0:T(8,128)S(1)} %get-tuple-element.51.refs_0_, s16[8,144,128]{2,1,0:T(8,128)(2,1)S(1)} %all-to-all-done.1.refs_1_, s32[1,128]{1,0:T(1,128)S(1)} %bitcast.78, f32[1,1024]{1,0:T(1,128)S(1)} %bitcast.76, f32[2,128]{1,0:T(2,128)S(1)} %copy-done.2), custom_call_target="tpu_custom_call" | custom-call | flops 20000000000 | tf_op jit(solution)/shard_map/finish/pallas_call | solution.py:275
  95.0 7.3 %all-to-all-done.refs_1_ = s16[8,144,128]{2,1,0:T(8,128)(2,1)S(1)} async-done(((s16[8,144,128]{2,1,0:T(8,128)(2,1)}), s16[8,144,128]{2,1,0:T(8,128)(2,1)S(1)}, u32[]{:S(2)}, u32[]{:S(2)}) %all-to-all-start) | async-done | bytes 294944 | tf_op jit(solution)/shard_map/all_to_all | solution.py:430
  102.3 1.1 %finish.3 = f32[2,2,2,32,1024]{4,3,2,1,0:T(8,128)} custom-call(f32[128,1024]{1,0:T(8,128)S(1)} %get-tuple-element.47.refs_0_, s16[8,144,128]{2,1,0:T(8,128)(2,1)S(1)} %all-to-all-done.refs_1_, s32[1,128]{1,0:T(1,128)S(1)} %bitcast.79, f32[1,1024]{1,0:T(1,128)S(1)} %bitcast.77, f32[2,128]{1,0:T(2,128)S(1)} %copy-done.2, ...), custom_call_target="tpu_custom_call", output_to_operand_aliasing={{}: (5, {})} | custom-call | flops 20000000000 | tf_op jit(solution)/shard_map/finish/pallas_call | solution.py:275
  (53 shorter events, 1.0 us)
Async XLA Ops:
  0.0 1.2 %copy-start = (bf16[1,512,1024]{2,1,0:T(8,128)(2,1)S(1)}, bf16[1,512,1024]{2,1,0:T(8,128)(2,1)}, u32[]{:S(2)}) copy-start(bf16[1,512,1024]{2,1,0:T(8,128)(2,1)} %param.8) | copy-start | bytes 3145732
  0.0 4.4 %copy-start.7 = (s32[2]{0:T(128)S(1)}, s32[2]{0:T(128)}, u32[]{:S(2)}) copy-start(s32[2]{0:T(128)} %param.10) | copy-start | bytes 28
  0.0 6.2 %copy-start.6 = (s32[4,4]{1,0:T(4,128)S(1)}, s32[4,4]{1,0:T(4,128)}, u32[]{:S(2)}) copy-start(s32[4,4]{1,0:T(4,128)} %param.9) | copy-start | bytes 196
  1.2 6.5 %collective-permute-start = (bf16[4,16,1024]{2,1,0:T(8,128)(2,1)S(1)}, bf16[4,16,1024]{2,1,0:T(8,128)(2,1)S(1)}, u32[]{:S(2)}, u32[]{:S(2)}) collective-permute-start(bf16[4,16,1024]{2,1,0:T(8,128)(2,1)S(1)} %dynamic-slice_bitcast_fusion.2), channel_id=1, source_target_pairs={{0,1},{1,0},{2,3},{3,2},{4,5},{5,4},{6,7},{7,6},{8,9},{9,8},{10,11... | collective-permute-start | bytes 393224 | tf_op jit(solution)/shard_map/ppermute | solution.py:307
  7.7 5.3 %collective-permute-start.10 = (bf16[4,16,1024]{2,1,0:T(8,128)(2,1)S(1)}, bf16[4,16,1024]{2,1,0:T(8,128)(2,1)S(1)}, u32[]{:S(2)}, u32[]{:S(2)}) collective-permute-start(bf16[4,16,1024]{2,1,0:T(8,128)(2,1)S(1)} %get-tuple-element.37), channel_id=1, source_target_pairs={{0,1},{1,0},{2,3},{3,2},{4,5},{5,4},{6,7},{7,6},{8,9},{9,8},{10,11... | collective-permute-start | bytes 393224 | tf_op jit(solution)/shard_map/ppermute | solution.py:307
  9.6 9.0 %collective-permute-start.3 = (bf16[2,4,16,1024]{3,2,1,0:T(8,128)(2,1)S(1)}, bf16[2,4,16,1024]{3,2,1,0:T(8,128)(2,1)S(1)}, u32[]{:S(2)}, u32[]{:S(2)}) collective-permute-start(bf16[2,4,16,1024]{3,2,1,0:T(8,128)(2,1)S(1)} %begin.2.refs_2_), channel_id=1, source_target_pairs={{0,2},{1,3},{2,0},{3,1},{4,6},{5,7},{6,4},{7,5},{8,10},{9,11},{10,... | collective-permute-start | bytes 786440 | tf_op jit(solution)/shard_map/ppermute | solution.py:310
  11.2 7.4 %collective-permute-start.2 = (bf16[2,4,16,1024]{3,2,1,0:T(8,128)(2,1)S(1)}, bf16[2,4,16,1024]{3,2,1,0:T(8,128)(2,1)S(1)}, u32[]{:S(2)}, u32[]{:S(2)}) collective-permute-start(bf16[2,4,16,1024]{3,2,1,0:T(8,128)(2,1)S(1)} %begin.2.refs_2_), channel_id=1, source_target_pairs={{2,4},{3,5},{4,2},{5,3},{10,12},{11,13},{12,10},{13,11},{18,20},{1... | collective-permute-start | bytes 786440 | tf_op jit(solution)/shard_map/ppermute | solution.py:310
  11.9 6.7 %collective-permute-start.1 = (bf16[2,4,16,1024]{3,2,1,0:T(8,128)(2,1)S(1)}, bf16[2,4,16,1024]{3,2,1,0:T(8,128)(2,1)S(1)}, u32[]{:S(2)}, u32[]{:S(2)}) collective-permute-start(bf16[2,4,16,1024]{3,2,1,0:T(8,128)(2,1)S(1)} %pad_maximum_fusion.2), channel_id=1, source_target_pairs={{0,1},{1,0},{2,3},{3,2},{4,5},{5,4},{6,7},{7,6},{8,9},{9,8},{10,11... | collective-permute-start | bytes 786440 | tf_op jit(solution)/shard_map/ppermute | solution.py:307
  13.0 10.8 %collective-permute-start.12 = (bf16[2,4,16,1024]{3,2,1,0:T(8,128)(2,1)S(1)}, bf16[2,4,16,1024]{3,2,1,0:T(8,128)(2,1)S(1)}, u32[]{:S(2)}, u32[]{:S(2)}) collective-permute-start(bf16[2,4,16,1024]{3,2,1,0:T(8,128)(2,1)S(1)} %begin.3.refs_2_), channel_id=1, source_target_pairs={{0,2},{1,3},{2,0},{3,1},{4,6},{5,7},{6,4},{7,5},{8,10},{9,11},{10,... | collective-permute-start | bytes 786440 | tf_op jit(solution)/shard_map/ppermute | solution.py:310
  17.0 6.8 %collective-permute-start.11 = (bf16[2,4,16,1024]{3,2,1,0:T(8,128)(2,1)S(1)}, bf16[2,4,16,1024]{3,2,1,0:T(8,128)(2,1)S(1)}, u32[]{:S(2)}, u32[]{:S(2)}) collective-permute-start(bf16[2,4,16,1024]{3,2,1,0:T(8,128)(2,1)S(1)} %begin.3.refs_2_), channel_id=1, source_target_pairs={{2,4},{3,5},{4,2},{5,3},{10,12},{11,13},{12,10},{13,11},{18,20},{1... | collective-permute-start | bytes 786440 | tf_op jit(solution)/shard_map/ppermute | solution.py:310
  18.7 10.7 %collective-permute-start.5 = (bf16[2,4,16,1024]{3,2,1,0:T(8,128)(2,1)S(1)}, bf16[2,4,16,1024]{3,2,1,0:T(8,128)(2,1)S(1)}, u32[]{:S(2)}, u32[]{:S(2)}) collective-permute-start(bf16[2,4,16,1024]{3,2,1,0:T(8,128)(2,1)S(1)} %step_on.8.refs_2_.refs_3_), channel_id=1, source_target_pairs={{0,2},{1,3},{2,0},{3,1},{4,6},{5,7},{6,4},{7,5},{8,10},{9,11},{10,... | collective-permute-start | bytes 786440 | tf_op jit(solution)/shard_map/ppermute | solution.py:310
  23.1 6.2 %collective-permute-start.4 = (bf16[2,4,16,1024]{3,2,1,0:T(8,128)(2,1)S(1)}, bf16[2,4,16,1024]{3,2,1,0:T(8,128)(2,1)S(1)}, u32[]{:S(2)}, u32[]{:S(2)}) collective-permute-start(bf16[2,4,16,1024]{3,2,1,0:T(8,128)(2,1)S(1)} %step_on.8.refs_2_.refs_3_), channel_id=1, source_target_pairs={{2,4},{3,5},{4,2},{5,3},{10,12},{11,13},{12,10},{13,11},{18,20},{1... | collective-permute-start | bytes 786440 | tf_op jit(solution)/shard_map/ppermute | solution.py:310
  23.9 11.8 %collective-permute-start.14 = (bf16[2,4,16,1024]{3,2,1,0:T(8,128)(2,1)S(1)}, bf16[2,4,16,1024]{3,2,1,0:T(8,128)(2,1)S(1)}, u32[]{:S(2)}, u32[]{:S(2)}) collective-permute-start(bf16[2,4,16,1024]{3,2,1,0:T(8,128)(2,1)S(1)} %step_on.12.refs_2_.refs_3_), channel_id=1, source_target_pairs={{0,2},{1,3},{2,0},{3,1},{4,6},{5,7},{6,4},{7,5},{8,10},{9,11},{10,... | collective-permute-start | bytes 786440 | tf_op jit(solution)/shard_map/ppermute | solution.py:310
  28.6 7.1 %collective-permute-start.13 = (bf16[2,4,16,1024]{3,2,1,0:T(8,128)(2,1)S(1)}, bf16[2,4,16,1024]{3,2,1,0:T(8,128)(2,1)S(1)}, u32[]{:S(2)}, u32[]{:S(2)}) collective-permute-start(bf16[2,4,16,1024]{3,2,1,0:T(8,128)(2,1)S(1)} %step_on.12.refs_2_.refs_3_), channel_id=1, source_target_pairs={{2,4},{3,5},{4,2},{5,3},{10,12},{11,13},{12,10},{13,11},{18,20},{1... | collective-permute-start | bytes 786440 | tf_op jit(solution)/shard_map/ppermute | solution.py:310
  29.4 12.3 %collective-permute-start.7 = (bf16[2,4,16,1024]{3,2,1,0:T(8,128)(2,1)S(1)}, bf16[2,4,16,1024]{3,2,1,0:T(8,128)(2,1)S(1)}, u32[]{:S(2)}, u32[]{:S(2)}) collective-permute-start(bf16[2,4,16,1024]{3,2,1,0:T(8,128)(2,1)S(1)} %step_on.9.refs_3_.refs_4_), channel_id=1, source_target_pairs={{0,2},{1,3},{2,0},{3,1},{4,6},{5,7},{6,4},{7,5},{8,10},{9,11},{10,... | collective-permute-start | bytes 786440 | tf_op jit(solution)/shard_map/ppermute | solution.py:310
  34.9 6.9 %collective-permute-start.6 = (bf16[2,4,16,1024]{3,2,1,0:T(8,128)(2,1)S(1)}, bf16[2,4,16,1024]{3,2,1,0:T(8,128)(2,1)S(1)}, u32[]{:S(2)}, u32[]{:S(2)}) collective-permute-start(bf16[2,4,16,1024]{3,2,1,0:T(8,128)(2,1)S(1)} %step_on.9.refs_3_.refs_4_), channel_id=1, source_target_pairs={{2,4},{3,5},{4,2},{5,3},{10,12},{11,13},{12,10},{13,11},{18,20},{1... | collective-permute-start | bytes 786440 | tf_op jit(solution)/shard_map/ppermute | solution.py:310
  35.8 11.6 %collective-permute-start.16 = (bf16[2,4,16,1024]{3,2,1,0:T(8,128)(2,1)S(1)}, bf16[2,4,16,1024]{3,2,1,0:T(8,128)(2,1)S(1)}, u32[]{:S(2)}, u32[]{:S(2)}) collective-permute-start(bf16[2,4,16,1024]{3,2,1,0:T(8,128)(2,1)S(1)} %step_on.13.refs_3_.refs_4_), channel_id=1, source_target_pairs={{0,2},{1,3},{2,0},{3,1},{4,6},{5,7},{6,4},{7,5},{8,10},{9,11},{10,... | collective-permute-start | bytes 786440 | tf_op jit(solution)/shard_map/ppermute | solution.py:310
  40.5 6.9 %collective-permute-start.15 = (bf16[2,4,16,1024]{3,2,1,0:T(8,128)(2,1)S(1)}, bf16[2,4,16,1024]{3,2,1,0:T(8,128)(2,1)S(1)}, u32[]{:S(2)}, u32[]{:S(2)}) collective-permute-start(bf16[2,4,16,1024]{3,2,1,0:T(8,128)(2,1)S(1)} %step_on.13.refs_3_.refs_4_), channel_id=1, source_target_pairs={{2,4},{3,5},{4,2},{5,3},{10,12},{11,13},{12,10},{13,11},{18,20},{1... | collective-permute-start | bytes 786440 | tf_op jit(solution)/shard_map/ppermute | solution.py:310
  41.8 11.6 %collective-permute-start.9 = (bf16[2,4,16,1024]{3,2,1,0:T(8,128)(2,1)S(1)}, bf16[2,4,16,1024]{3,2,1,0:T(8,128)(2,1)S(1)}, u32[]{:S(2)}, u32[]{:S(2)}) collective-permute-start(bf16[2,4,16,1024]{3,2,1,0:T(8,128)(2,1)S(1)} %step_on.10.refs_4_.refs_5_), channel_id=1, source_target_pairs={{0,2},{1,3},{2,0},{3,1},{4,6},{5,7},{6,4},{7,5},{8,10},{9,11},{10,... | collective-permute-start | bytes 786440 | tf_op jit(solution)/shard_map/ppermute | solution.py:310
  46.1 8.0 %collective-permute-start.8 = (bf16[2,4,16,1024]{3,2,1,0:T(8,128)(2,1)S(1)}, bf16[2,4,16,1024]{3,2,1,0:T(8,128)(2,1)S(1)}, u32[]{:S(2)}, u32[]{:S(2)}) collective-permute-start(bf16[2,4,16,1024]{3,2,1,0:T(8,128)(2,1)S(1)} %step_on.10.refs_4_.refs_5_), channel_id=1, source_target_pairs={{2,4},{3,5},{4,2},{5,3},{10,12},{11,13},{12,10},{13,11},{18,20},{1... | collective-permute-start | bytes 786440 | tf_op jit(solution)/shard_map/ppermute | solution.py:310
  46.9 2.3 %copy-start.5 = (bf16[4,4]{1,0:T(4,128)(2,1)S(1)}, bf16[4,4]{1,0:T(4,128)(2,1)}, u32[]{:S(2)}) copy-start(bf16[4,4]{1,0:T(4,128)(2,1)} %convert_element_type.46) | copy-start | bytes 100
  46.9 8.2 %collective-permute-start.21 = (bf16[2,4,16,1024]{3,2,1,0:T(8,128)(2,1)S(1)}, bf16[2,4,16,1024]{3,2,1,0:T(8,128)(2,1)S(1)}, u32[]{:S(2)}, u32[]{:S(2)}) collective-permute-start(bf16[2,4,16,1024]{3,2,1,0:T(8,128)(2,1)S(1)} %choose.6), channel_id=1, source_target_pairs={{0,1},{1,0},{2,3},{3,2},{4,5},{5,4},{6,7},{7,6},{8,9},{9,8},{10,11... | collective-permute-start | bytes 786440 | tf_op jit(solution)/shard_map/ppermute | solution.py:307
  47.4 1.9 %copy-start.4 = (bf16[1024,1024]{1,0:T(8,128)(2,1)S(1)}, bf16[1024,1024]{1,0:T(8,128)(2,1)}, u32[]{:S(2)}) copy-start(bf16[1024,1024]{1,0:T(8,128)(2,1)} %param.7) | copy-start | bytes 6291460
  47.5 11.4 %collective-permute-start.22 = (bf16[2,4,16,1024]{3,2,1,0:T(8,128)(2,1)S(1)}, bf16[2,4,16,1024]{3,2,1,0:T(8,128)(2,1)S(1)}, u32[]{:S(2)}, u32[]{:S(2)}) collective-permute-start(bf16[2,4,16,1024]{3,2,1,0:T(8,128)(2,1)S(1)} %choose.7), channel_id=1, source_target_pairs={{0,1},{1,0},{2,3},{3,2},{4,5},{5,4},{6,7},{7,6},{8,9},{9,8},{10,11... | collective-permute-start | bytes 786440 | tf_op jit(solution)/shard_map/ppermute | solution.py:307
  49.4 10.5 %collective-permute-start.18 = (bf16[2,4,16,1024]{3,2,1,0:T(8,128)(2,1)S(1)}, bf16[2,4,16,1024]{3,2,1,0:T(8,128)(2,1)S(1)}, u32[]{:S(2)}, u32[]{:S(2)}) collective-permute-start(bf16[2,4,16,1024]{3,2,1,0:T(8,128)(2,1)S(1)} %step_on.14.refs_4_.refs_5_), channel_id=1, source_target_pairs={{0,2},{1,3},{2,0},{3,1},{4,6},{5,7},{6,4},{7,5},{8,10},{9,11},{10,... | collective-permute-start | bytes 786440 | tf_op jit(solution)/shard_map/ppermute | solution.py:310
  53.4 6.6 %collective-permute-start.17 = (bf16[2,4,16,1024]{3,2,1,0:T(8,128)(2,1)S(1)}, bf16[2,4,16,1024]{3,2,1,0:T(8,128)(2,1)S(1)}, u32[]{:S(2)}, u32[]{:S(2)}) collective-permute-start(bf16[2,4,16,1024]{3,2,1,0:T(8,128)(2,1)S(1)} %step_on.14.refs_4_.refs_5_), channel_id=1, source_target_pairs={{2,4},{3,5},{4,2},{5,3},{10,12},{11,13},{12,10},{13,11},{18,20},{1... | collective-permute-start | bytes 786440 | tf_op jit(solution)/shard_map/ppermute | solution.py:310
  54.3 10.1 %collective-permute-start.19 = (bf16[2,4,16,1024]{3,2,1,0:T(8,128)(2,1)S(1)}, bf16[2,4,16,1024]{3,2,1,0:T(8,128)(2,1)S(1)}, u32[]{:S(2)}, u32[]{:S(2)}) collective-permute-start(bf16[2,4,16,1024]{3,2,1,0:T(8,128)(2,1)S(1)} %choose.4), channel_id=1, source_target_pairs={{0,1},{1,0},{2,3},{3,2},{4,5},{5,4},{6,7},{7,6},{8,9},{9,8},{10,11... | collective-permute-start | bytes 786440 | tf_op jit(solution)/shard_map/ppermute | solution.py:307
  59.9 2.7 %collective-permute-start.23 = (f32[256,1024]{1,0:T(8,128)S(1)}, f32[256,1024]{1,0:T(8,128)S(1)}, u32[]{:S(2)}, u32[]{:S(2)}) collective-permute-start(f32[256,1024]{1,0:T(8,128)S(1)} %times.5), channel_id=1, source_target_pairs={{0,8},{8,0},{16,24},{24,16},{1,9},{9,1},{17,25},{25,17},{2,10},{10... | collective-permute-start | bytes 3145736 | tf_op jit(solution)/shard_map/ppermute | solution.py:364
  60.2 8.7 %collective-permute-start.20 = (bf16[2,4,16,1024]{3,2,1,0:T(8,128)(2,1)S(1)}, bf16[2,4,16,1024]{3,2,1,0:T(8,128)(2,1)S(1)}, u32[]{:S(2)}, u32[]{:S(2)}) collective-permute-start(bf16[2,4,16,1024]{3,2,1,0:T(8,128)(2,1)S(1)} %choose.5), channel_id=1, source_target_pairs={{0,1},{1,0},{2,3},{3,2},{4,5},{5,4},{6,7},{7,6},{8,9},{9,8},{10,11... | collective-permute-start | bytes 786440 | tf_op jit(solution)/shard_map/ppermute | solution.py:307
  62.9 10.1 %collective-permute-start.26 = (s16[144,1024]{1,0:T(8,128)(2,1)S(1)}, s16[144,1024]{1,0:T(8,128)(2,1)S(1)}, u32[]{:S(2)}, u32[]{:S(2)}) collective-permute-start(s16[144,1024]{1,0:T(8,128)(2,1)S(1)} %get-tuple-element.40), channel_id=1, source_target_pairs={{0,16},{8,24},{16,0},{24,8},{1,17},{9,25},{17,1},{25,9},{2,18},{10... | collective-permute-start | bytes 884744 | tf_op jit(solution)/shard_map/ppermute | solution.py:370
  69.9 2.7 %collective-permute-start.24 = (f32[256,1024]{1,0:T(8,128)S(1)}, f32[256,1024]{1,0:T(8,128)S(1)}, u32[]{:S(2)}, u32[]{:S(2)}) collective-permute-start(f32[256,1024]{1,0:T(8,128)S(1)} %times.7), channel_id=1, source_target_pairs={{0,8},{8,0},{16,24},{24,16},{1,9},{9,1},{17,25},{25,17},{2,10},{10... | collective-permute-start | bytes 3145736 | tf_op jit(solution)/shard_map/ppermute | solution.py:364
  72.7 21.2 %copy-start.1 = (f32[1024]{0:T(1024)S(1)}, f32[1024]{0:T(1024)}, u32[]{:S(2)}) copy-start(f32[1024]{0:T(1024)} %param.12) | copy-start | bytes 12292
  72.7 21.2 %copy-start.2 = (f32[2,128]{1,0:T(2,128)S(1)}, f32[2,128]{1,0:T(2,128)}, u32[]{:S(2)}) copy-start(f32[2,128]{1,0:T(2,128)} %refs_4_.3) | copy-start | bytes 3076
  72.7 21.2 %copy-start.3 = (s32[128]{0:T(128)S(1)}, s32[128]{0:T(128)}, u32[]{:S(2)}) copy-start(s32[128]{0:T(128)} %param.13) | copy-start | bytes 1540
  73.9 14.4 %all-to-all-start.1 = ((s16[8,144,128]{2,1,0:T(8,128)(2,1)}), s16[8,144,128]{2,1,0:T(8,128)(2,1)S(1)}, u32[]{:S(2)}, u32[]{:S(2)}) async-start(s16[8,144,128]{2,1,0:T(8,128)(2,1)} %get-tuple-element.52), calls=%async_computation.1 | async-start | bytes 589824 | tf_op jit(solution)/shard_map/all_to_all | solution.py:430
  78.4 8.8 %collective-permute-start.25 = (s16[144,1024]{1,0:T(8,128)(2,1)S(1)}, s16[144,1024]{1,0:T(8,128)(2,1)S(1)}, u32[]{:S(2)}, u32[]{:S(2)}) collective-permute-start(s16[144,1024]{1,0:T(8,128)(2,1)S(1)} %get-tuple-element.46), channel_id=1, source_target_pairs={{0,16},{8,24},{16,0},{24,8},{1,17},{9,25},{17,1},{25,9},{2,18},{10... | collective-permute-start | bytes 884744 | tf_op jit(solution)/shard_map/ppermute | solution.py:370
  88.3 14.0 %all-to-all-start = ((s16[8,144,128]{2,1,0:T(8,128)(2,1)}), s16[8,144,128]{2,1,0:T(8,128)(2,1)S(1)}, u32[]{:S(2)}, u32[]{:S(2)}) async-start(s16[8,144,128]{2,1,0:T(8,128)(2,1)} %get-tuple-element.48), calls=%async_computation | async-start | bytes 589824 | tf_op jit(solution)/shard_map/all_to_all | solution.py:430

commit v6 on v5

--- a/solution.py
+++ b/solution.py
@@ -11,7 +11,7 @@
 OCTAVE = 128.0
 LANES = 128
 TILE_ROWS = 16
-WIDE = 4
+WIDE = 8
 VMEM = 8 * 1024 * 1024
 SHORT = pl.CostEstimate(flops=1_000_000, bytes_accessed=0, transcendentals=0)
 LONG = pl.CostEstimate(flops=20_000_000_000, bytes_accessed=0, transcendentals=0)

time: 104 us -> 104 us (level)
  no operation moved by 1% of the time
where the time goes in v6:
time: 104 us; the launch traced here: 103 us
  starting transfers between devices  60.5 us (58%)
  waiting for transfers between devices  29.7 us (29%)
  Pallas kernels  8.09 us (8%)
  local copies, waits for them, and re-layouts  2.27 us (2%)
  between operations  1.77 us (2%)
  other arithmetic  1.11 us (1%)
    ppermute x8, starting transfers between devices, shift(): lax.ppermute(values, 'outpair', even)  33.1 us
    ppermute x7, waiting for transfers between devices, swap_x(): return lax.ppermute(values, 'outpair', beside)  10.6 us
    all_to_all x2, starting transfers between devices, on_device(): lax.all_to_all(blocks, 'outpair', split_axis=0, concat_axis=0, tiled=True)  10.1 us
    ppermute x7, starting transfers between devices, swap_x(): return lax.ppermute(values, 'outpair', beside)  8.73 us
    all_to_all x2, waiting for transfers between devices, on_device(): lax.all_to_all(blocks, 'outpair', split_axis=0, concat_axis=0, tiled=True)  7.61 us
    ppermute x2, waiting for transfers between devices, sum_part(): coded[p] = lax.ppermute(sent[p], 'inpair', across(1))  7.25 us
    ppermute x8, starting transfers between devices, shift(): lax.ppermute(values, 'outpair', odd)  5.33 us
    ppermute x2, waiting for transfers between devices, sum_part(): lax.ppermute(times(away, live, aligned, LONG if p else SHORT), 'inpair',...  3.21 us
  transfers between devices with their start and end apart: 29, of which 13 were waited for; matrix products, arithmetic and copies ran while one was open for 2% of the time, Pallas kernels for 6%

profile of v6, /device:TPU:0, one launch (start us, length us, event | category | flops | bytes accessed | tf_op | source)
XLA Modules:
  0.0 103.4 jit_solution(15750399594931620021)
XLA Ops:
  0.0 1.2 %copy-done = bf16[1,512,1024]{2,1,0:T(8,128)(2,1)S(1)} copy-done((bf16[1,512,1024]{2,1,0:T(8,128)(2,1)S(1)}, bf16[1,512,1024]{2,1,0:T(8,128)(2,1)}, u32[]{:S(2)}) %copy-start) | copy-done | bytes 1048600
  1.2 3.0 %collective-permute-start = (bf16[4,16,1024]{2,1,0:T(8,128)(2,1)S(1)}, bf16[4,16,1024]{2,1,0:T(8,128)(2,1)S(1)}, u32[]{:S(2)}, u32[]{:S(2)}) collective-permute-start(bf16[4,16,1024]{2,1,0:T(8,128)(2,1)S(1)} %dynamic-slice_bitcast_fusion.2), channel_id=1, source_target_pairs={{0,1},{1,0},{2,3},{3,2},{4,5},{5,4},{6,7},{7,6},{8,9},{9,8},{10,11... | collective-permute-start | bytes 393224 | tf_op jit(solution)/shard_map/ppermute | solution.py:307
  4.4 0.6 fusion.2
  6.3 0.6 convert_element_type.46
  6.9 0.9 collective-permute-done.refs_3_
  7.7 1.7 %collective-permute-start.10 = (bf16[4,16,1024]{2,1,0:T(8,128)(2,1)S(1)}, bf16[4,16,1024]{2,1,0:T(8,128)(2,1)S(1)}, u32[]{:S(2)}, u32[]{:S(2)}) collective-permute-start(bf16[4,16,1024]{2,1,0:T(8,128)(2,1)S(1)} %get-tuple-element.37), channel_id=1, source_target_pairs={{0,1},{1,0},{2,3},{3,2},{4,5},{5,4},{6,7},{7,6},{8,9},{9,8},{10,11... | collective-permute-start | bytes 393224 | tf_op jit(solution)/shard_map/ppermute | solution.py:307
  9.6 1.6 %collective-permute-start.3 = (bf16[2,4,16,1024]{3,2,1,0:T(8,128)(2,1)S(1)}, bf16[2,4,16,1024]{3,2,1,0:T(8,128)(2,1)S(1)}, u32[]{:S(2)}, u32[]{:S(2)}) collective-permute-start(bf16[2,4,16,1024]{3,2,1,0:T(8,128)(2,1)S(1)} %begin.2.refs_2_), channel_id=1, source_target_pairs={{0,2},{1,3},{2,0},{3,1},{4,6},{5,7},{6,4},{7,5},{8,10},{9,11},{10,... | collective-permute-start | bytes 786440 | tf_op jit(solution)/shard_map/ppermute | solution.py:310
  11.2 0.7 collective-permute-start.2
  11.9 0.6 collective-permute-start.1
  12.5 0.5 collective-permute-done.10.refs_3_
  13.0 3.9 %collective-permute-start.12 = (bf16[2,4,16,1024]{3,2,1,0:T(8,128)(2,1)S(1)}, bf16[2,4,16,1024]{3,2,1,0:T(8,128)(2,1)S(1)}, u32[]{:S(2)}, u32[]{:S(2)}) collective-permute-start(bf16[2,4,16,1024]{3,2,1,0:T(8,128)(2,1)S(1)} %begin.3.refs_2_), channel_id=1, source_target_pairs={{0,2},{1,3},{2,0},{3,1},{4,6},{5,7},{6,4},{7,5},{8,10},{9,11},{10,... | collective-permute-start | bytes 786440 | tf_op jit(solution)/shard_map/ppermute | solution.py:310
  17.0 0.7 collective-permute-start.11
  17.6 0.9 collective-permute-done.1
  18.7 4.4 %collective-permute-start.5 = (bf16[2,4,16,1024]{3,2,1,0:T(8,128)(2,1)S(1)}, bf16[2,4,16,1024]{3,2,1,0:T(8,128)(2,1)S(1)}, u32[]{:S(2)}, u32[]{:S(2)}) collective-permute-start(bf16[2,4,16,1024]{3,2,1,0:T(8,128)(2,1)S(1)} %step_on.8.refs_2_.refs_3_), channel_id=1, source_target_pairs={{0,2},{1,3},{2,0},{3,1},{4,6},{5,7},{6,4},{7,5},{8,10},{9,11},{10,... | collective-permute-start | bytes 786440 | tf_op jit(solution)/shard_map/ppermute | solution.py:310
  23.1 0.7 collective-permute-start.4
  23.9 4.7 %collective-permute-start.14 = (bf16[2,4,16,1024]{3,2,1,0:T(8,128)(2,1)S(1)}, bf16[2,4,16,1024]{3,2,1,0:T(8,128)(2,1)S(1)}, u32[]{:S(2)}, u32[]{:S(2)}) collective-permute-start(bf16[2,4,16,1024]{3,2,1,0:T(8,128)(2,1)S(1)} %step_on.12.refs_2_.refs_3_), channel_id=1, source_target_pairs={{0,2},{1,3},{2,0},{3,1},{4,6},{5,7},{6,4},{7,5},{8,10},{9,11},{10,... | collective-permute-start | bytes 786440 | tf_op jit(solution)/shard_map/ppermute | solution.py:310
  28.6 0.7 collective-permute-start.13
  29.3 0.1 collective-permute-done.5.refs_5_
  29.5 5.4 %collective-permute-start.7 = (bf16[2,4,16,1024]{3,2,1,0:T(8,128)(2,1)S(1)}, bf16[2,4,16,1024]{3,2,1,0:T(8,128)(2,1)S(1)}, u32[]{:S(2)}, u32[]{:S(2)}) collective-permute-start(bf16[2,4,16,1024]{3,2,1,0:T(8,128)(2,1)S(1)} %step_on.9.refs_3_.refs_4_), channel_id=1, source_target_pairs={{0,2},{1,3},{2,0},{3,1},{4,6},{5,7},{6,4},{7,5},{8,10},{9,11},{10,... | collective-permute-start | bytes 786440 | tf_op jit(solution)/shard_map/ppermute | solution.py:310
  34.9 0.7 collective-permute-start.6
  35.5 0.2 collective-permute-done.14.refs_5_
  35.8 4.7 %collective-permute-start.16 = (bf16[2,4,16,1024]{3,2,1,0:T(8,128)(2,1)S(1)}, bf16[2,4,16,1024]{3,2,1,0:T(8,128)(2,1)S(1)}, u32[]{:S(2)}, u32[]{:S(2)}) collective-permute-start(bf16[2,4,16,1024]{3,2,1,0:T(8,128)(2,1)S(1)} %step_on.13.refs_3_.refs_4_), channel_id=1, source_target_pairs={{0,2},{1,3},{2,0},{3,1},{4,6},{5,7},{6,4},{7,5},{8,10},{9,11},{10,... | collective-permute-start | bytes 786440 | tf_op jit(solution)/shard_map/ppermute | solution.py:310
  40.5 0.7 collective-permute-start.15
  41.2 0.6 collective-permute-done.7.refs_5_
  41.8 4.3 %collective-permute-start.9 = (bf16[2,4,16,1024]{3,2,1,0:T(8,128)(2,1)S(1)}, bf16[2,4,16,1024]{3,2,1,0:T(8,128)(2,1)S(1)}, u32[]{:S(2)}, u32[]{:S(2)}) collective-permute-start(bf16[2,4,16,1024]{3,2,1,0:T(8,128)(2,1)S(1)} %step_on.10.refs_4_.refs_5_), channel_id=1, source_target_pairs={{0,2},{1,3},{2,0},{3,1},{4,6},{5,7},{6,4},{7,5},{8,10},{9,11},{10,... | collective-permute-start | bytes 786440 | tf_op jit(solution)/shard_map/ppermute | solution.py:310
  46.1 0.7 collective-permute-start.8
  46.8 0.1 choose.6
  46.9 0.5 collective-permute-start.21
  47.4 0.1 choose.7
  47.5 1.7 %collective-permute-start.22 = (bf16[2,4,16,1024]{3,2,1,0:T(8,128)(2,1)S(1)}, bf16[2,4,16,1024]{3,2,1,0:T(8,128)(2,1)S(1)}, u32[]{:S(2)}, u32[]{:S(2)}) collective-permute-start(bf16[2,4,16,1024]{3,2,1,0:T(8,128)(2,1)S(1)} %choose.7), channel_id=1, source_target_pairs={{0,1},{1,0},{2,3},{3,2},{4,5},{5,4},{6,7},{7,6},{8,9},{9,8},{10,11... | collective-permute-start | bytes 786440 | tf_op jit(solution)/shard_map/ppermute | solution.py:307
  49.2 0.1 broadcast_bitcast_fusion
  49.3 0.1 bitcast_multiply_fusion.w_ref
  49.4 4.0 %collective-permute-start.18 = (bf16[2,4,16,1024]{3,2,1,0:T(8,128)(2,1)S(1)}, bf16[2,4,16,1024]{3,2,1,0:T(8,128)(2,1)S(1)}, u32[]{:S(2)}, u32[]{:S(2)}) collective-permute-start(bf16[2,4,16,1024]{3,2,1,0:T(8,128)(2,1)S(1)} %step_on.14.refs_4_.refs_5_), channel_id=1, source_target_pairs={{0,2},{1,3},{2,0},{3,1},{4,6},{5,7},{6,4},{7,5},{8,10},{9,11},{10,... | collective-permute-start | bytes 786440 | tf_op jit(solution)/shard_map/ppermute | solution.py:310
  53.5 0.7 collective-permute-start.17
  54.2 0.1 choose.4
  54.3 0.8 collective-permute-start.19
  55.1 3.8 %collective-permute-done.22 = bf16[2,4,16,1024]{3,2,1,0:T(8,128)(2,1)S(1)} collective-permute-done((bf16[2,4,16,1024]{3,2,1,0:T(8,128)(2,1)S(1)}, bf16[2,4,16,1024]{3,2,1,0:T(8,128)(2,1)S(1)}, u32[]{:S(2)}, u32[]{:S(2)}) %collective-permute-start.22) | collective-permute-done | bytes 262176 | tf_op jit(solution)/shard_map/ppermute | solution.py:307
  59.0 0.1 pad_maximum_fusion
  59.1 0.1 constant_dynamic-slice_fusion.2
  59.2 0.7 times.5
  60.1 0.1 choose.5
  60.2 0.5 collective-permute-start.20
  60.6 0.7 times.4
  61.3 1.3 %collective-permute-done.23 = f32[256,1024]{1,0:T(8,128)S(1)} collective-permute-done((f32[256,1024]{1,0:T(8,128)S(1)}, f32[256,1024]{1,0:T(8,128)S(1)}, u32[]{:S(2)}, u32[]{:S(2)}) %collective-permute-start.23) | collective-permute-done | bytes 1048608 | tf_op jit(solution)/shard_map/ppermute | solution.py:364
  62.6 0.2 settle.2
  62.9 1.6 %collective-permute-start.26 = (s16[144,1024]{1,0:T(8,128)(2,1)S(1)}, s16[144,1024]{1,0:T(8,128)(2,1)S(1)}, u32[]{:S(2)}, u32[]{:S(2)}) collective-permute-start(s16[144,1024]{1,0:T(8,128)(2,1)S(1)} %get-tuple-element.40), channel_id=1, source_target_pairs={{0,16},{8,24},{16,0},{24,8},{1,17},{9,25},{17,1},{25,9},{2,18},{10... | collective-permute-start | bytes 884744 | tf_op jit(solution)/shard_map/ppermute | solution.py:370
  64.4 4.5 %collective-permute-done.20 = bf16[2,4,16,1024]{3,2,1,0:T(8,128)(2,1)S(1)} collective-permute-done((bf16[2,4,16,1024]{3,2,1,0:T(8,128)(2,1)S(1)}, bf16[2,4,16,1024]{3,2,1,0:T(8,128)(2,1)S(1)}, u32[]{:S(2)}, u32[]{:S(2)}) %collective-permute-start.20) | collective-permute-done | bytes 262176 | tf_op jit(solution)/shard_map/ppermute | solution.py:307
  68.9 0.1 maximum_bitcast_fusion.2
  69.0 0.1 pad_maximum_fusion.1
  69.1 0.1 constant_dynamic-slice_fusion
  69.2 0.7 times.7
  70.0 0.7 times.6
  70.7 1.9 %collective-permute-done.24 = f32[256,1024]{1,0:T(8,128)S(1)} collective-permute-done((f32[256,1024]{1,0:T(8,128)S(1)}, f32[256,1024]{1,0:T(8,128)S(1)}, u32[]{:S(2)}, u32[]{:S(2)}) %collective-permute-start.24) | collective-permute-done | bytes 1048608 | tf_op jit(solution)/shard_map/ppermute | solution.py:364
  72.7 0.2 settle.3
  72.9 0.9 merge.3
  73.9 4.6 %all-to-all-start.1 = ((s16[8,144,128]{2,1,0:T(8,128)(2,1)}), s16[8,144,128]{2,1,0:T(8,128)(2,1)S(1)}, u32[]{:S(2)}, u32[]{:S(2)}) async-start(s16[8,144,128]{2,1,0:T(8,128)(2,1)} %get-tuple-element.52), calls=%async_computation.1 | async-start | bytes 589824 | tf_op jit(solution)/shard_map/all_to_all | solution.py:430
  78.4 1.5 %collective-permute-start.25 = (s16[144,1024]{1,0:T(8,128)(2,1)S(1)}, s16[144,1024]{1,0:T(8,128)(2,1)S(1)}, u32[]{:S(2)}, u32[]{:S(2)}) collective-permute-start(s16[144,1024]{1,0:T(8,128)(2,1)S(1)} %get-tuple-element.46), channel_id=1, source_target_pairs={{0,16},{8,24},{16,0},{24,8},{1,17},{9,25},{17,1},{25,9},{2,18},{10... | collective-permute-start | bytes 884744 | tf_op jit(solution)/shard_map/ppermute | solution.py:370
  79.9 7.3 %collective-permute-done.25.coded_ref = s16[144,1024]{1,0:T(8,128)(2,1)S(1)} collective-permute-done((s16[144,1024]{1,0:T(8,128)(2,1)S(1)}, s16[144,1024]{1,0:T(8,128)(2,1)S(1)}, u32[]{:S(2)}, u32[]{:S(2)}) %collective-permute-start.25) | collective-permute-done | bytes 294944 | tf_op jit(solution)/shard_map/ppermute | solution.py:370
  87.2 0.9 merge.2
  88.1 0.2 all-to-all-done.1.refs_1_
  88.3 5.5 %all-to-all-start = ((s16[8,144,128]{2,1,0:T(8,128)(2,1)}), s16[8,144,128]{2,1,0:T(8,128)(2,1)S(1)}, u32[]{:S(2)}, u32[]{:S(2)}) async-start(s16[8,144,128]{2,1,0:T(8,128)(2,1)} %get-tuple-element.48), calls=%async_computation | async-start | bytes 589824 | tf_op jit(solution)/shard_map/all_to_all | solution.py:430
  93.9 1.1 %finish.2.refs_5_ = f32[2,2,2,32,1024]{4,3,2,1,0:T(8,128)} custom-call(f32[128,1024]{1,0:T(8,128)S(1)} %get-tuple-element.51.refs_0_, s16[8,144,128]{2,1,0:T(8,128)(2,1)S(1)} %all-to-all-done.1.refs_1_, s32[1,128]{1,0:T(1,128)S(1)} %bitcast.78, f32[1,1024]{1,0:T(1,128)S(1)} %bitcast.76, f32[2,128]{1,0:T(2,128)S(1)} %copy-done.2), custom_call_target="tpu_custom_call" | custom-call | flops 20000000000 | tf_op jit(solution)/shard_map/finish/pallas_call | solution.py:275
  94.9 7.4 %all-to-all-done.refs_1_ = s16[8,144,128]{2,1,0:T(8,128)(2,1)S(1)} async-done(((s16[8,144,128]{2,1,0:T(8,128)(2,1)}), s16[8,144,128]{2,1,0:T(8,128)(2,1)S(1)}, u32[]{:S(2)}, u32[]{:S(2)}) %all-to-all-start) | async-done | bytes 294944 | tf_op jit(solution)/shard_map/all_to_all | solution.py:430
  102.3 1.0 %finish.3 = f32[2,2,2,32,1024]{4,3,2,1,0:T(8,128)} custom-call(f32[128,1024]{1,0:T(8,128)S(1)} %get-tuple-element.47.refs_0_, s16[8,144,128]{2,1,0:T(8,128)(2,1)S(1)} %all-to-all-done.refs_1_, s32[1,128]{1,0:T(1,128)S(1)} %bitcast.79, f32[1,1024]{1,0:T(1,128)S(1)} %bitcast.77, f32[2,128]{1,0:T(2,128)S(1)} %copy-done.2, ...), custom_call_target="tpu_custom_call", output_to_operand_aliasing={{}: (5, {})} | custom-call | flops 20000000000 | tf_op jit(solution)/shard_map/finish/pallas_call | solution.py:275
  (53 shorter events, 1.0 us)
Async XLA Ops:
  0.0 1.2 %copy-start = (bf16[1,512,1024]{2,1,0:T(8,128)(2,1)S(1)}, bf16[1,512,1024]{2,1,0:T(8,128)(2,1)}, u32[]{:S(2)}) copy-start(bf16[1,512,1024]{2,1,0:T(8,128)(2,1)} %param.8) | copy-start | bytes 3145732
  0.0 4.4 %copy-start.7 = (s32[2]{0:T(128)S(1)}, s32[2]{0:T(128)}, u32[]{:S(2)}) copy-start(s32[2]{0:T(128)} %param.10) | copy-start | bytes 28
  0.0 6.2 %copy-start.6 = (s32[4,4]{1,0:T(4,128)S(1)}, s32[4,4]{1,0:T(4,128)}, u32[]{:S(2)}) copy-start(s32[4,4]{1,0:T(4,128)} %param.9) | copy-start | bytes 196
  1.2 6.5 %collective-permute-start = (bf16[4,16,1024]{2,1,0:T(8,128)(2,1)S(1)}, bf16[4,16,1024]{2,1,0:T(8,128)(2,1)S(1)}, u32[]{:S(2)}, u32[]{:S(2)}) collective-permute-start(bf16[4,16,1024]{2,1,0:T(8,128)(2,1)S(1)} %dynamic-slice_bitcast_fusion.2), channel_id=1, source_target_pairs={{0,1},{1,0},{2,3},{3,2},{4,5},{5,4},{6,7},{7,6},{8,9},{9,8},{10,11... | collective-permute-start | bytes 393224 | tf_op jit(solution)/shard_map/ppermute | solution.py:307
  7.7 5.3 %collective-permute-start.10 = (bf16[4,16,1024]{2,1,0:T(8,128)(2,1)S(1)}, bf16[4,16,1024]{2,1,0:T(8,128)(2,1)S(1)}, u32[]{:S(2)}, u32[]{:S(2)}) collective-permute-start(bf16[4,16,1024]{2,1,0:T(8,128)(2,1)S(1)} %get-tuple-element.37), channel_id=1, source_target_pairs={{0,1},{1,0},{2,3},{3,2},{4,5},{5,4},{6,7},{7,6},{8,9},{9,8},{10,11... | collective-permute-start | bytes 393224 | tf_op jit(solution)/shard_map/ppermute | solution.py:307
  9.6 9.0 %collective-permute-start.3 = (bf16[2,4,16,1024]{3,2,1,0:T(8,128)(2,1)S(1)}, bf16[2,4,16,1024]{3,2,1,0:T(8,128)(2,1)S(1)}, u32[]{:S(2)}, u32[]{:S(2)}) collective-permute-start(bf16[2,4,16,1024]{3,2,1,0:T(8,128)(2,1)S(1)} %begin.2.refs_2_), channel_id=1, source_target_pairs={{0,2},{1,3},{2,0},{3,1},{4,6},{5,7},{6,4},{7,5},{8,10},{9,11},{10,... | collective-permute-start | bytes 786440 | tf_op jit(solution)/shard_map/ppermute | solution.py:310
  11.2 7.4 %collective-permute-start.2 = (bf16[2,4,16,1024]{3,2,1,0:T(8,128)(2,1)S(1)}, bf16[2,4,16,1024]{3,2,1,0:T(8,128)(2,1)S(1)}, u32[]{:S(2)}, u32[]{:S(2)}) collective-permute-start(bf16[2,4,16,1024]{3,2,1,0:T(8,128)(2,1)S(1)} %begin.2.refs_2_), channel_id=1, source_target_pairs={{2,4},{3,5},{4,2},{5,3},{10,12},{11,13},{12,10},{13,11},{18,20},{1... | collective-permute-start | bytes 786440 | tf_op jit(solution)/shard_map/ppermute | solution.py:310
  11.9 6.7 %collective-permute-start.1 = (bf16[2,4,16,1024]{3,2,1,0:T(8,128)(2,1)S(1)}, bf16[2,4,16,1024]{3,2,1,0:T(8,128)(2,1)S(1)}, u32[]{:S(2)}, u32[]{:S(2)}) collective-permute-start(bf16[2,4,16,1024]{3,2,1,0:T(8,128)(2,1)S(1)} %pad_maximum_fusion.2), channel_id=1, source_target_pairs={{0,1},{1,0},{2,3},{3,2},{4,5},{5,4},{6,7},{7,6},{8,9},{9,8},{10,11... | collective-permute-start | bytes 786440 | tf_op jit(solution)/shard_map/ppermute | solution.py:307
  13.0 10.8 %collective-permute-start.12 = (bf16[2,4,16,1024]{3,2,1,0:T(8,128)(2,1)S(1)}, bf16[2,4,16,1024]{3,2,1,0:T(8,128)(2,1)S(1)}, u32[]{:S(2)}, u32[]{:S(2)}) collective-permute-start(bf16[2,4,16,1024]{3,2,1,0:T(8,128)(2,1)S(1)} %begin.3.refs_2_), channel_id=1, source_target_pairs={{0,2},{1,3},{2,0},{3,1},{4,6},{5,7},{6,4},{7,5},{8,10},{9,11},{10,... | collective-permute-start | bytes 786440 | tf_op jit(solution)/shard_map/ppermute | solution.py:310
  17.0 6.8 %collective-permute-start.11 = (bf16[2,4,16,1024]{3,2,1,0:T(8,128)(2,1)S(1)}, bf16[2,4,16,1024]{3,2,1,0:T(8,128)(2,1)S(1)}, u32[]{:S(2)}, u32[]{:S(2)}) collective-permute-start(bf16[2,4,16,1024]{3,2,1,0:T(8,128)(2,1)S(1)} %begin.3.refs_2_), channel_id=1, source_target_pairs={{2,4},{3,5},{4,2},{5,3},{10,12},{11,13},{12,10},{13,11},{18,20},{1... | collective-permute-start | bytes 786440 | tf_op jit(solution)/shard_map/ppermute | solution.py:310
  18.7 10.7 %collective-permute-start.5 = (bf16[2,4,16,1024]{3,2,1,0:T(8,128)(2,1)S(1)}, bf16[2,4,16,1024]{3,2,1,0:T(8,128)(2,1)S(1)}, u32[]{:S(2)}, u32[]{:S(2)}) collective-permute-start(bf16[2,4,16,1024]{3,2,1,0:T(8,128)(2,1)S(1)} %step_on.8.refs_2_.refs_3_), channel_id=1, source_target_pairs={{0,2},{1,3},{2,0},{3,1},{4,6},{5,7},{6,4},{7,5},{8,10},{9,11},{10,... | collective-permute-start | bytes 786440 | tf_op jit(solution)/shard_map/ppermute | solution.py:310
  23.1 6.3 %collective-permute-start.4 = (bf16[2,4,16,1024]{3,2,1,0:T(8,128)(2,1)S(1)}, bf16[2,4,16,1024]{3,2,1,0:T(8,128)(2,1)S(1)}, u32[]{:S(2)}, u32[]{:S(2)}) collective-permute-start(bf16[2,4,16,1024]{3,2,1,0:T(8,128)(2,1)S(1)} %step_on.8.refs_2_.refs_3_), channel_id=1, source_target_pairs={{2,4},{3,5},{4,2},{5,3},{10,12},{11,13},{12,10},{13,11},{18,20},{1... | collective-permute-start | bytes 786440 | tf_op jit(solution)/shard_map/ppermute | solution.py:310
  23.9 11.8 %collective-permute-start.14 = (bf16[2,4,16,1024]{3,2,1,0:T(8,128)(2,1)S(1)}, bf16[2,4,16,1024]{3,2,1,0:T(8,128)(2,1)S(1)}, u32[]{:S(2)}, u32[]{:S(2)}) collective-permute-start(bf16[2,4,16,1024]{3,2,1,0:T(8,128)(2,1)S(1)} %step_on.12.refs_2_.refs_3_), channel_id=1, source_target_pairs={{0,2},{1,3},{2,0},{3,1},{4,6},{5,7},{6,4},{7,5},{8,10},{9,11},{10,... | collective-permute-start | bytes 786440 | tf_op jit(solution)/shard_map/ppermute | solution.py:310
  28.6 7.1 %collective-permute-start.13 = (bf16[2,4,16,1024]{3,2,1,0:T(8,128)(2,1)S(1)}, bf16[2,4,16,1024]{3,2,1,0:T(8,128)(2,1)S(1)}, u32[]{:S(2)}, u32[]{:S(2)}) collective-permute-start(bf16[2,4,16,1024]{3,2,1,0:T(8,128)(2,1)S(1)} %step_on.12.refs_2_.refs_3_), channel_id=1, source_target_pairs={{2,4},{3,5},{4,2},{5,3},{10,12},{11,13},{12,10},{13,11},{18,20},{1... | collective-permute-start | bytes 786440 | tf_op jit(solution)/shard_map/ppermute | solution.py:310
  29.5 12.3 %collective-permute-start.7 = (bf16[2,4,16,1024]{3,2,1,0:T(8,128)(2,1)S(1)}, bf16[2,4,16,1024]{3,2,1,0:T(8,128)(2,1)S(1)}, u32[]{:S(2)}, u32[]{:S(2)}) collective-permute-start(bf16[2,4,16,1024]{3,2,1,0:T(8,128)(2,1)S(1)} %step_on.9.refs_3_.refs_4_), channel_id=1, source_target_pairs={{0,2},{1,3},{2,0},{3,1},{4,6},{5,7},{6,4},{7,5},{8,10},{9,11},{10,... | collective-permute-start | bytes 786440 | tf_op jit(solution)/shard_map/ppermute | solution.py:310
  34.9 6.9 %collective-permute-start.6 = (bf16[2,4,16,1024]{3,2,1,0:T(8,128)(2,1)S(1)}, bf16[2,4,16,1024]{3,2,1,0:T(8,128)(2,1)S(1)}, u32[]{:S(2)}, u32[]{:S(2)}) collective-permute-start(bf16[2,4,16,1024]{3,2,1,0:T(8,128)(2,1)S(1)} %step_on.9.refs_3_.refs_4_), channel_id=1, source_target_pairs={{2,4},{3,5},{4,2},{5,3},{10,12},{11,13},{12,10},{13,11},{18,20},{1... | collective-permute-start | bytes 786440 | tf_op jit(solution)/shard_map/ppermute | solution.py:310
  35.8 11.6 %collective-permute-start.16 = (bf16[2,4,16,1024]{3,2,1,0:T(8,128)(2,1)S(1)}, bf16[2,4,16,1024]{3,2,1,0:T(8,128)(2,1)S(1)}, u32[]{:S(2)}, u32[]{:S(2)}) collective-permute-start(bf16[2,4,16,1024]{3,2,1,0:T(8,128)(2,1)S(1)} %step_on.13.refs_3_.refs_4_), channel_id=1, source_target_pairs={{0,2},{1,3},{2,0},{3,1},{4,6},{5,7},{6,4},{7,5},{8,10},{9,11},{10,... | collective-permute-start | bytes 786440 | tf_op jit(solution)/shard_map/ppermute | solution.py:310
  40.5 6.9 %collective-permute-start.15 = (bf16[2,4,16,1024]{3,2,1,0:T(8,128)(2,1)S(1)}, bf16[2,4,16,1024]{3,2,1,0:T(8,128)(2,1)S(1)}, u32[]{:S(2)}, u32[]{:S(2)}) collective-permute-start(bf16[2,4,16,1024]{3,2,1,0:T(8,128)(2,1)S(1)} %step_on.13.refs_3_.refs_4_), channel_id=1, source_target_pairs={{2,4},{3,5},{4,2},{5,3},{10,12},{11,13},{12,10},{13,11},{18,20},{1... | collective-permute-start | bytes 786440 | tf_op jit(solution)/shard_map/ppermute | solution.py:310
  41.8 11.6 %collective-permute-start.9 = (bf16[2,4,16,1024]{3,2,1,0:T(8,128)(2,1)S(1)}, bf16[2,4,16,1024]{3,2,1,0:T(8,128)(2,1)S(1)}, u32[]{:S(2)}, u32[]{:S(2)}) collective-permute-start(bf16[2,4,16,1024]{3,2,1,0:T(8,128)(2,1)S(1)} %step_on.10.refs_4_.refs_5_), channel_id=1, source_target_pairs={{0,2},{1,3},{2,0},{3,1},{4,6},{5,7},{6,4},{7,5},{8,10},{9,11},{10,... | collective-permute-start | bytes 786440 | tf_op jit(solution)/shard_map/ppermute | solution.py:310
  46.1 8.0 %collective-permute-start.8 = (bf16[2,4,16,1024]{3,2,1,0:T(8,128)(2,1)S(1)}, bf16[2,4,16,1024]{3,2,1,0:T(8,128)(2,1)S(1)}, u32[]{:S(2)}, u32[]{:S(2)}) collective-permute-start(bf16[2,4,16,1024]{3,2,1,0:T(8,128)(2,1)S(1)} %step_on.10.refs_4_.refs_5_), channel_id=1, source_target_pairs={{2,4},{3,5},{4,2},{5,3},{10,12},{11,13},{12,10},{13,11},{18,20},{1... | collective-permute-start | bytes 786440 | tf_op jit(solution)/shard_map/ppermute | solution.py:310
  46.9 2.3 %copy-start.5 = (bf16[4,4]{1,0:T(4,128)(2,1)S(1)}, bf16[4,4]{1,0:T(4,128)(2,1)}, u32[]{:S(2)}) copy-start(bf16[4,4]{1,0:T(4,128)(2,1)} %convert_element_type.46) | copy-start | bytes 100
  46.9 8.2 %collective-permute-start.21 = (bf16[2,4,16,1024]{3,2,1,0:T(8,128)(2,1)S(1)}, bf16[2,4,16,1024]{3,2,1,0:T(8,128)(2,1)S(1)}, u32[]{:S(2)}, u32[]{:S(2)}) collective-permute-start(bf16[2,4,16,1024]{3,2,1,0:T(8,128)(2,1)S(1)} %choose.6), channel_id=1, source_target_pairs={{0,1},{1,0},{2,3},{3,2},{4,5},{5,4},{6,7},{7,6},{8,9},{9,8},{10,11... | collective-permute-start | bytes 786440 | tf_op jit(solution)/shard_map/ppermute | solution.py:307
  47.4 1.9 %copy-start.4 = (bf16[1024,1024]{1,0:T(8,128)(2,1)S(1)}, bf16[1024,1024]{1,0:T(8,128)(2,1)}, u32[]{:S(2)}) copy-start(bf16[1024,1024]{1,0:T(8,128)(2,1)} %param.7) | copy-start | bytes 6291460
  47.5 11.4 %collective-permute-start.22 = (bf16[2,4,16,1024]{3,2,1,0:T(8,128)(2,1)S(1)}, bf16[2,4,16,1024]{3,2,1,0:T(8,128)(2,1)S(1)}, u32[]{:S(2)}, u32[]{:S(2)}) collective-permute-start(bf16[2,4,16,1024]{3,2,1,0:T(8,128)(2,1)S(1)} %choose.7), channel_id=1, source_target_pairs={{0,1},{1,0},{2,3},{3,2},{4,5},{5,4},{6,7},{7,6},{8,9},{9,8},{10,11... | collective-permute-start | bytes 786440 | tf_op jit(solution)/shard_map/ppermute | solution.py:307
  49.4 10.6 %collective-permute-start.18 = (bf16[2,4,16,1024]{3,2,1,0:T(8,128)(2,1)S(1)}, bf16[2,4,16,1024]{3,2,1,0:T(8,128)(2,1)S(1)}, u32[]{:S(2)}, u32[]{:S(2)}) collective-permute-start(bf16[2,4,16,1024]{3,2,1,0:T(8,128)(2,1)S(1)} %step_on.14.refs_4_.refs_5_), channel_id=1, source_target_pairs={{0,2},{1,3},{2,0},{3,1},{4,6},{5,7},{6,4},{7,5},{8,10},{9,11},{10,... | collective-permute-start | bytes 786440 | tf_op jit(solution)/shard_map/ppermute | solution.py:310
  53.5 6.5 %collective-permute-start.17 = (bf16[2,4,16,1024]{3,2,1,0:T(8,128)(2,1)S(1)}, bf16[2,4,16,1024]{3,2,1,0:T(8,128)(2,1)S(1)}, u32[]{:S(2)}, u32[]{:S(2)}) collective-permute-start(bf16[2,4,16,1024]{3,2,1,0:T(8,128)(2,1)S(1)} %step_on.14.refs_4_.refs_5_), channel_id=1, source_target_pairs={{2,4},{3,5},{4,2},{5,3},{10,12},{11,13},{12,10},{13,11},{18,20},{1... | collective-permute-start | bytes 786440 | tf_op jit(solution)/shard_map/ppermute | solution.py:310
  54.3 10.1 %collective-permute-start.19 = (bf16[2,4,16,1024]{3,2,1,0:T(8,128)(2,1)S(1)}, bf16[2,4,16,1024]{3,2,1,0:T(8,128)(2,1)S(1)}, u32[]{:S(2)}, u32[]{:S(2)}) collective-permute-start(bf16[2,4,16,1024]{3,2,1,0:T(8,128)(2,1)S(1)} %choose.4), channel_id=1, source_target_pairs={{0,1},{1,0},{2,3},{3,2},{4,5},{5,4},{6,7},{7,6},{8,9},{9,8},{10,11... | collective-permute-start | bytes 786440 | tf_op jit(solution)/shard_map/ppermute | solution.py:307
  59.9 2.7 %collective-permute-start.23 = (f32[256,1024]{1,0:T(8,128)S(1)}, f32[256,1024]{1,0:T(8,128)S(1)}, u32[]{:S(2)}, u32[]{:S(2)}) collective-permute-start(f32[256,1024]{1,0:T(8,128)S(1)} %times.5), channel_id=1, source_target_pairs={{0,8},{8,0},{16,24},{24,16},{1,9},{9,1},{17,25},{25,17},{2,10},{10... | collective-permute-start | bytes 3145736 | tf_op jit(solution)/shard_map/ppermute | solution.py:364
  60.2 8.7 %collective-permute-start.20 = (bf16[2,4,16,1024]{3,2,1,0:T(8,128)(2,1)S(1)}, bf16[2,4,16,1024]{3,2,1,0:T(8,128)(2,1)S(1)}, u32[]{:S(2)}, u32[]{:S(2)}) collective-permute-start(bf16[2,4,16,1024]{3,2,1,0:T(8,128)(2,1)S(1)} %choose.5), channel_id=1, source_target_pairs={{0,1},{1,0},{2,3},{3,2},{4,5},{5,4},{6,7},{7,6},{8,9},{9,8},{10,11... | collective-permute-start | bytes 786440 | tf_op jit(solution)/shard_map/ppermute | solution.py:307
  62.9 10.1 %collective-permute-start.26 = (s16[144,1024]{1,0:T(8,128)(2,1)S(1)}, s16[144,1024]{1,0:T(8,128)(2,1)S(1)}, u32[]{:S(2)}, u32[]{:S(2)}) collective-permute-start(s16[144,1024]{1,0:T(8,128)(2,1)S(1)} %get-tuple-element.40), channel_id=1, source_target_pairs={{0,16},{8,24},{16,0},{24,8},{1,17},{9,25},{17,1},{25,9},{2,18},{10... | collective-permute-start | bytes 884744 | tf_op jit(solution)/shard_map/ppermute | solution.py:370
  69.9 2.7 %collective-permute-start.24 = (f32[256,1024]{1,0:T(8,128)S(1)}, f32[256,1024]{1,0:T(8,128)S(1)}, u32[]{:S(2)}, u32[]{:S(2)}) collective-permute-start(f32[256,1024]{1,0:T(8,128)S(1)} %times.7), channel_id=1, source_target_pairs={{0,8},{8,0},{16,24},{24,16},{1,9},{9,1},{17,25},{25,17},{2,10},{10... | collective-permute-start | bytes 3145736 | tf_op jit(solution)/shard_map/ppermute | solution.py:364
  72.7 21.2 %copy-start.1 = (f32[1024]{0:T(1024)S(1)}, f32[1024]{0:T(1024)}, u32[]{:S(2)}) copy-start(f32[1024]{0:T(1024)} %param.12) | copy-start | bytes 12292
  72.7 21.2 %copy-start.2 = (f32[2,128]{1,0:T(2,128)S(1)}, f32[2,128]{1,0:T(2,128)}, u32[]{:S(2)}) copy-start(f32[2,128]{1,0:T(2,128)} %refs_4_.3) | copy-start | bytes 3076
  72.7 21.2 %copy-start.3 = (s32[128]{0:T(128)S(1)}, s32[128]{0:T(128)}, u32[]{:S(2)}) copy-start(s32[128]{0:T(128)} %param.13) | copy-start | bytes 1540
  73.9 14.4 %all-to-all-start.1 = ((s16[8,144,128]{2,1,0:T(8,128)(2,1)}), s16[8,144,128]{2,1,0:T(8,128)(2,1)S(1)}, u32[]{:S(2)}, u32[]{:S(2)}) async-start(s16[8,144,128]{2,1,0:T(8,128)(2,1)} %get-tuple-element.52), calls=%async_computation.1 | async-start | bytes 589824 | tf_op jit(solution)/shard_map/all_to_all | solution.py:430
  78.4 8.8 %collective-permute-start.25 = (s16[144,1024]{1,0:T(8,128)(2,1)S(1)}, s16[144,1024]{1,0:T(8,128)(2,1)S(1)}, u32[]{:S(2)}, u32[]{:S(2)}) collective-permute-start(s16[144,1024]{1,0:T(8,128)(2,1)S(1)} %get-tuple-element.46), channel_id=1, source_target_pairs={{0,16},{8,24},{16,0},{24,8},{1,17},{9,25},{17,1},{25,9},{2,18},{10... | collective-permute-start | bytes 884744 | tf_op jit(solution)/shard_map/ppermute | solution.py:370
  88.3 14.0 %all-to-all-start = ((s16[8,144,128]{2,1,0:T(8,128)(2,1)}), s16[8,144,128]{2,1,0:T(8,128)(2,1)S(1)}, u32[]{:S(2)}, u32[]{:S(2)}) async-start(s16[8,144,128]{2,1,0:T(8,128)(2,1)} %get-tuple-element.48), calls=%async_computation | async-start | bytes 589824 | tf_op jit(solution)/shard_map/all_to_all | solution.py:430
